TPU v7x, 32 devices: a whole 2x2x4 slice. The times are simulated.
32 devices in a mesh: bucket: 8 (over z, x), seq: 4 (over y, core).
Axes of the slice: x: 2, y: 2, z: 4, core: 2. Of those that a mesh axis runs over, the one named last changes fastest.
Arguments:
- tokens: bfloat16 [16384, 1152], P(('bucket', 'seq')), may hold values from -6 to 6
- condition: float32 [8, 1152], P('bucket'), may hold values from -6 to 6
- cotangent: bfloat16 [16384, 1152], P(('bucket', 'seq')), may hold values from -6 to 6
- lengths: int32 [8, 8], P('bucket'), may hold values from 0 to 1024, as said below
- bucket_ids: int32 [8], P('bucket'), may hold values from 0 to 9
- keep_flags: int32 [16384], P(('bucket', 'seq')), may hold values 0 or 1
- head_table: int32 [10, 16], replicated, may hold values 0 or 1
- chan_table: int32 [10, 4608], replicated, may hold values 0 or 1
- ada_master: float32 [1152, 6912], P('bucket', 'seq'), may hold values from -0.1875 to 0.1875
- ada_first: float32 [1152, 6912], P('bucket', 'seq'), may hold values from -224 to 224
- ada_second: float32 [1152, 6912], P('bucket', 'seq'), may hold values from 1474.56 to 5898.24
- ada_average: float32 [1152, 6912], P('bucket', 'seq'), may hold values from -0.1875 to 0.1875
- qkv_master: float32 [1152, 3456], P('bucket', 'seq'), may hold values from -0.1875 to 0.1875
- qkv_first: float32 [1152, 3456], P('bucket', 'seq'), may hold values from -320 to 320
- qkv_second: float32 [1152, 3456], P('bucket', 'seq'), may hold values from 2621.44 to 10485.76
- qkv_average: float32 [1152, 3456], P('bucket', 'seq'), may hold values from -0.1875 to 0.1875
- out_master: float32 [1152, 1152], P('bucket', 'seq'), may hold values from -2 to 2
- out_first: float32 [1152, 1152], P('bucket', 'seq'), may hold values from -64 to 64
- out_second: float32 [1152, 1152], P('bucket', 'seq'), may hold values from 64 to 256
- out_average: float32 [1152, 1152], P('bucket', 'seq'), may hold values from -2 to 2
- up_master: float32 [1152, 4608], P('bucket', 'seq'), may hold values from -0.1875 to 0.1875
- up_first: float32 [1152, 4608], P('bucket', 'seq'), may hold values from -192 to 192
- up_second: float32 [1152, 4608], P('bucket', 'seq'), may hold values from 1024 to 4096
- up_average: float32 [1152, 4608], P('bucket', 'seq'), may hold values from -0.1875 to 0.1875
- down_master: float32 [4608, 1152], P('bucket', 'seq'), may hold values from -0.09375 to 0.09375
- down_first: float32 [4608, 1152], P('bucket', 'seq'), may hold values from -384 to 384
- down_second: float32 [4608, 1152], P('bucket', 'seq'), may hold values from 4096 to 16384
- down_average: float32 [4608, 1152], P('bucket', 'seq'), may hold values from -0.09375 to 0.09375
- bias_master: float32 [16128], P(('bucket', 'seq')), may hold values from -2 to 2
- bias_first: float32 [16128], P(('bucket', 'seq')), may hold values from -320 to 320
- bias_second: float32 [16128], P(('bucket', 'seq')), may hold values from 2621.44 to 10485.76
- bias_average: float32 [16128], P(('bucket', 'seq')), may hold values from -2 to 2
Outputs:
- output: bfloat16 [16384, 1152], P(('bucket', 'seq'))
- token_grad: float32 [16384, 1152], P(('bucket', 'seq'))
- condition_grad: float32 [8, 1152], P('bucket')
- ada_master_new: float32 [1152, 6912], P('bucket', 'seq')
- ada_first_new: float32 [1152, 6912], P('bucket', 'seq')
- ada_second_new: float32 [1152, 6912], P('bucket', 'seq')
- ada_average_new: float32 [1152, 6912], P('bucket', 'seq')
- qkv_master_new: float32 [1152, 3456], P('bucket', 'seq')
- qkv_first_new: float32 [1152, 3456], P('bucket', 'seq')
- qkv_second_new: float32 [1152, 3456], P('bucket', 'seq')
- qkv_average_new: float32 [1152, 3456], P('bucket', 'seq')
- out_master_new: float32 [1152, 1152], P('bucket', 'seq')
- out_first_new: float32 [1152, 1152], P('bucket', 'seq')
- out_second_new: float32 [1152, 1152], P('bucket', 'seq')
- out_average_new: float32 [1152, 1152], P('bucket', 'seq')
- up_master_new: float32 [1152, 4608], P('bucket', 'seq')
- up_first_new: float32 [1152, 4608], P('bucket', 'seq')
- up_second_new: float32 [1152, 4608], P('bucket', 'seq')
- up_average_new: float32 [1152, 4608], P('bucket', 'seq')
- down_master_new: float32 [4608, 1152], P('bucket', 'seq')
- down_first_new: float32 [4608, 1152], P('bucket', 'seq')
- down_second_new: float32 [4608, 1152], P('bucket', 'seq')
- down_average_new: float32 [4608, 1152], P('bucket', 'seq')
- bias_master_new: float32 [16128], P(('bucket', 'seq'))
- bias_first_new: float32 [16128], P(('bucket', 'seq'))
- bias_second_new: float32 [16128], P(('bucket', 'seq'))
- bias_average_new: float32 [16128], P(('bucket', 'seq'))
Inputs may be any that keep to these rules, and one draw needn't show every extreme that they name: `lengths`: each group's images have 256 or 1024 tokens, stand first in its row with zeros after them, and fill its 2048 tokens; every draw holds an image of 1024 tokens.
All inputs are finite; a program needn't handle non-finite values. No bound on the sum of `keep_flags` on one device may be relied on, other than what follows from the above.
Results may differ from a plain program's by a relative error of at most 0.02.
Values may be sent and summed in bfloat16 or wider, within the bound.
A program may use at most 256 MiB of HBM per device.

v0:
```python
import jax
import jax.numpy as jnp
from jax import lax
from jax.sharding import PartitionSpec as P

STEP = 10


EPSILON = 1e-06
BETA_FIRST = 0.5
BETA_SECOND = 0.5
ADAM_EPSILON = 1e-08
MATRIX_DECAY = 0.01
EMA_DECAY = 0.9999
HIGHEST = lax.Precision.HIGHEST


def layer_norm(values):
    centre = values - jnp.mean(values, axis=-1, keepdims=True)
    spread = jnp.mean(centre * centre, axis=-1, keepdims=True)
    return centre * lax.rsqrt(spread + EPSILON)


def modulate(values, shift_row, scale_row):
    return layer_norm(values) * (1.0 + scale_row) + shift_row


def gelu_tanh(values):
    return jax.nn.gelu(values, approximate=True)


def segment_of(positions, image_ends):
    return jnp.sum((positions[:, None] >= image_ends[None, :]).astype(jnp.int32), axis=1)


def contract_rows(left, right):
    return lax.dot_general(
        left, right, (((0,), (0,)), ((), ())), preferred_element_type=jnp.float32
    )


def contract_last(left, right):
    return lax.dot_general(
        left, right, (((1,), (1,)), ((), ())), preferred_element_type=jnp.float32
    )


def adam_update(master, moment_one, moment_two, average, gradient, step_rate, decay_rate):
    one_new = BETA_FIRST * moment_one + (1.0 - BETA_FIRST) * gradient
    two_new = BETA_SECOND * moment_two + (1.0 - BETA_SECOND) * gradient * gradient
    one_hat = one_new / (1.0 - BETA_FIRST**STEP)
    two_hat = two_new / (1.0 - BETA_SECOND**STEP)
    master_new = master - step_rate * (
        one_hat / (jnp.sqrt(two_hat) + ADAM_EPSILON) + decay_rate * master
    )
    average_decay = min(EMA_DECAY, (1.0 + STEP) / (10.0 + STEP))
    average_new = average_decay * average + (1.0 - average_decay) * master_new
    return (master_new, one_new, two_new, average_new)


def on_device(
    tokens,
    condition,
    cotangent,
    lengths,
    bucket_ids,
    keep_flags,
    head_table,
    chan_table,
    ada_master,
    ada_first,
    ada_second,
    ada_average,
    qkv_master,
    qkv_first,
    qkv_second,
    qkv_average,
    out_master,
    out_first,
    out_second,
    out_average,
    up_master,
    up_first,
    up_second,
    up_average,
    down_master,
    down_first,
    down_second,
    down_average,
    bias_master,
    bias_first,
    bias_second,
    bias_average,
):
    width = tokens.shape[1]
    local_rows = tokens.shape[0]
    head_count = head_table.shape[1]
    head_size = width // head_count
    hidden_width = chan_table.shape[1]
    hidden_ratio = hidden_width // width
    table_cols = 10 + hidden_ratio
    seq_count = lax.axis_size("seq")
    group_rows = local_rows * seq_count
    bfloat = jnp.bfloat16
    single = jnp.float32
    seq_whole = (
        lax.all_gather(ada_master.astype(bfloat), "seq", axis=1, tiled=True),
        lax.all_gather(qkv_master.astype(bfloat), "seq", axis=1, tiled=True),
        lax.all_gather(out_master.astype(bfloat), "seq", axis=1, tiled=True),
        lax.all_gather(up_master.astype(bfloat), "seq", axis=1, tiled=True),
        lax.all_gather(down_master.astype(bfloat), "seq", axis=1, tiled=True),
        lax.all_gather(bias_master.astype(bfloat), "seq", axis=0, tiled=True),
    )
    gathered = (
        lax.all_gather(seq_whole[0], "bucket", axis=0, tiled=True),
        lax.all_gather(seq_whole[1], "bucket", axis=0, tiled=True),
        lax.all_gather(seq_whole[2], "bucket", axis=0, tiled=True),
        lax.all_gather(seq_whole[3], "bucket", axis=0, tiled=True),
        lax.all_gather(seq_whole[4], "bucket", axis=0, tiled=True),
        lax.all_gather(seq_whole[5], "bucket", axis=0, tiled=True),
    )
    ada_weight, qkv_weight, out_weight, up_weight, down_weight, bias_low = gathered
    bias_table = bias_low.astype(single).reshape(width, table_cols)
    ada_bias = bias_table[:, :6].T.reshape(6 * width)
    query_bias = bias_table[:, 6]
    value_bias = bias_table[:, 7]
    out_bias = bias_table[:, 8]
    up_bias = bias_table[:, 9 : table_cols - 1].reshape(hidden_width)
    down_bias = bias_table[:, table_cols - 1]
    silu_low = jax.nn.silu(condition[0]).astype(bfloat)
    modulation = jnp.dot(silu_low[None], ada_weight, preferred_element_type=single)[0] + ada_bias
    shift_one, scale_one, gate_one, shift_two, scale_two, gate_two = jnp.split(modulation, 6)
    selector = (jnp.arange(head_table.shape[0], dtype=jnp.int32) == bucket_ids[0]).astype(single)
    head_keep = jnp.dot(selector, head_table.astype(single))
    chan_keep = jnp.dot(selector, chan_table.astype(single))
    head_wide = jnp.repeat(head_keep, head_size)
    keep_float = keep_flags.astype(single)[:, None]
    image_ends = jnp.cumsum(lengths[0])
    query_pos = lax.axis_index("seq") * local_rows + jnp.arange(local_rows, dtype=jnp.int32)
    query_seg = segment_of(query_pos, image_ends)
    key_seg = segment_of(jnp.arange(group_rows, dtype=jnp.int32), image_ends)
    inputs_float = tokens.astype(single)
    first_in = modulate(inputs_float, shift_one, scale_one).astype(bfloat)
    qkv_bias = jnp.concatenate([query_bias, jnp.zeros_like(query_bias), value_bias])
    projected = (jnp.dot(first_in, qkv_weight, preferred_element_type=single) + qkv_bias).astype(
        bfloat
    )
    query_heads = projected[:, :width].reshape(local_rows, head_count, head_size)
    key_value = projected[:, width:]
    gathered_kv = lax.all_gather(key_value, "seq", axis=0, tiled=True)
    block_rows = min(512, group_rows)
    block_count = group_rows // block_rows
    score_scale = head_size ** (-0.5)
    block_ids = jnp.arange(block_count, dtype=jnp.int32)

    def kv_block(source, index):
        piece = lax.dynamic_slice_in_dim(source, index * block_rows, block_rows, 0)
        seg_block = lax.dynamic_slice_in_dim(key_seg, index * block_rows, block_rows, 0)
        key_part = piece[:, :width].reshape(block_rows, head_count, head_size)
        value_part = piece[:, width:].reshape(block_rows, head_count, head_size)
        return (key_part, value_part, seg_block)

    def block_scores(key_part, seg_block):
        raw = (
            jnp.einsum("qhd,khd->hqk", query_heads, key_part, preferred_element_type=single)
            * score_scale
        )
        return jnp.where((query_seg[:, None] == seg_block[None, :])[None], raw, -1e30)

    def stats_step(carry, index):
        top_now, total_now = carry
        key_part, value_part, seg_block = kv_block(gathered_kv, index)
        scores = block_scores(key_part, seg_block)
        top_new = jnp.maximum(top_now, jnp.max(scores, axis=-1))
        total_new = total_now * jnp.exp(top_now - top_new) + jnp.sum(
            jnp.exp(scores - top_new[:, :, None]), axis=-1
        )
        return ((top_new, total_new), None)

    stats_init = (
        jnp.full((head_count, local_rows), -1e30, single),
        jnp.zeros((head_count, local_rows), single),
    )
    (top_all, total_all), _ = lax.scan(stats_step, stats_init, block_ids)
    log_total = top_all + jnp.log(total_all)

    def output_step(accum, index):
        key_part, value_part, seg_block = kv_block(gathered_kv, index)
        probs = jnp.exp(block_scores(key_part, seg_block) - log_total[:, :, None]).astype(bfloat)
        return (
            accum + jnp.einsum("hqk,khd->qhd", probs, value_part, preferred_element_type=single),
            None,
        )

    attended, _ = lax.scan(
        output_step, jnp.zeros((local_rows, head_count, head_size), single), block_ids
    )
    attended = attended.reshape(local_rows, width)
    branch_in = (attended * head_wide).astype(bfloat)
    attn_out = jnp.dot(branch_in, out_weight, preferred_element_type=single) + out_bias
    middle = inputs_float + gate_one * attn_out
    second_in = modulate(middle, shift_two, scale_two).astype(bfloat)
    hidden_pre = jnp.dot(second_in, up_weight, preferred_element_type=single) + up_bias
    hidden_act = (gelu_tanh(hidden_pre) * chan_keep).astype(bfloat)
    mlp_out = jnp.dot(hidden_act, down_weight, preferred_element_type=single) + down_bias
    output = (middle + gate_two * keep_float * mlp_out).astype(bfloat)
    upstream = cotangent.astype(single)
    mlp_grad = (gate_two * keep_float * upstream).astype(bfloat)
    gate_two_grad = jnp.sum(keep_float * upstream * mlp_out, axis=0)
    down_bias_grad = jnp.sum(mlp_grad, axis=0, dtype=single)
    down_grad = contract_rows(hidden_act, mlp_grad)
    act_grad = contract_last(mlp_grad, down_weight)
    _, gelu_back = jax.vjp(gelu_tanh, hidden_pre)
    pre_grad = gelu_back(act_grad * chan_keep)[0].astype(bfloat)
    up_grad = contract_rows(second_in, pre_grad)
    up_bias_grad = jnp.sum(pre_grad, axis=0, dtype=single)
    second_grad = contract_last(pre_grad, up_weight)
    _, norm_two_back = jax.vjp(modulate, middle, shift_two, scale_two)
    middle_norm_grad, shift_two_grad, scale_two_grad = norm_two_back(second_grad)
    middle_grad = upstream + middle_norm_grad
    branch_grad = (gate_one * middle_grad).astype(bfloat)
    gate_one_grad = jnp.sum(middle_grad * attn_out, axis=0)
    out_grad = contract_rows(branch_in, branch_grad)
    out_bias_grad = jnp.sum(branch_grad, axis=0, dtype=single)
    attended_grad = (contract_last(branch_grad, out_weight) * head_wide).astype(bfloat)
    delta_rows = jnp.sum(
        (attended_grad.astype(single) * attended).reshape(local_rows, head_count, head_size),
        axis=-1,
    ).T
    grad_heads = attended_grad.reshape(local_rows, head_count, head_size)

    def backward_step(query_accum, index):
        key_part, value_part, seg_block = kv_block(gathered_kv, index)
        probs = jnp.exp(block_scores(key_part, seg_block) - log_total[:, :, None])
        probs_low = probs.astype(bfloat)
        prob_grad = jnp.einsum(
            "qhd,khd->hqk", grad_heads, value_part, preferred_element_type=single
        )
        score_grad = (probs * (prob_grad - delta_rows[:, :, None])).astype(bfloat)
        query_accum = query_accum + jnp.einsum(
            "hqk,khd->qhd", score_grad, key_part, preferred_element_type=single
        )
        key_grad = (
            jnp.einsum("hqk,qhd->khd", score_grad, query_heads, preferred_element_type=single)
            * score_scale
        )
        value_grad = jnp.einsum(
            "hqk,qhd->khd", probs_low, grad_heads, preferred_element_type=single
        )
        block_terms = jnp.concatenate(
            [key_grad.reshape(block_rows, width), value_grad.reshape(block_rows, width)], axis=1
        )
        return (query_accum, block_terms)

    query_sum, kv_terms = lax.scan(
        backward_step, jnp.zeros((local_rows, head_count, head_size), single), block_ids
    )
    kv_terms = kv_terms.reshape(group_rows, 2 * width)
    kv_grad = lax.psum_scatter(
        kv_terms.astype(jnp.bfloat16), "seq", scatter_dimension=0, tiled=True
    ).astype(jnp.float32)
    projected_grad = jnp.concatenate(
        [(query_sum * score_scale).reshape(local_rows, width), kv_grad], axis=1
    ).astype(bfloat)
    qkv_grad = contract_rows(first_in, projected_grad)
    query_bias_grad = jnp.sum(projected_grad[:, :width], axis=0, dtype=single)
    value_bias_grad = jnp.sum(projected_grad[:, 2 * width :], axis=0, dtype=single)
    first_grad = contract_last(projected_grad, qkv_weight)
    _, norm_one_back = jax.vjp(modulate, inputs_float, shift_one, scale_one)
    input_norm_grad, shift_one_grad, scale_one_grad = norm_one_back(first_grad)
    token_grad = middle_grad + input_norm_grad
    modulation_grad = jnp.concatenate(
        [
            shift_one_grad,
            scale_one_grad,
            gate_one_grad,
            shift_two_grad,
            scale_two_grad,
            gate_two_grad,
        ]
    )
    ada_grad = silu_low.astype(single)[:, None] * modulation_grad[None, :]
    modulation_total = lax.psum(modulation_grad, "seq")
    silu_grad = jnp.dot(ada_weight, modulation_total, precision=HIGHEST)
    _, silu_back = jax.vjp(jax.nn.silu, condition[0])
    condition_grad = silu_back(silu_grad)[0][None]
    bias_grad = jnp.concatenate(
        [
            modulation_grad.reshape(6, width).T,
            query_bias_grad[:, None],
            value_bias_grad[:, None],
            out_bias_grad[:, None],
            up_bias_grad.reshape(width, hidden_ratio),
            down_bias_grad[:, None],
        ],
        axis=1,
    ).reshape(width * table_cols)
    row_sums = (
        lax.psum_scatter(ada_grad, "bucket", scatter_dimension=0, tiled=True),
        lax.psum_scatter(qkv_grad, "bucket", scatter_dimension=0, tiled=True),
        lax.psum_scatter(out_grad, "bucket", scatter_dimension=0, tiled=True),
        lax.psum_scatter(up_grad, "bucket", scatter_dimension=0, tiled=True),
        lax.psum_scatter(down_grad, "bucket", scatter_dimension=0, tiled=True),
        lax.psum_scatter(bias_grad, "bucket", scatter_dimension=0, tiled=True),
    )
    reduced = (
        lax.psum_scatter(
            row_sums[0].astype(jnp.bfloat16), "seq", scatter_dimension=1, tiled=True
        ).astype(jnp.float32),
        lax.psum_scatter(
            row_sums[1].astype(jnp.bfloat16), "seq", scatter_dimension=1, tiled=True
        ).astype(jnp.float32),
        lax.psum_scatter(
            row_sums[2].astype(jnp.bfloat16), "seq", scatter_dimension=1, tiled=True
        ).astype(jnp.float32),
        lax.psum_scatter(
            row_sums[3].astype(jnp.bfloat16), "seq", scatter_dimension=1, tiled=True
        ).astype(jnp.float32),
        lax.psum_scatter(
            row_sums[4].astype(jnp.bfloat16), "seq", scatter_dimension=1, tiled=True
        ).astype(jnp.float32),
        lax.psum_scatter(
            row_sums[5].astype(jnp.bfloat16), "seq", scatter_dimension=0, tiled=True
        ).astype(jnp.float32),
    )
    out_rate = (group_rows / (16.0 * width)) ** 0.5
    ada_new = adam_update(
        ada_master, ada_first, ada_second, ada_average, reduced[0], width ** (-0.5), MATRIX_DECAY
    )
    qkv_new = adam_update(
        qkv_master, qkv_first, qkv_second, qkv_average, reduced[1], width ** (-0.5), MATRIX_DECAY
    )
    out_new = adam_update(
        out_master, out_first, out_second, out_average, reduced[2], out_rate, MATRIX_DECAY
    )
    up_new = adam_update(
        up_master, up_first, up_second, up_average, reduced[3], width ** (-0.5), MATRIX_DECAY
    )
    down_new = adam_update(
        down_master,
        down_first,
        down_second,
        down_average,
        reduced[4],
        hidden_width ** (-0.5),
        MATRIX_DECAY,
    )
    bias_new = adam_update(bias_master, bias_first, bias_second, bias_average, reduced[5], 0.3, 0.0)
    return (
        output,
        token_grad,
        condition_grad,
        ada_new[0],
        ada_new[1],
        ada_new[2],
        ada_new[3],
        qkv_new[0],
        qkv_new[1],
        qkv_new[2],
        qkv_new[3],
        out_new[0],
        out_new[1],
        out_new[2],
        out_new[3],
        up_new[0],
        up_new[1],
        up_new[2],
        up_new[3],
        down_new[0],
        down_new[1],
        down_new[2],
        down_new[3],
        bias_new[0],
        bias_new[1],
        bias_new[2],
        bias_new[3],
    )


def solution(mesh):
    in_specs = (
        P(("bucket", "seq"), None),
        P("bucket", None),
        P(("bucket", "seq"), None),
        P("bucket", None),
        P("bucket"),
        P(("bucket", "seq")),
        P(),
        P(),
        P("bucket", "seq"),
        P("bucket", "seq"),
        P("bucket", "seq"),
        P("bucket", "seq"),
        P("bucket", "seq"),
        P("bucket", "seq"),
        P("bucket", "seq"),
        P("bucket", "seq"),
        P("bucket", "seq"),
        P("bucket", "seq"),
        P("bucket", "seq"),
        P("bucket", "seq"),
        P("bucket", "seq"),
        P("bucket", "seq"),
        P("bucket", "seq"),
        P("bucket", "seq"),
        P("bucket", "seq"),
        P("bucket", "seq"),
        P("bucket", "seq"),
        P("bucket", "seq"),
        P(("bucket", "seq")),
        P(("bucket", "seq")),
        P(("bucket", "seq")),
        P(("bucket", "seq")),
    )
    out_specs = (
        P(("bucket", "seq"), None),
        P(("bucket", "seq"), None),
        P("bucket", None),
        P("bucket", "seq"),
        P("bucket", "seq"),
        P("bucket", "seq"),
        P("bucket", "seq"),
        P("bucket", "seq"),
        P("bucket", "seq"),
        P("bucket", "seq"),
        P("bucket", "seq"),
        P("bucket", "seq"),
        P("bucket", "seq"),
        P("bucket", "seq"),
        P("bucket", "seq"),
        P("bucket", "seq"),
        P("bucket", "seq"),
        P("bucket", "seq"),
        P("bucket", "seq"),
        P("bucket", "seq"),
        P("bucket", "seq"),
        P("bucket", "seq"),
        P("bucket", "seq"),
        P(("bucket", "seq")),
        P(("bucket", "seq")),
        P(("bucket", "seq")),
        P(("bucket", "seq")),
    )
    return jax.shard_map(
        on_device, mesh=mesh, in_specs=in_specs, out_specs=out_specs, check_vma=False
    )
```

profile of v0, /device:TPU:0, one launch (start us, length us, event | category | flops | bytes accessed | tf_op | source)
XLA Modules:
  0.0 2989.1 jit_solution(18293778833768392632)
XLA Ops:
  9.4 25.9 all-gather.29.cloned.1.call-done
  63.0 38.4 %all-reduce.1 = bf16[16128]{0:T(1024)(128)(2,1)S(1)} all-reduce(bf16[16128]{0:T(1024)(128)(2,1)S(1)} %dynamic-update-slice.1), channel_id=1, replica_groups=mesh['bucket'=8,'seq'=4] {'bucket'}, use_global_device_ids=true, to_apply=%add.1 | all-reduce | flops 16128 | bytes 64512
  105.3 153.5 %all-gather.13.cloned.1.call-done = bf16[1152,6912]{1,0:T(8,128)(2,1)} async-done(((bf16[144,6912]{1,0:T(8,128)(2,1)}), bf16[1152,6912]{1,0:T(8,128)(2,1)}) %all-gather.13.cloned.1.call-update) | async-done | bytes 15925264 | tf_op jit(solution)/shard_map/all_gather | solution.py:115
  267.1 112.2 %all-gather.15.cloned.1.call-done = bf16[1152,3456]{1,0:T(8,128)(2,1)} async-done(((bf16[144,3456]{1,0:T(8,128)(2,1)}), bf16[1152,3456]{1,0:T(8,128)(2,1)}) %all-gather.15.cloned.1.call-update) | async-done | bytes 7962640 | tf_op jit(solution)/shard_map/all_gather | solution.py:116
  406.9 59.0 %all-gather.17.cloned.1.call-done = bf16[2048,2304]{1,0:T(8,128)(2,1)} async-done(((bf16[512,2304]{1,0:T(8,128)(2,1)}), bf16[2048,2304]{1,0:T(8,128)(2,1)}) %all-gather.17.cloned.1.call-update) | async-done | bytes 9437200 | tf_op jit(solution)/shard_map/all_gather | solution.py:150
  478.6 84.5 %while.37 = (s32[]{:T(128)}, f32[16,512]{1,0:T(8,128)S(1)}, f32[16,512]{1,0:T(8,128)S(1)}, s32[512]{0:T(512)S(1)}, s32[4]{0:T(128)S(1)}, /*index=5*/s32[2048]{0:...) while((s32[]{:T(128)}, f32[16,512]{1,0:T(8,128)S(1)}, ...), condition=%wide.region_8.9_spmd.clone, body=%wide.region_5.8_spmd.clone.sunk | while | flops 633643008 | bytes 39493824 | solution.py:184
  563.7 52.9 %while.38 = (s32[]{:T(128)}, f32[512,16,72]{0,2,1:T(8,128)}, s32[4]{0:T(128)S(1)}, bf16[2048,2304]{0,1:T(8,128)(2,1)}, s32[512]{0:T(512)S(1)}, /*index=5*/s32[20...) while((s32[]{:T(128)}, f32[512,16,72]{0,2,1:T(8,128)}, ...), condition=%wide.region_10.11_spmd.clone, body=%wide.region_9.10_spmd.clone.sunk | while | flops 1226178560 | bytes 13541593 | solution.py:195
  627.0 49.8 %all-gather.23.cloned.1.call-done = bf16[1152,4608]{1,0:T(8,128)(2,1)} async-done(((bf16[144,4608]{1,0:T(8,128)(2,1)}), bf16[1152,4608]{1,0:T(8,128)(2,1)}) %all-gather.23.cloned.1.call-update) | async-done | bytes 10616848 | tf_op jit(solution)/shard_map/all_gather | solution.py:118
  703.9 345.6 %reduce-scatter.32.cloned.1.call-done = f32[576,1152]{1,0:T(8,128)} async-done(((f32[4608,1152]{1,0:T(8,128)}), f32[576,1152]{1,0:T(8,128)}) %reduce-scatter.32.cloned.1.call-update) | async-done | bytes 2654224 | tf_op jit(solution)/shard_map/reduce_scatter | solution.py:303
  1055.2 26.8 reduce-scatter.42.cloned.1.call-done
  1086.3 19.2 all-gather.25.cloned.1.call-done
  1108.2 152.5 %all-gather.27.cloned.1.call-done = bf16[4608,1152]{1,0:T(8,128)(2,1)} async-done(((bf16[576,1152]{1,0:T(8,128)(2,1)}), bf16[4608,1152]{1,0:T(8,128)(2,1)}) %all-gather.27.cloned.1.call-update) | async-done | bytes 10616848 | tf_op jit(solution)/shard_map/all_gather | solution.py:119
  1260.7 18.1 convert_reduce_fusion
  1302.6 215.4 %while.39 = (s32[]{:T(128)}, f32[512,16,72]{0,2,1:T(8,128)}, bf16[4,512,2304]{2,1,0:T(8,128)(2,1)}, s32[4]{0:T(128)S(1)}, bf16[2048,2304]{0,1:T(8,128)(2,1)}, /*...) while((s32[]{:T(128)}, f32[512,16,72]{0,2,1:T(8,128)}, ...), condition=%wide.region_17.18_spmd.clone, body=%wide.region_16.17_spmd.clone.sunk | while | flops 3069181952 | bytes 163029840 | solution.py:255
  1545.4 49.5 %reduce-scatter.22.cloned.1.call-done = bf16[512,2304]{1,0:T(8,128)(2,1)} async-done(((bf16[2048,2304]{1,0:T(8,128)(2,1)}), bf16[512,2304]{1,0:T(8,128)(2,1)}) %reduce-scatter.22.cloned.1.call-update) | async-done | bytes 2359312 | tf_op jit(solution)/shard_map/reduce_scatter | solution.py:259
  1617.8 16.5 convert_reduce_fusion.2
  1645.6 15.2 convolution_reduce_fusion.2
  1671.7 30.8 %reduce-scatter.28.cloned.1.call-done = f32[144,1152]{1,0:T(8,128)} async-done(((f32[1152,1152]{1,0:T(8,128)}), f32[144,1152]{1,0:T(8,128)}) %reduce-scatter.28.cloned.1.call-update) | async-done | bytes 663568 | tf_op jit(solution)/shard_map/reduce_scatter | solution.py:301
  1704.8 349.0 %reduce-scatter.30.cloned.1.call-done = f32[144,4608]{1,0:T(8,128)} async-done(((f32[1152,4608]{1,0:T(8,128)}), f32[144,4608]{1,0:T(8,128)}) %reduce-scatter.30.cloned.1.call-update) | async-done | bytes 2654224 | tf_op jit(solution)/shard_map/reduce_scatter | solution.py:302
  2058.2 267.8 %reduce-scatter.26.cloned.1.call-done = f32[144,3456]{1,0:T(8,128)} async-done(((f32[1152,3456]{1,0:T(8,128)}), f32[144,3456]{1,0:T(8,128)}) %reduce-scatter.26.cloned.1.call-update) | async-done | bytes 1990672 | tf_op jit(solution)/shard_map/reduce_scatter | solution.py:300
  2329.4 512.1 %reduce-scatter.24.cloned.1.call-done = f32[144,6912]{1,0:T(8,128)} async-done(((f32[1152,6912]{1,0:T(8,128)}), f32[144,6912]{1,0:T(8,128)}) %reduce-scatter.24.cloned.1.call-update) | async-done | bytes 3981328 | tf_op jit(solution)/shard_map/reduce_scatter | solution.py:299
  2850.6 15.1 reduce-scatter.38.cloned.1.call-done
  2870.7 37.5 %all-reduce.2 = bf16[16128]{0:T(1024)(128)(2,1)S(1)} all-reduce(f32[16128]{0:T(1024)S(1)} %reshape.336), channel_id=13, replica_groups=mesh['bucket'=8,'seq'=4] {'bucket'}, use_global_device_ids=true, to_apply=%region_43.44.clone | all-reduce | flops 16128 | bytes 96768
  2937.7 38.6 %reduce-scatter.34.cloned.1.call-done = bf16[1728,144]{1,0:T(8,128)(2,1)} async-done(((bf16[6912,144]{1,0:T(8,128)(2,1)}), bf16[1728,144]{1,0:T(8,128)(2,1)}) %reduce-scatter.34.cloned.1.call-update) | async-done | bytes 497680
  (468 shorter events, 626.6 us)
Async XLA Ops:
  7.2 28.1 all-gather.29.cloned.1.call-start
  9.3 249.5 %all-gather.13.cloned.1.call-start = ((), (), s32[]{:S(2)}) async-start(), calls=%async_computation.11 | async-start | bytes 17915904 | tf_op jit(solution)/shard_map/all_gather | solution.py:115
  40.8 338.6 %all-gather.15.cloned.1.call-start = ((), (), s32[]{:S(2)}) async-start(), calls=%async_computation.12 | async-start | bytes 8957952 | tf_op jit(solution)/shard_map/all_gather | solution.py:116
  53.0 352.4 %all-gather.21.cloned.1.call-start = ((), (), s32[]{:S(2)}) async-start(), calls=%async_computation.15 | async-start | bytes 1658880 | tf_op jit(solution)/shard_map/all_gather | solution.py:110
  53.9 412.1 %all-gather.17.cloned.1.call-start = ((), (), s32[]{:S(2)}) async-start(), calls=%async_computation.13 | async-start | bytes 11796480 | tf_op jit(solution)/shard_map/all_gather | solution.py:150
  104.2 275.2 %copy-start.35 = (f32[512]{0:T(512)}, f32[512]{0:T(512)S(1)}, u32[]{:S(2)}) copy-start(f32[512]{0:T(512)S(1)} %broadcast_multiply_fusion.2) | copy-start | bytes 6148
  104.7 274.7 %copy-start.41 = (f32[512]{0:T(512)}, f32[512]{0:T(512)S(1)}, u32[]{:S(2)}) copy-start(f32[512]{0:T(512)S(1)} %fusion.62) | copy-start | bytes 6148
  391.6 227.1 %all-gather.19.cloned.1.call-start = ((), (), s32[]{:S(2)}) async-start(), calls=%async_computation.14 | async-start | bytes 2985984 | tf_op jit(solution)/shard_map/all_gather | solution.py:117
  400.8 276.0 %all-gather.23.cloned.1.call-start = ((), (), s32[]{:S(2)}) async-start(), calls=%async_computation.16 | async-start | bytes 11943936 | tf_op jit(solution)/shard_map/all_gather | solution.py:118
  405.5 644.0 %reduce-scatter.32.cloned.1.call-start = ((), (), s32[]{:S(2)}) async-start(), calls=%async_computation.24 | async-start | bytes 23887872 | tf_op jit(solution)/shard_map/reduce_scatter | solution.py:303
  618.6 674.5 %copy-start.6 = (f32[512,1152]{1,0:T(8,128)}, f32[512,1152]{1,0:T(8,128)S(1)}, u32[]{:S(2)}) copy-start(f32[512,1152]{1,0:T(8,128)S(1)} %copy.235) | copy-start | bytes 7077892
  624.5 666.4 %copy-start.57 = (f32[512]{0:T(512)}, f32[512]{0:T(512)S(1)}, u32[]{:S(2)}) copy-start(f32[512]{0:T(512)S(1)} %broadcast_multiply_fusion.1) | copy-start | bytes 6148
  703.9 378.1 %reduce-scatter.42.cloned.1.call-start = ((), (), s32[]{:S(2)}) async-start(), calls=%async_computation.30 | async-start | bytes 1843200
  1055.1 50.4 %all-gather.25.cloned.1.call-start = ((), (), s32[]{:S(2)}) async-start(), calls=%async_computation.17 | async-start | bytes 1843200 | tf_op jit(solution)/shard_map/all_gather | solution.py:111
  1086.2 174.5 %all-gather.27.cloned.1.call-start = ((), (), s32[]{:S(2)}) async-start(), calls=%async_computation.18 | async-start | bytes 11943936 | tf_op jit(solution)/shard_map/all_gather | solution.py:119
  1108.1 486.8 %reduce-scatter.22.cloned.1.call-start = ((), (), s32[]{:S(2)}) async-start(), calls=%async_computation.19 | async-start | bytes 11796480 | tf_op jit(solution)/shard_map/reduce_scatter | solution.py:259
  1518.1 184.5 %reduce-scatter.28.cloned.1.call-start = ((), (), s32[]{:S(2)}) async-start(), calls=%async_computation.22 | async-start | bytes 5971968 | tf_op jit(solution)/shard_map/reduce_scatter | solution.py:301
  1524.1 529.7 %reduce-scatter.30.cloned.1.call-start = ((), (), s32[]{:S(2)}) async-start(), calls=%async_computation.23 | async-start | bytes 23887872 | tf_op jit(solution)/shard_map/reduce_scatter | solution.py:302
  1540.1 785.9 %reduce-scatter.26.cloned.1.call-start = ((), (), s32[]{:S(2)}) async-start(), calls=%async_computation.21 | async-start | bytes 17915904 | tf_op jit(solution)/shard_map/reduce_scatter | solution.py:300
  1605.0 1236.6 %reduce-scatter.24.cloned.1.call-start = ((), (), s32[]{:S(2)}) async-start(), calls=%async_computation.20 | async-start | bytes 35831808 | tf_op jit(solution)/shard_map/reduce_scatter | solution.py:299
  1671.7 1194.1 %reduce-scatter.38.cloned.1.call-start = ((), (), s32[]{:S(2)}) async-start(), calls=%async_computation.28 | async-start | bytes 737280
  1704.8 1211.1 %reduce-scatter.40.cloned.1.call-start = ((), (), s32[]{:S(2)}) async-start(), calls=%async_computation.29 | async-start | bytes 2949120
  2058.1 875.3 %reduce-scatter.36.cloned.1.call-start = ((), (), s32[]{:S(2)}) async-start(), calls=%async_computation.27 | async-start | bytes 2211840
  2329.4 646.9 %reduce-scatter.34.cloned.1.call-start = ((), (), s32[]{:S(2)}) async-start(), calls=%async_computation.26 | async-start | bytes 4423680
  (91 other events, 1545.0 us)
Sparse Core Ops, SparseCore 0:
  10.2 25.0 all-gather.28
  40.9 217.8 all-gather.12
  261.5 117.7 all-gather.14
  381.4 16.6 all-gather.20
  399.4 66.4 all-gather.16
  468.5 55.0 all-gather.18
  525.7 151.0 all-gather.22
  704.0 345.4 reduce-scatter.31
  1055.2 26.7 reduce-scatter.41
  1086.4 19.0 all-gather.24
  1108.2 152.4 all-gather.26
  1518.2 76.5 reduce-scatter.21
  1598.5 104.0 reduce-scatter.27
  1706.8 346.9 reduce-scatter.29
  2057.5 268.3 reduce-scatter.25
  2329.7 511.7 reduce-scatter.23
  2844.5 21.1 reduce-scatter.37
  2868.1 33.0 reduce-scatter.39
  2904.0 29.3 reduce-scatter.35
  2935.8 40.4 reduce-scatter.33
where the time goes:
time: 3000 us; the launch traced here: 2990 us
  waiting for transfers between devices  2220 us (74%)
  matrix products  384 us (13%)
  local copies, waits for them, and re-layouts  135 us (4%)
  blocking collectives  117 us (4%)
  other arithmetic  102 us (3%)
    reduce_scatter x1, waiting for transfers between devices, on_device(): lax.psum_scatter(ada_grad, 'bucket', scatter_dimension=0, tiled=True)  512 us
    reduce_scatter x1, waiting for transfers between devices, on_device(): lax.psum_scatter(up_grad, 'bucket', scatter_dimension=0, tiled=True)  349 us
    reduce_scatter x1, waiting for transfers between devices, on_device(): lax.psum_scatter(down_grad, 'bucket', scatter_dimension=0, tiled=True)  346 us
    reduce_scatter x1, waiting for transfers between devices, on_device(): lax.psum_scatter(qkv_grad, 'bucket', scatter_dimension=0, tiled=True)  268 us
    all_gather x1, waiting for transfers between devices, on_device(): lax.all_gather(seq_whole[0], 'bucket', axis=0, tiled=True)  154 us
    all_gather x1, waiting for transfers between devices, on_device(): lax.all_gather(seq_whole[4], 'bucket', axis=0, tiled=True)  153 us
    all_gather x1, waiting for transfers between devices, on_device(): lax.all_gather(seq_whole[1], 'bucket', axis=0, tiled=True)  112 us
    unnamed x25, waiting for transfers between devices  95.1 us
  transfers between devices with their start and end apart: 20, of which 17 were waited for; matrix products, arithmetic and copies ran while one was open for 10% of the time, Pallas kernels for 0%

commit v1 on v0

v1 whole, which is shorter than its diff:
```python
import functools
import math

import jax
import jax.numpy as jnp
from jax import lax
from jax.experimental import pallas as pl
from jax.experimental.pallas import tpu as pltpu
from jax.sharding import PartitionSpec as P

STEP = 10


EPSILON = 1e-06
BETA_FIRST = 0.5
BETA_SECOND = 0.5
ADAM_EPSILON = 1e-08
MATRIX_DECAY = 0.01
EMA_DECAY = 0.9999
HIGHEST = lax.Precision.HIGHEST
LOG2E = math.log2(math.e)
LANES = 128
TILE = 256
VMEM_LIMIT = 60 * 1024 * 1024
bfloat = jnp.bfloat16
single = jnp.float32


def layer_norm(values):
    centre = values - jnp.mean(values, axis=-1, keepdims=True)
    spread = jnp.mean(centre * centre, axis=-1, keepdims=True)
    return centre * lax.rsqrt(spread + EPSILON)


def modulate(values, shift_row, scale_row):
    return layer_norm(values) * (1.0 + scale_row) + shift_row


def dot_nn(left, right):
    return lax.dot_general(left, right, (((1,), (0,)), ((), ())), preferred_element_type=single)


def dot_nt(left, right):
    return lax.dot_general(left, right, (((1,), (1,)), ((), ())), preferred_element_type=single)


def dot_tn(left, right):
    return lax.dot_general(left, right, (((0,), (0,)), ((), ())), preferred_element_type=single)


def adam_update(master, moment_one, moment_two, average, gradient, step_rate, decay_rate):
    one_new = BETA_FIRST * moment_one + (1.0 - BETA_FIRST) * gradient
    two_new = BETA_SECOND * moment_two + (1.0 - BETA_SECOND) * gradient * gradient
    one_hat = one_new / (1.0 - BETA_FIRST**STEP)
    two_hat = two_new / (1.0 - BETA_SECOND**STEP)
    master_new = master - step_rate * (
        one_hat / (jnp.sqrt(two_hat) + ADAM_EPSILON) + decay_rate * master
    )
    average_decay = min(EMA_DECAY, (1.0 + STEP) / (10.0 + STEP))
    average_new = average_decay * average + (1.0 - average_decay) * master_new
    return (master_new, one_new, two_new, average_new)


def params(*semantics):
    return pltpu.CompilerParams(
        dimension_semantics=semantics or None, vmem_limit_bytes=VMEM_LIMIT
    )


def cost(flops, moved, exps=0):
    return pl.CostEstimate(flops=int(flops), bytes_accessed=int(moved), transcendentals=int(exps))


def exchange(values, axis, bit):
    count = lax.axis_size(axis)
    return lax.ppermute(values, axis, [(i, i ^ bit) for i in range(count)])


def pick(values, index, axis):
    return lax.dynamic_index_in_dim(values, index, axis, keepdims=False)


IN_VMEM = pl.BlockSpec(memory_space=pltpu.VMEM)
IN_HBM = pl.BlockSpec(memory_space=pl.ANY)


def cube_path():
    return lax.axis_size("bucket") == 8 and lax.axis_size("seq") == 4


BLOCKS, PLANES = 8, 4
X, Z0, Z1, CORE, Y = ("bucket", 1), ("bucket", 2), ("bucket", 4), ("seq", 1), ("seq", 2)


def gather_all(block, layout):
    width = block.shape[1]
    if layout == "rows":
        return lax.all_gather(block, ("bucket", "seq"), axis=0, tiled=True)
    tall = lax.all_gather(block, "bucket", axis=0, tiled=True)
    return lax.all_gather(tall, "seq", axis=0)


def place_in_kernel():
    if cube_path():
        return lax.axis_index("bucket"), lax.axis_index("seq")
    return 0, 0


DIMS = {"planes": (Y, CORE, Z1, Z0, X), "rows": (Z1, Z0, X, Y, CORE)}
MESH = pl.DeviceIdType.MESH


def my_coords():
    bucket, seq = lax.axis_index("bucket"), lax.axis_index("seq")
    return {
        (axis, amount): ((bucket if axis == "bucket" else seq) // amount) % 2
        for axis, amount in (X, Z0, Z1, CORE, Y)
    }


def partner(bit):
    bucket, seq = lax.axis_index("bucket"), lax.axis_index("seq")
    axis, amount = bit
    return (bucket ^ amount, seq) if axis == "bucket" else (bucket, seq ^ amount)


def peer_at(distance):
    bucket, seq = lax.axis_index("bucket"), lax.axis_index("seq")
    return bucket ^ (distance >> 2), seq ^ (distance & 3)


def greet(peers):
    barrier = pltpu.get_barrier_semaphore()
    for peer in peers:
        pl.semaphore_signal(barrier, inc=1, device_id=peer, device_id_type=MESH)
    pl.semaphore_wait(barrier, len(peers))


class Gathering:
    def __init__(self, own, out, layout, order, first, rows, send, recv, base):
        self.own, self.out, self.dims, self.order = own, out, DIMS[layout], order
        self.first, self.rows, self.send, self.recv, self.base = first, rows, send, recv, base
        self.me = my_coords()

    def view(self, free, flipped=None):
        index = tuple(
            slice(None)
            if dim in free
            else (1 - self.me[dim] if dim == flipped else self.me[dim])
            for dim in self.dims
        )
        return self.out.at[index + (pl.ds(self.first, self.rows), slice(None))]

    def copy(self, source, place, slot, bit):
        return pltpu.make_async_remote_copy(
            src_ref=source,
            dst_ref=place,
            send_sem=self.send.at[self.base + slot],
            recv_sem=self.recv.at[self.base + slot],
            device_id=partner(bit),
            device_id_type=MESH,
        )

    def hop(self, phase):
        place = self.view(self.order[:phase])
        source = self.own if phase == 0 else place
        return self.copy(source, place, phase, self.order[phase])

    def across(self, phase):
        if phase == 0:
            return self.copy(self.own, self.view(()), 4, CORE)
        place = self.view(self.order[: phase - 1], self.order[phase - 1])
        return self.copy(place, place, 4 + phase, CORE)

    def keep(self):
        return pltpu.make_async_copy(self.own, self.view(()), self.send.at[self.base + 9])

    def begin(self):
        self.hop(0).start()
        self.across(0).start()
        self.keep().start()

    def advance(self, phase):
        if phase == 0:
            self.keep().wait()
        self.hop(phase).wait_recv()
        if phase < 3:
            self.hop(phase + 1).start()
        self.across(phase + 1).start()

    def finish(self):
        for phase in range(5):
            self.across(phase).wait_recv()
        for phase in range(4):
            self.hop(phase).wait_send()
        for phase in range(5):
            self.across(phase).wait_send()


GATHER_SEMS = 10
PAIR_SHARES = (32, 32, 32, 32, 16)
REST_SHARES = (48, 48, 48)
PAIR_PARTS = (
    (Z1, Y, X, Z0),
    (Z1, X, Y, Z0),
    (Z1, Z0, X, Y),
    (Z1, Z0, Y, X),
    (Z1, Z0, X, Y),
)
PAIR_EVENTS = (
    (0, 0), (1, 0), (2, 0), (0, 1), (3, 0), (1, 1), (4, 0), (2, 1), (0, 2), (3, 1),
    (1, 2), (2, 2), (4, 1), (3, 2), (4, 2), (2, 3), (0, 3), (3, 3), (4, 3), (1, 3),
)
UP_PARTS = (
    (Z1, Y, Z0, X),
    (Z1, Y, X, Z0),
    (Z1, X, Z0, Y),
)
DOWN_PARTS = (
    (Z1, Z0, Y, X),
    (Z0, Z1, Y, X),
    (Y, Z1, X, Z0),
)
REST_EVENTS = (
    (5, 0), (0, 0), (1, 0), (0, 1), (2, 0), (1, 1), (3, 0), (4, 0), (2, 1), (5, 1),
    (1, 2), (0, 2), (5, 2), (3, 1), (4, 1), (3, 2), (0, 3), (2, 2), (4, 2), (3, 3),
    (1, 3), (2, 3), (4, 3), (5, 3),
)
PAIR_SUM_PARTS = (
    (Y, X, Z0, Z1),
    (X, Z0, Y, Z1),
    (Z0, X, Y, Z1),
    (Y, Z0, X, Z1),
    (Y, X, Z0, Z1),
)
PAIR_SUM_EVENTS = (
    (0, -1), (1, -1), (2, -1), (3, -1), (4, -1), (0, 0), (1, 0), (2, 0), (0, 1), (1, 1),
    (3, 0), (2, 1), (0, 2), (4, 0), (1, 2), (3, 1), (4, 1), (2, 2), (0, 3), (1, 3),
    (3, 2), (4, 2), (2, 3), (3, 3), (4, 3),
)
UP_SUM_PARTS = (
    (X, Y, Z0, Z1),
    (Z0, X, Y, Z1),
    (X, Y, Z0, Z1),
)
DOWN_SUM_PARTS = (
    (Z0, X, Y, Z1),
    (Z0, X, Y, Z1),
    (X, Y, Z0, Z1),
)
REST_SUM_EVENTS = (
    (0, -1), (1, -1), (2, -1), (3, -1), (4, -1), (5, -1), (0, 0), (1, 0), (0, 1), (2, 0),
    (3, 0), (2, 1), (5, 0), (4, 0), (0, 2), (1, 1), (2, 2), (5, 1), (0, 3), (1, 2),
    (3, 1), (2, 3), (5, 2), (3, 2), (4, 1), (1, 3), (5, 3), (4, 2), (3, 3), (4, 3),
)
NOTE_EVENT = 5
KV_EVENTS = (2, 6, 10, 14)


def split_gatherings(block_ref, out_ref, layout, shares, orders, send, recv, base):
    moving, first = [], 0
    for index, (count, order) in enumerate(zip(shares, orders)):
        own = block_ref.at[pl.ds(first, count), :]
        slot = base + GATHER_SEMS * index
        moving.append(Gathering(own, out_ref, layout, order, first, count, send, recv, slot))
        first += count
    return moving


def first_gather_kernel(
    note_ref,
    ada_ref,
    block_ref,
    out_ref,
    inbox_ref,
    silu_ref,
    mod_ref,
    parts,
    returns,
    note_send,
    note_recv,
    mod_send,
    mod_recv,
    send,
    recv,
):
    bucket, seq = lax.axis_index("bucket"), lax.axis_index("seq")
    me = bucket * PLANES + seq
    count = BLOCKS * PLANES
    barrier = pltpu.get_barrier_semaphore()

    @pl.loop(1, count)
    def _(distance):
        pl.semaphore_signal(barrier, inc=1, device_id=peer_at(distance), device_id_type=MESH)

    pl.semaphore_wait(barrier, count - 1)

    def note(distance):
        peer = peer_at(distance)
        return pltpu.make_async_remote_copy(
            src_ref=note_ref.at[peer[0] * PLANES + peer[1]],
            dst_ref=inbox_ref.at[me],
            send_sem=note_send.at[distance],
            recv_sem=note_recv.at[distance],
            device_id=peer,
            device_id_type=MESH,
        )

    def answer(distance):
        peer = peer_at(distance)
        return pltpu.make_async_remote_copy(
            src_ref=parts.at[peer[0]],
            dst_ref=returns.at[me],
            send_sem=mod_send.at[distance],
            recv_sem=mod_recv.at[distance],
            device_id=peer,
            device_id_type=MESH,
        )

    @pl.loop(1, count)
    def _(distance):
        note(distance).start()

    inbox_ref[me] = note_ref[me]
    moving = split_gatherings(
        block_ref, out_ref, "planes", PAIR_SHARES, PAIR_PARTS, send, recv, 0
    )
    for part in moving:
        part.begin()

    for part, phase in PAIR_EVENTS[:NOTE_EVENT]:
        moving[part].advance(phase)

    @pl.loop(1, count)
    def _(distance):
        note(distance).wait_recv()

    rows = ada_ref.shape[0]
    heard = jnp.concatenate([inbox_ref[PLANES * g, :, :] for g in range(BLOCKS)])
    silu = jax.nn.silu(heard[:, :rows]).astype(bfloat)
    silu_ref[...] = silu
    mods = dot_nn(silu, ada_ref[...])
    for group in range(BLOCKS):
        parts[group] = mods[group : group + 1, :]
    returns[me] = parts[bucket]

    @pl.loop(1, count)
    def _(distance):
        answer(distance).start()

    for part, phase in PAIR_EVENTS[NOTE_EVENT:]:
        moving[part].advance(phase)

    @pl.loop(1, count)
    def _(distance):
        answer(distance).wait_recv()

    for plane in range(PLANES):
        mod_ref[plane] = sum(returns[PLANES * g + plane] for g in range(BLOCKS))
    for part in moving:
        part.finish()

    @pl.loop(1, count)
    def _(distance):
        note(distance).wait_send()
        answer(distance).wait_send()


def first_gather(notes, ada_low, block):
    rows, width = block.shape
    count = BLOCKS * PLANES
    cols = ada_low.shape[1]
    out, inbox, silu, mods = pl.pallas_call(
        first_gather_kernel,
        out_shape=(
            jax.ShapeDtypeStruct((2, 2, 2, 2, 2, rows, width), bfloat),
            jax.ShapeDtypeStruct(notes.shape, single),
            jax.ShapeDtypeStruct((BLOCKS, rows), bfloat),
            jax.ShapeDtypeStruct((PLANES, 1, cols), single),
        ),
        in_specs=[IN_VMEM] * 3,
        out_specs=(IN_HBM, IN_VMEM, IN_VMEM, IN_VMEM),
        scratch_shapes=[
            pltpu.VMEM((BLOCKS, 1, cols), single),
            pltpu.VMEM((count, 1, cols), single),
        ]
        + [pltpu.SemaphoreType.DMA((count,))] * 4
        + [pltpu.SemaphoreType.DMA((len(PAIR_PARTS) * GATHER_SEMS,))] * 2,
        compiler_params=pltpu.CompilerParams(
            collective_id=1, has_side_effects=True, vmem_limit_bytes=VMEM_LIMIT
        ),
        cost_estimate=cost(0, 64 * rows * width),
        name="first_gather",
    )(notes, ada_low, block)
    return out.reshape(PLANES, BLOCKS * rows, width), inbox, silu, mods


def second_gather_kernel(
    up_ref, down_ref, kv_ref, up_out, down_out, kv_out, send, recv
):
    me = my_coords()
    greet([partner(bit) for bit in (X, Z0, Z1, CORE, Y)])
    base = len(UP_PARTS) * GATHER_SEMS
    moving = split_gatherings(
        up_ref, up_out, "planes", REST_SHARES, UP_PARTS, send, recv, 0
    )
    moving += split_gatherings(
        down_ref, down_out, "rows", REST_SHARES, DOWN_PARTS, send, recv, base
    )
    base = len(moving) * GATHER_SEMS

    def kv_copy(source, place, slot, bit):
        return pltpu.make_async_remote_copy(
            src_ref=source,
            dst_ref=place,
            send_sem=send.at[base + slot],
            recv_sem=recv.at[base + slot],
            device_id=partner(bit),
            device_id_type=MESH,
        )

    count = kv_ref.shape[0] // len(KV_EVENTS)
    overs, nears, fars, keeps = [], [], [], []
    for index in range(len(KV_EVENTS)):
        rows = pl.ds(index * count, count)
        own = kv_ref.at[rows, :]
        mine = kv_out.at[me[Y], me[CORE], rows, :]
        other = kv_out.at[1 - me[Y], me[CORE], rows, :]
        overs.append(kv_copy(own, mine, 4 * index, Y))
        nears.append(kv_copy(own, mine, 4 * index + 1, CORE))
        fars.append(kv_copy(other, other, 4 * index + 2, CORE))
        keeps.append(pltpu.make_async_copy(own, mine, send.at[base + 4 * index + 3]))
    for part in moving:
        part.begin()
    for copy in nears + keeps:
        copy.start()
    for index, (part, phase) in enumerate(REST_EVENTS):
        for piece, event in enumerate(KV_EVENTS):
            if index == event:
                overs[piece].start()
        moving[part].advance(phase)
    for over, far in zip(overs, fars):
        over.wait_recv()
        far.start()
    for part in moving:
        part.finish()
    for over, near, far, keep in zip(overs, nears, fars, keeps):
        near.wait_recv()
        far.wait_recv()
        keep.wait()
        for copy in (over, near, far):
            copy.wait_send()


def second_gather(up_block, down_block, key_value):
    rows, width = up_block.shape
    local, wide = key_value.shape
    blocks = jax.ShapeDtypeStruct((2, 2, 2, 2, 2, rows, width), bfloat)
    up, down, kv = pl.pallas_call(
        second_gather_kernel,
        out_shape=(blocks, blocks, jax.ShapeDtypeStruct((2, 2, local, wide), bfloat)),
        in_specs=[IN_VMEM] * 3,
        out_specs=(IN_HBM,) * 3,
        scratch_shapes=[pltpu.SemaphoreType.DMA(((len(UP_PARTS) + len(DOWN_PARTS)) * GATHER_SEMS + 4 * len(KV_EVENTS),))] * 2,
        compiler_params=pltpu.CompilerParams(
            collective_id=2, has_side_effects=True, vmem_limit_bytes=VMEM_LIMIT
        ),
        cost_estimate=cost(0, 128 * rows * width),
        name="second_gather",
    )(up_block, down_block, key_value)
    count = BLOCKS * PLANES * rows
    return (
        up.reshape(PLANES, BLOCKS * rows, width),
        down.reshape(count, width),
        kv.reshape(PLANES * local, wide),
    )


def slot_of(bucket_bits, seq_bits):
    slot = 0
    for axis, amount in SLOT_DIMS:
        bits = bucket_bits if axis == "bucket" else seq_bits
        slot = slot * 2 + ((bits >> amount.bit_length() - 1) & 1)
    return slot


def natural_sum(far, near, layout):
    width = far.shape[2]
    both = jnp.concatenate([near, far])
    index = {
        (b, s): slot_of(b, s) + near.shape[0] * (s % 2)
        for b in range(BLOCKS)
        for s in range(PLANES)
    }
    if layout == "rows":
        picked = [index[b, s] for b in range(BLOCKS) for s in range(PLANES)]
        gradient = jnp.stack([both[k] for k in picked]).reshape(-1, width)
        part = lax.psum_scatter(gradient, ("bucket", "seq"), scatter_dimension=0, tiled=True)
        return part.astype(single)
    picked = [index[b, s] for s in range(PLANES) for b in range(BLOCKS)]
    gradient = jnp.stack([both[k] for k in picked]).reshape(PLANES, -1, width)
    part = lax.psum_scatter(gradient, "seq", scatter_dimension=0)
    return lax.psum_scatter(part, "bucket", scatter_dimension=0, tiled=True).astype(single)


SLOT_DIMS = (Y, X, Z1, Z0)


class Scattering:
    def __init__(self, far, near, total, arrivals, out, order, first, rows, send, recv, base):
        self.far, self.near, self.total, self.arrivals = far, near, total, arrivals
        self.out, self.order, self.first, self.rows = out, order, first, rows
        self.send, self.recv, self.base = send, recv, base
        self.span = (pl.ds(first, rows), slice(None))

    def copy(self, source, place, slot, bit):
        return pltpu.make_async_remote_copy(
            src_ref=source,
            dst_ref=place,
            send_sem=self.send.at[self.base + slot],
            recv_sem=self.recv.at[self.base + slot],
            device_id=partner(bit),
            device_id_type=MESH,
        )

    def across(self):
        index = (slice(None),) * 4 + self.span
        return self.copy(self.far.at[index], self.total.at[index], 4, CORE)

    def place(self, fixed):
        return tuple(fixed.get(dim, slice(None)) for dim in SLOT_DIMS)

    def hop(self, phase):
        fixed = {dim: 0 for dim in self.order[:phase]} | {self.order[phase]: 1}
        source = self.total.at[self.place(fixed) + self.span]
        place = self.arrivals[phase].at[(slice(None),) * (3 - phase) + self.span]
        return self.copy(source, place, phase, self.order[phase])

    def add(self, fixed, source, source_dims):
        free = [dim for dim in SLOT_DIMS if dim not in fixed]

        def one(step):
            index = dict(fixed)
            for place, dim in enumerate(free):
                index[dim] = (step >> place) & 1
            spot = tuple(index[dim] for dim in SLOT_DIMS) + self.span
            term = source[tuple(index[dim] for dim in source_dims) + self.span]
            self.total[spot] = (self.total[spot].astype(single) + term.astype(single)).astype(
                bfloat
            )

        if free:
            pl.loop(0, 2 ** len(free))(one)
        else:
            one(0)

    def advance(self, phase):
        if phase < 0:
            self.across().wait_recv()
            source, dims, fixed = self.near, SLOT_DIMS, {}
        else:
            self.hop(phase).wait_recv()
            done = self.order[: phase + 1]
            dims = tuple(dim for dim in SLOT_DIMS if dim not in done)
            source, fixed = self.arrivals[phase], {dim: 0 for dim in done}
        if phase == 3:
            spot = (0,) * 4 + self.span
            self.out[self.span] = self.total[spot].astype(single) + source[self.span].astype(
                single
            )
            return
        ahead = self.order[phase + 1]
        self.add(fixed | {ahead: 1}, source, dims)
        self.hop(phase + 1).start()
        self.add(fixed | {ahead: 0}, source, dims)

    def finish(self):
        self.across().wait_send()
        for phase in range(4):
            self.hop(phase).wait_send()


SCATTER_SEMS = 5


def scatter_scratch(rows, width):
    return [
        pltpu.VMEM((2,) * free + (rows, width), bfloat) for free in (4, 3, 2, 1, 0)
    ]


def split_scatterings(far, near, scratch, out, shares, orders, send, recv, base):
    moving, first = [], 0
    for index, (count, order) in enumerate(zip(shares, orders)):
        slot = base + SCATTER_SEMS * index
        moving.append(
            Scattering(
                far, near, scratch[0], scratch[1:], out, order, first, count, send, recv, slot
            )
        )
        first += count
    return moving


def first_scatter_kernel(
    kv_far, kv_near, up_far, up_near, down_far, down_near, kv_out, up_out, down_out, *refs
):
    up_scratch, down_scratch, (kv_total, kv_arrival, send, recv) = refs[:5], refs[5:10], refs[10:]
    greet([partner(bit) for bit in (X, Z0, Z1, CORE, Y)])
    base = len(UP_SUM_PARTS) * SCATTER_SEMS
    moving = split_scatterings(
        up_far, up_near, up_scratch, up_out, REST_SHARES, UP_SUM_PARTS, send, recv, 0
    ) + split_scatterings(
        down_far, down_near, down_scratch, down_out, REST_SHARES, DOWN_SUM_PARTS, send, recv, base
    )
    base = len(moving) * SCATTER_SEMS
    local = kv_out.shape[0]
    count = local // len(KV_EVENTS)

    def kv_copy(source, place, slot, bit):
        return pltpu.make_async_remote_copy(
            src_ref=source,
            dst_ref=place,
            send_sem=send.at[base + slot],
            recv_sem=recv.at[base + slot],
            device_id=partner(bit),
            device_id_type=MESH,
        )

    nears, overs = [], []
    for index in range(len(KV_EVENTS)):
        rows = pl.ds(index * count, count)
        nears.append(
            kv_copy(kv_far.at[:, rows, :], kv_total.at[:, rows, :], 2 * index, CORE)
        )
        overs.append(
            kv_copy(kv_total.at[1, rows, :], kv_arrival.at[rows, :], 2 * index + 1, Y)
        )
    nears[0].start()
    for part in moving:
        part.across().start()
    for near in nears[1:]:
        near.start()

    def kv_add(index, side):
        rows = pl.ds(index * count, count)
        kv_total[side, rows, :] = (
            kv_total[side, rows, :].astype(single) + kv_near[side, rows, :].astype(single)
        ).astype(bfloat)

    for index, (part, phase) in enumerate(REST_SUM_EVENTS):
        for piece, event in enumerate(KV_SUM_EVENTS):
            if index == event:
                nears[piece].wait_recv()
                kv_add(piece, 1)
                overs[piece].start()
                kv_add(piece, 0)
        moving[part].advance(phase)
    for index, over in enumerate(overs):
        over.wait_recv()
        rows = pl.ds(index * count, count)
        kv_out[rows, :] = (
            kv_total[0, rows, :].astype(single) + kv_arrival[rows, :].astype(single)
        ).astype(bfloat)
    for part in moving:
        part.finish()
    for copy in nears + overs:
        copy.wait_send()


KV_SUM_EVENTS = (2, 9, 13, 17)


def first_scatter(kv_far, kv_near, up_far, up_near, down_far, down_near):
    rows, width = up_far.shape[1:]
    local, wide = kv_far.shape[1:]
    cube = (2, 2, 2, 2, rows, width)
    mine = jax.ShapeDtypeStruct((rows, width), single)
    sems = (len(UP_SUM_PARTS) + len(DOWN_SUM_PARTS)) * SCATTER_SEMS + 2 * len(KV_SUM_EVENTS)
    return pl.pallas_call(
        first_scatter_kernel,
        out_shape=(jax.ShapeDtypeStruct((local, wide), bfloat), mine, mine),
        in_specs=[IN_HBM, IN_VMEM] * 3,
        out_specs=(IN_VMEM,) * 3,
        scratch_shapes=scatter_scratch(rows, width)
        + scatter_scratch(rows, width)
        + [pltpu.VMEM((2, local, wide), bfloat), pltpu.VMEM((local, wide), bfloat)]
        + [pltpu.SemaphoreType.DMA((sems,))] * 2,
        compiler_params=pltpu.CompilerParams(
            collective_id=3, has_side_effects=True, vmem_limit_bytes=VMEM_LIMIT
        ),
        cost_estimate=cost(0, 128 * rows * width),
        name="first_scatter",
    )(
        kv_far,
        kv_near,
        up_far.reshape(cube),
        up_near.reshape(cube),
        down_far.reshape(cube),
        down_near.reshape(cube),
    )


def last_scatter_kernel(
    note_ref,
    ada_ref,
    far_ref,
    near_ref,
    out_ref,
    mod_ref,
    bias_ref,
    silu_ref,
    *refs,
):
    scratch, refs = refs[:5], refs[5:]
    inbox, parts, returns, note_send, note_recv, back_send, back_recv, send, recv = refs
    bucket, seq = lax.axis_index("bucket"), lax.axis_index("seq")
    me = bucket * PLANES + seq
    count = BLOCKS * PLANES
    barrier = pltpu.get_barrier_semaphore()

    @pl.loop(1, count)
    def _(distance):
        pl.semaphore_signal(barrier, inc=1, device_id=peer_at(distance), device_id_type=MESH)

    pl.semaphore_wait(barrier, count - 1)

    def note(distance):
        peer = peer_at(distance)
        return pltpu.make_async_remote_copy(
            src_ref=note_ref.at[peer[0] * PLANES + peer[1]],
            dst_ref=inbox.at[me],
            send_sem=note_send.at[distance],
            recv_sem=note_recv.at[distance],
            device_id=peer,
            device_id_type=MESH,
        )

    def answer(distance):
        peer = peer_at(distance)
        return pltpu.make_async_remote_copy(
            src_ref=parts.at[peer[0]],
            dst_ref=returns.at[me],
            send_sem=back_send.at[distance],
            recv_sem=back_recv.at[distance],
            device_id=peer,
            device_id_type=MESH,
        )

    moving = split_scatterings(
        far_ref, near_ref, scratch, out_ref, PAIR_SHARES, PAIR_SUM_PARTS, send, recv, 0
    )
    for part in moving:
        part.across().start()

    @pl.loop(1, count)
    def _(distance):
        note(distance).start()

    inbox[me] = note_ref[me]
    for part, phase in PAIR_SUM_EVENTS[:SUM_NOTE_EVENT]:
        moving[part].advance(phase)

    @pl.loop(1, count)
    def _(distance):
        note(distance).wait_recv()

    rows, cols = ada_ref.shape
    spot = bias_ref.shape[1]
    sums = [sum(inbox[PLANES * g + s] for s in range(PLANES)) for g in range(BLOCKS)]
    bias_ref[...] = sum(sums)[:, :spot]
    mods = jnp.concatenate(sums)[:, spot : spot + cols]
    mod_ref[...] = mods
    silu = lax.dot_general(
        mods,
        ada_ref[...].astype(single),
        (((1,), (1,)), ((), ())),
        preferred_element_type=single,
        precision=HIGHEST,
    )
    for group in range(BLOCKS):
        parts[group, :, :rows] = silu[group : group + 1, :]
        parts[group, :, rows:] = jnp.zeros((1, parts.shape[2] - rows), single)
    returns[me] = parts[bucket]

    @pl.loop(1, count)
    def _(distance):
        answer(distance).start()

    for part, phase in PAIR_SUM_EVENTS[SUM_NOTE_EVENT:]:
        moving[part].advance(phase)

    @pl.loop(1, count)
    def _(distance):
        answer(distance).wait_recv()

    for group in range(BLOCKS):
        silu_ref[group] = sum(returns[PLANES * group + s] for s in range(PLANES))
    for part in moving:
        part.finish()

    @pl.loop(1, count)
    def _(distance):
        note(distance).wait_send()
        answer(distance).wait_send()


SUM_NOTE_EVENT = 9


def last_scatter(notes, ada_low, far, near, spot):
    rows, width = far.shape[1:]
    cube = (2, 2, 2, 2, rows, width)
    count = BLOCKS * PLANES
    cols = ada_low.shape[1]
    return pl.pallas_call(
        last_scatter_kernel,
        out_shape=(
            jax.ShapeDtypeStruct((rows, width), single),
            jax.ShapeDtypeStruct((BLOCKS, cols), single),
            jax.ShapeDtypeStruct((1, spot), single),
            jax.ShapeDtypeStruct((BLOCKS, 1, 2 * LANES), single),
        ),
        in_specs=[IN_VMEM, IN_VMEM, IN_HBM, IN_VMEM],
        out_specs=(IN_VMEM,) * 4,
        scratch_shapes=scatter_scratch(rows, width)
        + [
            pltpu.VMEM(notes.shape, single),
            pltpu.VMEM((BLOCKS, 1, 2 * LANES), single),
            pltpu.VMEM((count, 1, 2 * LANES), single),
        ]
        + [pltpu.SemaphoreType.DMA((count,))] * 4
        + [pltpu.SemaphoreType.DMA((len(PAIR_SUM_PARTS) * SCATTER_SEMS,))] * 2,
        compiler_params=pltpu.CompilerParams(
            collective_id=4, has_side_effects=True, vmem_limit_bytes=VMEM_LIMIT
        ),
        cost_estimate=cost(0, 64 * rows * width),
        name="last_scatter",
    )(notes, ada_low, far.reshape(cube), near.reshape(cube))


def whole(shape):
    return pl.BlockSpec(shape, lambda *_: (0,) * len(shape))


def qkv_kernel(cols, x_ref, shift_ref, scale_ref, bias_ref, w_ref, a_ref, q_ref, kv_ref, acc):
    step = pl.program_id(0)
    width = x_ref.shape[1]

    @pl.when(step == 0)
    def _():
        values = x_ref[...].astype(single)
        a_ref[...] = modulate(values, shift_ref[...], scale_ref[...]).astype(bfloat)

    wide = -(-cols // LANES) * LANES
    part = dot_nn(a_ref[...], w_ref[0, :, :wide])[:, :cols]
    for index in range(PLANES):

        @pl.when(step == index)
        def _():
            acc[:, index * cols : (index + 1) * cols] = part

    @pl.when(step == PLANES - 1)
    def _():
        q_ref[...] = (acc[:, :width] + bias_ref[:, :width]).astype(bfloat)
        kv_ref[...] = (acc[:, width:] + bias_ref[:, width:]).astype(bfloat)


def project_qkv(tokens, shift_row, scale_row, bias_row, weight):
    rows, width = tokens.shape
    cols = 3 * width // PLANES
    return pl.pallas_call(
        functools.partial(qkv_kernel, cols),
        grid=(PLANES,),
        out_shape=(
            jax.ShapeDtypeStruct((rows, width), bfloat),
            jax.ShapeDtypeStruct((rows, width), bfloat),
            jax.ShapeDtypeStruct((rows, 2 * width), bfloat),
        ),
        in_specs=[
            whole((rows, width)),
            whole((1, width)),
            whole((1, width)),
            whole((1, 3 * width)),
            pl.BlockSpec((1,) + weight.shape[1:], lambda s: (s, 0, 0)),
        ],
        out_specs=(whole((rows, width)), whole((rows, width)), whole((rows, 2 * width))),
        scratch_shapes=[pltpu.VMEM((rows, 3 * width), single)],
        compiler_params=params("arbitrary"),
        cost_estimate=cost(6 * rows * width * width, 8 * width * width),
        name="project_qkv",
    )(tokens, shift_row, scale_row, bias_row, weight)


def image_of(len_ref, position):
    start, length, end = jnp.int32(0), jnp.int32(0), jnp.int32(0)
    for index in range(len_ref.shape[1]):
        here = len_ref[0, index]
        inside = jnp.logical_and(position >= end, position < end + here)
        start = jnp.where(inside, end, start)
        length = jnp.where(inside, here, length)
        end = end + here
    return start, length


def head_windows(heads, size):
    for head in range(heads):
        low, high = head * size, (head + 1) * size
        yield head, low // LANES * LANES, -(-high // LANES) * LANES, low, high


def head_mask(low, high, left, right):
    lane = lax.broadcasted_iota(jnp.int32, (1, high - low), 1) + low
    return jnp.logical_and(lane >= left, lane < right)


LONG, SHORT = 1024, 256


def attend_kernel(heads, len_ref, q_ref, hm_ref, kv, ob_ref, log_ref, out):
    rows, width = q_ref.shape
    size = width // heads
    my_seq = lax.axis_index("seq")
    factor = size ** (-0.5) * LOG2E

    def run(tile_start, start, span):
        tile = pl.ds(tile_start, TILE)
        keys = pl.ds(start, span)
        logs = jnp.zeros((TILE, LANES), single)
        lane = lax.broadcasted_iota(jnp.int32, (TILE, LANES), 1)
        for head, low, high, left, right in head_windows(heads, size):
            mask = head_mask(low, high, left, right)
            query = q_ref[tile, low:high] * mask.astype(single).astype(bfloat)
            scores = dot_nt(query, kv[keys, low:high])
            top = jnp.max(scores, axis=-1, keepdims=True)
            expo = jnp.exp2((scores - top) * factor)
            total = jnp.sum(expo, axis=-1, keepdims=True)
            part = dot_nn(expo.astype(bfloat), kv[keys, width + low : width + high]) / total
            out[tile, low:high] = jnp.where(mask, part, out[tile, low:high])
            logs = jnp.where(lane == head, top * factor + jnp.log2(total), logs)
        log_ref[:, tile] = logs.T[:heads, :]

    @pl.loop(0, rows // TILE)
    def _(index):
        tile_start = pl.multiple_of(index * TILE, TILE)
        start, length = image_of(len_ref, my_seq * rows + tile_start)
        start = pl.multiple_of(start, SHORT)

        @pl.when(length > SHORT)
        def _():
            run(tile_start, start, LONG)

        @pl.when(length <= SHORT)
        def _():
            run(tile_start, start, SHORT)

    ob_ref[...] = (out[...] * hm_ref[...]).astype(bfloat)


def attend(lengths, query, kv, head_row, heads):
    rows, width = query.shape
    group = kv.shape[0]
    return pl.pallas_call(
        functools.partial(attend_kernel, heads),
        out_shape=(
            jax.ShapeDtypeStruct((rows, width), bfloat),
            jax.ShapeDtypeStruct((heads, rows), single),
        ),
        in_specs=[pl.BlockSpec(memory_space=pltpu.SMEM)]
        + [IN_VMEM] * 3,
        out_specs=(IN_VMEM,) * 2,
        scratch_shapes=[pltpu.VMEM((rows, width), single)],
        compiler_params=params(),
        cost_estimate=cost(16 * rows * LONG * width, 10 * group * width, heads * rows * LONG),
        name="attend",
    )(lengths, query, head_row, kv)


def out_kernel(
    ob_ref, w_ref, bias_ref, x_ref, gate_ref, shift_ref, scale_ref, r_ref, mid_ref, a_ref
):
    step = pl.program_id(0)
    width = x_ref.shape[1]
    steps = pl.num_programs(0)
    cols = width // 4
    part = dot_nn(ob_ref[...], w_ref[0])[:, -cols:]
    for index in range(4):

        @pl.when(step == index)
        def _():
            r_ref[:, index * cols : (index + 1) * cols] = part

    @pl.when(step == steps - 1)
    def _():
        result = r_ref[...] + bias_ref[...]
        r_ref[...] = result
        middle = x_ref[...].astype(single) + gate_ref[...] * result
        mid_ref[...] = middle
        a_ref[...] = modulate(middle, shift_ref[...], scale_ref[...]).astype(bfloat)


def project_out(branch, weight, bias_row, tokens, gate_row, shift_row, scale_row):
    rows, width = tokens.shape
    planes = weight.shape[0]
    row = whole((1, width))
    return pl.pallas_call(
        out_kernel,
        grid=(planes,),
        out_shape=(
            jax.ShapeDtypeStruct((rows, width), single),
            jax.ShapeDtypeStruct((rows, width), single),
            jax.ShapeDtypeStruct((rows, width), bfloat),
        ),
        in_specs=[
            whole((rows, width)),
            pl.BlockSpec((1, width, 3 * LANES), lambda s: (s, 0, 2)),
            row,
            whole((rows, width)),
            row,
            row,
            row,
        ],
        out_specs=(whole((rows, width)),) * 3,
        compiler_params=params("arbitrary"),
        cost_estimate=cost(2 * rows * width * width, 2 * width * width + 12 * rows * width),
        name="project_out",
    )(branch, weight, bias_row, tokens, gate_row, shift_row, scale_row)


def out_copies(source, layout, plane, buffer, seq_bits, far_ref, near_ref, sem):
    my_bucket, my_seq = place_in_kernel()
    rows = far_ref.shape[1]
    copies = []
    for index in range(BLOCKS):
        if layout == "rows":
            bits, part = index % PLANES, index // PLANES
            seq = my_seq ^ bits
            bucket = plane * (BLOCKS // PLANES) + part
            start = pl.multiple_of((part * PLANES + seq) * rows, 16)
            side = bits % 2
        else:
            bits, bucket, start, side = seq_bits, index, index * rows, seq_bits_side(seq_bits)
        target = far_ref if side else near_ref
        slot = slot_of(bucket ^ my_bucket, bits if layout == "rows" else seq_bits[0])
        copies.append(
            pltpu.make_async_copy(
                source.at[buffer, pl.ds(start, rows), :], target.at[slot], sem.at[buffer, index]
            )
        )
    return copies


def seq_bits_side(seq_bits):
    return seq_bits[1]


def ffn_kernel(a_ref, df_ref, cm_ref, b_ref, up_ref, down_ref, *refs):
    f_ref, da_ref, up_far, up_near, down_far, down_near, db_ref = refs[:7]
    up, down, up_grad, down_grad, up_sem, down_sem, up_out, down_out = refs[7:]
    width = a_ref.shape[1]
    my_seq = place_in_kernel()[1]

    def loads(bits):
        plane = my_seq ^ bits
        rows = pl.ds(pl.multiple_of(plane * width, LANES), width)
        return (
            pltpu.make_async_copy(up_ref.at[plane], up.at[plane], up_sem.at[bits]),
            pltpu.make_async_copy(down_ref.at[rows, :], down.at[rows, :], down_sem.at[bits]),
        )

    for bits in (1, 3, 0, 2):
        for copy in loads(bits):
            copy.start()
    f_ref[...] = jnp.zeros_like(f_ref)
    da_ref[...] = jnp.zeros_like(da_ref)

    def one(plane, low, high, buffer):
        first, grad = a_ref[...], df_ref[...]
        hidden_rows = pl.ds(pl.multiple_of(plane * width + low, LANES), high - low)
        keep = cm_ref[plane, :, low:high]
        pre = dot_nn(first, up[plane, :, low:high]) + b_ref[plane, :, low:high]
        root = math.sqrt(2.0 / math.pi)
        square = pre * pre
        bend = jnp.tanh(root * pre * (1.0 + 0.044715 * square))
        half = 0.5 * (1.0 + bend)
        hidden = (pre * half * keep).astype(bfloat)
        slope = half + 0.5 * pre * (1.0 - bend * bend) * (root * (1.0 + 0.134145 * square))
        back = (dot_nt(grad, down[hidden_rows, :]) * keep * slope).astype(bfloat)
        f_ref[...] += dot_nn(hidden, down[hidden_rows, :])
        da_ref[...] += dot_nt(back, up[plane, :, low:high])
        up_grad[buffer, :, low:high] = dot_tn(first, back).astype(bfloat)
        down_grad[buffer, low:high, :] = dot_tn(hidden, grad).astype(bfloat)
        db_ref[plane, :, low:high] = jnp.sum(back.astype(single), axis=0, keepdims=True)

    cut = -(-width // 2 // LANES) * LANES

    def sends(plane, buffer, side_bits, far_side):
        return out_copies(
            up_grad, "planes", plane, buffer, (side_bits, far_side), up_far, up_near, up_out
        ) + out_copies(
            down_grad, "rows", plane, buffer, None, down_far, down_near, down_out
        )

    for far_side in (1, 0):

        @pl.loop(0, 2)
        def _(above):
            bits = above * 2 + far_side
            plane = my_seq ^ bits
            if not far_side:
                for copy in sends(plane, above, bits, far_side):
                    copy.wait()
            for copy in loads(bits):
                copy.wait()
            one(plane, 0, cut, above)
            one(plane, cut, width, above)
            for copy in sends(plane, above, bits, far_side):
                copy.start()

    for above in range(2):
        for copy in sends(my_seq ^ (above * 2), above, above * 2, 0):
            copy.wait()


def feed_forward(first, grad, chan_row, bias_row, up_weight, down_weight):
    rows, width = first.shape
    hidden = chan_row.shape[1]
    blocks = jax.ShapeDtypeStruct((BLOCKS * PLANES // 2, width // BLOCKS, width), bfloat)
    result = pl.pallas_call(
        ffn_kernel,
        out_shape=(
            jax.ShapeDtypeStruct((rows, width), single),
            jax.ShapeDtypeStruct((rows, width), single),
            blocks,
            blocks,
            blocks,
            blocks,
            jax.ShapeDtypeStruct((PLANES, 1, width), single),
        ),
        in_specs=[IN_VMEM] * 4 + [IN_HBM] * 2,
        out_specs=(IN_VMEM, IN_VMEM) + (IN_HBM,) * 4 + (IN_VMEM,),
        scratch_shapes=[
            pltpu.VMEM((PLANES, width, width), bfloat),
            pltpu.VMEM((hidden, width), bfloat),
            pltpu.VMEM((2, width, width), bfloat),
            pltpu.VMEM((2, width, width), bfloat),
            pltpu.SemaphoreType.DMA((PLANES,)),
            pltpu.SemaphoreType.DMA((PLANES,)),
            pltpu.SemaphoreType.DMA((2, BLOCKS)),
            pltpu.SemaphoreType.DMA((2, BLOCKS)),
        ],
        compiler_params=params(),
        cost_estimate=cost(12 * rows * width * hidden, 8 * width * hidden, rows * hidden),
        name="feed_forward",
    )(
        first,
        grad,
        chan_row.reshape(PLANES, 1, width),
        bias_row.reshape(PLANES, 1, width),
        up_weight,
        down_weight,
    )
    return result


def back_out_kernel(heads, dr_ref, w_ref, hm_ref, ob_ref, do_ref, delta_ref, acc):
    step = pl.program_id(0)
    part = dot_nt(dr_ref[0], w_ref[0])

    @pl.when(step == 0)
    def _():
        acc[...] = part

    @pl.when(step > 0)
    def _():
        acc[...] += part

    @pl.when(step == pl.num_programs(0) - 1)
    def _():
        width = acc.shape[1]
        size = width // heads
        grad = (acc[...] * hm_ref[...]).astype(bfloat)
        do_ref[...] = grad
        terms = grad.astype(single) * ob_ref[...].astype(single)
        head = lax.broadcasted_iota(jnp.int32, (heads, width), 0)
        lane = lax.broadcasted_iota(jnp.int32, (heads, width), 1)
        chosen = jnp.logical_and(lane >= head * size, lane < (head + 1) * size)
        delta_ref[...] = lax.dot_general(
            chosen.astype(single),
            terms,
            (((1,), (1,)), ((), ())),
            preferred_element_type=single,
            precision=HIGHEST,
        )


def back_out(dr_planes, weight, head_row, branch, heads):
    rows, width = branch.shape
    planes = weight.shape[0]
    return pl.pallas_call(
        functools.partial(back_out_kernel, heads),
        grid=(planes,),
        out_shape=(
            jax.ShapeDtypeStruct((rows, width), bfloat),
            jax.ShapeDtypeStruct((heads, rows), single),
        ),
        in_specs=[
            pl.BlockSpec((1, rows, 3 * LANES), lambda s: (s, 0, 0)),
            pl.BlockSpec((1, width, 3 * LANES), lambda s: (s, 0, 2)),
            whole((1, width)),
            whole((rows, width)),
        ],
        out_specs=(whole((rows, width)), whole((heads, rows))),
        scratch_shapes=[pltpu.VMEM((rows, width), single)],
        compiler_params=params("arbitrary"),
        cost_estimate=cost(2 * rows * width * width, 2 * width * width),
        name="back_out",
    )(dr_planes, weight, head_row, branch)


def attend_back_kernel(
    heads, len_ref, q_ref, do_ref, log_ref, delta_ref, kv, dq_ref, far_ref, near_ref, dq, dk, dv
):
    rows, width = q_ref.shape
    size = width // heads
    my_seq = lax.axis_index("seq")
    scale = size ** (-0.5)
    factor = scale * LOG2E
    dk[...] = jnp.zeros_like(dk)
    dv[...] = jnp.zeros_like(dv)

    def run(tile_start, start, span):
        tile = pl.ds(tile_start, TILE)
        keys = pl.ds(start, span)
        for head, low, high, left, right in head_windows(heads, size):
            mask = head_mask(low, high, left, right)
            chosen = mask.astype(single).astype(bfloat)
            query = q_ref[tile, low:high] * chosen
            grad = do_ref[tile, low:high] * chosen
            key = kv[keys, low:high]
            probs = jnp.exp2(dot_nt(key, query) * factor - log_ref[head : head + 1, tile])
            slope = dot_nt(kv[keys, width + low : width + high], grad)
            score_grad = (probs * (slope - delta_ref[head : head + 1, tile])).astype(bfloat)
            dv[keys, low:high] += dot_nn(probs.astype(bfloat), grad)
            dk[keys, low:high] += dot_nn(score_grad, query)
            part = dot_tn(score_grad, key)
            dq[tile, low:high] = jnp.where(mask, part, dq[tile, low:high])

    @pl.loop(0, rows // TILE)
    def _(index):
        tile_start = pl.multiple_of(index * TILE, TILE)
        start, length = image_of(len_ref, my_seq * rows + tile_start)
        start = pl.multiple_of(start, SHORT)

        @pl.when(length > SHORT)
        def _():
            run(tile_start, start, LONG)

        @pl.when(length <= SHORT)
        def _():
            run(tile_start, start, SHORT)

    dq_ref[...] = (dq[...] * scale).astype(bfloat)
    base = place_in_kernel()[1]
    for bits in range(PLANES):
        place = pl.ds(pl.multiple_of((base ^ bits) * rows, rows), rows)
        target = far_ref if bits % 2 else near_ref
        target[bits // 2, :, :width] = (dk[place, :] * scale).astype(bfloat)
        target[bits // 2, :, width:] = dv[place, :].astype(bfloat)


def attend_back(lengths, query, grad, logs, delta, kv, heads):
    rows, width = query.shape
    group = kv.shape[0]
    return pl.pallas_call(
        functools.partial(attend_back_kernel, heads),
        out_shape=(
            jax.ShapeDtypeStruct((rows, width), bfloat),
            jax.ShapeDtypeStruct((2, rows, 2 * width), bfloat),
            jax.ShapeDtypeStruct((2, rows, 2 * width), bfloat),
        ),
        in_specs=[pl.BlockSpec(memory_space=pltpu.SMEM)]
        + [IN_VMEM] * 5,
        out_specs=(IN_VMEM,) * 3,
        scratch_shapes=[
            pltpu.VMEM((rows, width), single),
            pltpu.VMEM((group, width), single),
            pltpu.VMEM((group, width), single),
        ],
        compiler_params=params(),
        cost_estimate=cost(40 * rows * LONG * width, 20 * group * width, heads * rows * LONG),
        name="attend_back",
    )(lengths, query, grad, logs, delta, kv)


def back_qkv_kernel(
    a_ref, ob_ref, dy_ref, dr_ref, w_ref, da_ref, far_ref, near_ref, stage, sem
):
    my_seq = place_in_kernel()[1]
    wide = dy_ref.shape[2]
    below = wide - LANES
    da_ref[...] = jnp.zeros_like(da_ref)

    def sends(plane, buffer, bits, far_side):
        return out_copies(
            stage, "planes", plane, buffer, (bits, far_side), far_ref, near_ref, sem
        )

    for far_side in (1, 0):

        @pl.loop(0, 2)
        def _(above):
            bits = above * 2 + far_side
            plane = my_seq ^ bits
            if not far_side:
                for copy in sends(plane, above, bits, far_side):
                    copy.wait()
            da_ref[...] += dot_nt(dy_ref[plane], w_ref[plane, :, :wide])
            first = dot_tn(a_ref[...], dy_ref[plane])
            second = dot_tn(ob_ref[...], dr_ref[plane])
            stage[above, :, :below] = first[:, :below].astype(bfloat)
            stage[above, :, below:wide] = (first[:, below:] + second[:, :LANES]).astype(bfloat)
            stage[above, :, wide:] = second[:, LANES:].astype(bfloat)
            for copy in sends(plane, above, bits, far_side):
                copy.start()

    for above in range(2):
        for copy in sends(my_seq ^ (above * 2), above, above * 2, 0):
            copy.wait()


def back_qkv(first_in, branch, dy_planes, dr_planes, weight):
    rows, width = first_in.shape
    blocks = jax.ShapeDtypeStruct((BLOCKS * PLANES // 2, width // BLOCKS, width), bfloat)
    return pl.pallas_call(
        back_qkv_kernel,
        out_shape=(jax.ShapeDtypeStruct((rows, width), single), blocks, blocks),
        in_specs=[IN_VMEM] * 5,
        out_specs=(IN_VMEM, IN_HBM, IN_HBM),
        scratch_shapes=[
            pltpu.VMEM((2, width, width), bfloat),
            pltpu.SemaphoreType.DMA((2, BLOCKS)),
        ],
        compiler_params=params(),
        cost_estimate=cost(14 * rows * width * width, 4 * weight.size),
        name="back_qkv",
    )(first_in, branch, dy_planes, dr_planes, weight)


def on_device(
    tokens,
    condition,
    cotangent,
    lengths,
    bucket_ids,
    keep_flags,
    head_table,
    chan_table,
    ada_master,
    ada_first,
    ada_second,
    ada_average,
    qkv_master,
    qkv_first,
    qkv_second,
    qkv_average,
    out_master,
    out_first,
    out_second,
    out_average,
    up_master,
    up_first,
    up_second,
    up_average,
    down_master,
    down_first,
    down_second,
    down_average,
    bias_master,
    bias_first,
    bias_second,
    bias_average,
):
    local_rows, width = tokens.shape
    heads = head_table.shape[1]
    head_size = width // heads
    hidden_width = chan_table.shape[1]
    hidden_ratio = hidden_width // width
    table_cols = 10 + hidden_ratio
    my_bucket, my_seq = lax.axis_index("bucket"), lax.axis_index("seq")
    buckets, seqs = lax.axis_size("bucket"), lax.axis_size("seq")
    group_rows = local_rows * seqs
    block_rows = qkv_master.shape[0]
    pair_block = jnp.concatenate([qkv_master, out_master], axis=1).astype(bfloat)
    down_block = lax.all_to_all(
        down_master.astype(bfloat), "seq", split_axis=0, concat_axis=1, tiled=True
    )
    up_block = up_master.astype(bfloat)
    ada_low = ada_master.astype(bfloat)
    if cube_path():
        count = bias_master.shape[0]
        spots = (LANES * 2, LANES * 4)
        slices = jnp.pad(condition.reshape(buckets, block_rows), ((0, 0), (0, spots[0] - block_rows)))
        told = jnp.broadcast_to(
            jnp.pad(bias_master, (0, spots[1] - count)), (buckets * seqs, spots[1])
        )
        notes = jnp.concatenate([jnp.repeat(slices, seqs, axis=0), told], axis=1)[:, None, :]
        pair_weight, inbox, silu_rows, mod_row = first_gather(notes, ada_low, pair_block)
        bias_low = inbox[:, 0, spots[0] : spots[0] + count].astype(bfloat).reshape(-1)
    else:
        pair_weight = gather_all(pair_block, "planes")
        bias_low = lax.all_gather(
            bias_master.astype(bfloat), ("bucket", "seq"), axis=0, tiled=True
        )
        silu_low = jax.nn.silu(condition).astype(bfloat)
        silu_all = lax.all_gather(silu_low, "bucket", axis=0, tiled=True)
        silu_rows = lax.dynamic_slice_in_dim(silu_all, my_bucket * block_rows, block_rows, 1)
        mod_part = lax.psum_scatter(
            dot_nn(silu_rows, ada_low), "bucket", scatter_dimension=0, tiled=True
        )
        mod_row = lax.all_gather(mod_part, "seq", axis=1, tiled=True)

    bias_table = bias_low.astype(single).reshape(width, table_cols).T
    modulation = mod_row.reshape(6, 1, width) + bias_table[:6, None, :]
    shift_one, scale_one, gate_one, shift_two, scale_two, gate_two = modulation
    value_bias = bias_table[7:8]
    qkv_bias = jnp.concatenate([bias_table[6:7], jnp.zeros_like(value_bias), value_bias], axis=1)
    out_bias = bias_table[8:9]
    up_bias = bias_table[9 : table_cols - 1].T.reshape(1, hidden_width)
    down_bias = bias_table[table_cols - 1 :]
    selector = (
        jnp.arange(head_table.shape[0], dtype=jnp.int32)[:, None] == bucket_ids[None, :]
    ).astype(single)
    head_row = jnp.repeat(jnp.sum(selector * head_table.astype(single), axis=0), head_size)[None]
    chan_row = jnp.sum(selector * chan_table.astype(single), axis=0)[None]
    keep_float = keep_flags.astype(single)[:, None]
    upstream = cotangent.astype(single)
    mlp_grad = (gate_two * keep_float * upstream).astype(bfloat)

    first_in, query, key_value = project_qkv(tokens, shift_one, scale_one, qkv_bias, pair_weight)
    if cube_path():
        up_weight, down_weight, near = second_gather(up_block, down_block, key_value)
    else:
        up_weight = gather_all(up_block, "planes")
        down_weight = gather_all(down_block, "rows")
        near = lax.all_gather(key_value, "seq", axis=0, tiled=True)
    branch_in, logs = attend(lengths, query, near, head_row, heads)
    attn_out, middle, second_in = project_out(
        branch_in, pair_weight, out_bias, tokens, gate_one, shift_two, scale_two
    )
    mlp_sum, second_grad, up_far, up_near, down_far, down_near, up_bias_grad = feed_forward(
        second_in, mlp_grad, chan_row, up_bias, up_weight, down_weight
    )
    mlp_out = mlp_sum + down_bias
    output = (middle + gate_two * keep_float * mlp_out).astype(bfloat)
    gate_two_grad = jnp.sum(keep_float * upstream * mlp_out, axis=0)
    down_bias_grad = jnp.sum(mlp_grad, axis=0, dtype=single)
    _, norm_two_back = jax.vjp(modulate, middle, shift_two[0], scale_two[0])
    middle_norm_grad, shift_two_grad, scale_two_grad = norm_two_back(second_grad)
    middle_grad = upstream + middle_norm_grad
    branch_grad = (gate_one * middle_grad).astype(bfloat)
    gate_one_grad = jnp.sum(middle_grad * attn_out, axis=0)
    out_bias_grad = jnp.sum(branch_grad, axis=0, dtype=single)
    out_cols = width // seqs
    dr_planes = jnp.pad(
        branch_grad.reshape(local_rows, seqs, out_cols).transpose(1, 0, 2),
        ((0, 0), (0, 0), (3 * LANES - out_cols, 0)),
    )
    attended_grad, delta = back_out(dr_planes, pair_weight, head_row, branch_in, heads)
    query_grad, kv_far, kv_near = attend_back(
        lengths, query, attended_grad, logs, delta, near, heads
    )
    if cube_path():
        kv_grad, up_new_grad, down_new_grad = first_scatter(
            kv_far, kv_near, up_far, up_near, down_far, down_near
        )
    else:
        terms = jnp.stack([kv_near[0], kv_far[0], kv_near[1], kv_far[1]])
        kv_grad = lax.psum_scatter(terms, "seq", scatter_dimension=0)
        up_new_grad = natural_sum(up_far, up_near, "planes")
        down_new_grad = natural_sum(down_far, down_near, "rows")
    projected_grad = jnp.concatenate([query_grad, kv_grad], axis=1)
    qkv_cols = 3 * width // seqs
    dy_planes = jnp.pad(
        projected_grad.reshape(local_rows, seqs, qkv_cols).transpose(1, 0, 2),
        ((0, 0), (0, 0), (0, -qkv_cols % LANES)),
    )
    first_grad, pair_far, pair_near = back_qkv(
        first_in, branch_in, dy_planes, dr_planes, pair_weight
    )
    query_bias_grad = jnp.sum(projected_grad[:, :width], axis=0, dtype=single)
    value_bias_grad = jnp.sum(projected_grad[:, 2 * width :], axis=0, dtype=single)
    inputs_float = tokens.astype(single)
    _, norm_one_back = jax.vjp(modulate, inputs_float, shift_one[0], scale_one[0])
    input_norm_grad, shift_one_grad, scale_one_grad = norm_one_back(first_grad)
    token_grad = middle_grad + input_norm_grad
    mod_grads = jnp.stack(
        [
            shift_one_grad,
            scale_one_grad,
            gate_one_grad,
            shift_two_grad,
            scale_two_grad,
            gate_two_grad,
        ]
    )
    bias_grad = jnp.concatenate(
        [
            mod_grads.T,
            query_bias_grad[:, None],
            value_bias_grad[:, None],
            out_bias_grad[:, None],
            up_bias_grad.reshape(width, hidden_ratio),
            down_bias_grad[:, None],
        ],
        axis=1,
    ).reshape(width * table_cols)
    mod_parts = mod_grads.reshape(seqs, 6 * width // seqs)
    if cube_path():
        count = bias_master.shape[0]
        spot = -(-count // LANES) * LANES
        notes = jnp.concatenate(
            [
                bias_grad.reshape(buckets * seqs, count),
                jnp.zeros((buckets * seqs, spot - count), single),
                jnp.tile(mod_parts, (buckets, 1)),
            ],
            axis=1,
        )
        notes = jnp.pad(notes, ((0, 0), (0, -notes.shape[1] % LANES)))[:, None, :]
        pair_new_grad, mod_all, bias_sum, silu_sum = last_scatter(
            notes, ada_low, pair_far, pair_near, spot
        )
        bias_new_grad = bias_sum[0, :count]
        silu_grad = silu_sum[:, 0, :block_rows].reshape(1, width)
    else:
        pair_new_grad = natural_sum(pair_far, pair_near, "planes")
        mod_mine = lax.psum_scatter(mod_parts, "seq", scatter_dimension=0, tiled=True)
        mod_all = lax.all_gather(mod_mine, "bucket", axis=0, tiled=True)
        silu_part = lax.dot_general(
            mod_all,
            ada_low.astype(single),
            (((1,), (1,)), ((), ())),
            preferred_element_type=single,
            precision=HIGHEST,
        )
        silu_grad = lax.all_to_all(
            lax.psum(silu_part, "seq"), "bucket", split_axis=0, concat_axis=1, tiled=True
        )
        bias_new_grad = lax.psum_scatter(
            bias_grad, ("bucket", "seq"), scatter_dimension=0, tiled=True
        )
    ada_new_grad = lax.dot_general(
        silu_rows.astype(single),
        mod_all,
        (((0,), (0,)), ((), ())),
        preferred_element_type=single,
        precision=HIGHEST,
    )
    _, silu_back = jax.vjp(jax.nn.silu, condition)
    condition_grad = silu_back(silu_grad)[0]
    down_mine = lax.all_to_all(
        down_new_grad.astype(bfloat), "seq", split_axis=1, concat_axis=0, tiled=True
    ).astype(single)
    out_rate = (group_rows / (16.0 * width)) ** 0.5
    ada_new = adam_update(
        ada_master, ada_first, ada_second, ada_average, ada_new_grad, width ** (-0.5), MATRIX_DECAY
    )
    qkv_new = adam_update(
        qkv_master,
        qkv_first,
        qkv_second,
        qkv_average,
        pair_new_grad[:, :qkv_cols],
        width ** (-0.5),
        MATRIX_DECAY,
    )
    out_new = adam_update(
        out_master,
        out_first,
        out_second,
        out_average,
        pair_new_grad[:, qkv_cols:],
        out_rate,
        MATRIX_DECAY,
    )
    up_new = adam_update(
        up_master, up_first, up_second, up_average, up_new_grad, width ** (-0.5), MATRIX_DECAY
    )
    down_new = adam_update(
        down_master,
        down_first,
        down_second,
        down_average,
        down_mine,
        hidden_width ** (-0.5),
        MATRIX_DECAY,
    )
    bias_new = adam_update(
        bias_master, bias_first, bias_second, bias_average, bias_new_grad, 0.3, 0.0
    )
    return (
        output,
        token_grad,
        condition_grad,
        *ada_new,
        *qkv_new,
        *out_new,
        *up_new,
        *down_new,
        *bias_new,
    )


def solution(mesh):
    in_specs = (
        P(("bucket", "seq"), None),
        P("bucket", None),
        P(("bucket", "seq"), None),
        P("bucket", None),
        P("bucket"),
        P(("bucket", "seq")),
        P(),
        P(),
        P("bucket", "seq"),
        P("bucket", "seq"),
        P("bucket", "seq"),
        P("bucket", "seq"),
        P("bucket", "seq"),
        P("bucket", "seq"),
        P("bucket", "seq"),
        P("bucket", "seq"),
        P("bucket", "seq"),
        P("bucket", "seq"),
        P("bucket", "seq"),
        P("bucket", "seq"),
        P("bucket", "seq"),
        P("bucket", "seq"),
        P("bucket", "seq"),
        P("bucket", "seq"),
        P("bucket", "seq"),
        P("bucket", "seq"),
        P("bucket", "seq"),
        P("bucket", "seq"),
        P(("bucket", "seq")),
        P(("bucket", "seq")),
        P(("bucket", "seq")),
        P(("bucket", "seq")),
    )
    out_specs = (
        P(("bucket", "seq"), None),
        P(("bucket", "seq"), None),
        P("bucket", None),
        P("bucket", "seq"),
        P("bucket", "seq"),
        P("bucket", "seq"),
        P("bucket", "seq"),
        P("bucket", "seq"),
        P("bucket", "seq"),
        P("bucket", "seq"),
        P("bucket", "seq"),
        P("bucket", "seq"),
        P("bucket", "seq"),
        P("bucket", "seq"),
        P("bucket", "seq"),
        P("bucket", "seq"),
        P("bucket", "seq"),
        P("bucket", "seq"),
        P("bucket", "seq"),
        P("bucket", "seq"),
        P("bucket", "seq"),
        P("bucket", "seq"),
        P("bucket", "seq"),
        P(("bucket", "seq")),
        P(("bucket", "seq")),
        P(("bucket", "seq")),
        P(("bucket", "seq")),
    )
    return jax.shard_map(
        on_device, mesh=mesh, in_specs=in_specs, out_specs=out_specs, check_vma=False
    )
```

time: 3000 us -> 674 us (0.22)
  waiting for transfers between devices: 2220 us -> 0.01 us
  Pallas kernels: 0 us -> 551 us
  matrix products: 384 us -> 3.37 us
  blocking collectives: 117 us -> 0 us
  local copies, waits for them, and re-layouts: 135 us -> 51.5 us
  other arithmetic: 102 us -> 48.3 us
    reduce_scatter x6 -> x0, waiting for transfers between devices: 1550 us -> none  [the longest x1 512 us: on_device(): lax.psum_scatter(ada_grad, 'bucket', scatter_dimension=0, tiled=True)]
    all_gather x9 -> x0, waiting for transfers between devices: 572 us -> none  [the longest x1 154 us: on_device(): lax.all_gather(seq_whole[0], 'bucket', axis=0, tiled=True)]
    pallas_call x0 -> x11, Pallas kernels: none -> 551 us  [the longest x1 133 us: first_scatter(): pl.pallas_call(first_scatter_kernel, out_shape=(jax.ShapeDtypeStruct((loc...]
    dot_general x44 -> x1, matrix products: 384 us -> 3.37 us  [on_device(): lax.dot_general(silu_rows.astype(single), mod_all, (((0,), (0,)), ((), ()...]
    unnamed x25 -> x0, waiting for transfers between devices: 95.1 us -> none
    unnamed x4 -> x0, blocking collectives: 88.6 us -> none
    unnamed x188 -> x140, local copies, waits for them, and re-layouts: 53.2 us -> 15 us
    reduce_sum x7 -> x4, other arithmetic: 38.9 us -> 6.8 us  [the longest x1 5.16 us: on_device(): gate_two_grad = jnp.sum(keep_float * upstream * mlp_out, axis=0)]
  transfers between devices with their start and end apart: 20 -> 2, of which waited for: 17 -> 0; matrix products, arithmetic and copies ran while one was open for 10% -> 5% of each run, Pallas kernels for 0% -> 12%
where the time goes in v1:
time: 674 us; the launch traced here: 666 us
  Pallas kernels  551 us (82%)
  local copies, waits for them, and re-layouts  51.5 us (8%)
  other arithmetic  48.3 us (7%)
  starting transfers between devices  8.61 us (1%)
    pallas_call x1, Pallas kernels, first_scatter(): pl.pallas_call(first_scatter_kernel, out_shape=(jax.ShapeDtypeStruct((loc...  133 us
    pallas_call x1, Pallas kernels, second_gather(): pl.pallas_call(second_gather_kernel, out_shape=(blocks, blocks, jax.Shape...  129 us
    pallas_call x1, Pallas kernels, first_gather(): pl.pallas_call(first_gather_kernel, out_shape=(jax.ShapeDtypeStruct((2, 2...  67.4 us
    pallas_call x1, Pallas kernels, last_scatter(): pl.pallas_call(last_scatter_kernel, out_shape=(jax.ShapeDtypeStruct((rows...  62.8 us
    pallas_call x1, Pallas kernels, feed_forward(): pl.pallas_call(ffn_kernel, out_shape=(jax.ShapeDtypeStruct((rows, width),...  49.7 us
    pallas_call x1, Pallas kernels, attend_back(): pl.pallas_call(functools.partial(attend_back_kernel, heads), out_shape=(j...  33.1 us
    pallas_call x1, Pallas kernels, back_qkv(): pl.pallas_call(back_qkv_kernel, out_shape=(jax.ShapeDtypeStruct((rows, wi...  23.3 us
    pallas_call x1, Pallas kernels, attend(): pl.pallas_call(functools.partial(attend_kernel, heads), out_shape=(jax.Sh...  19.8 us
  transfers between devices with their start and end apart: 2, of which 0 were waited for; matrix products, arithmetic and copies ran while one was open for 5% of the time, Pallas kernels for 12%

profile of v1, /device:TPU:0, one launch (start us, length us, event | category | flops | bytes accessed | tf_op | source)
XLA Modules:
  0.0 665.6 jit_solution(8918449524613270940)
XLA Ops:
  3.1 4.2 all-to-all-start
  10.0 67.4 %first_gather.1 = (bf16[2,2,2,2,2,144,1152]{6,5,4,3,2,1,0:T(8,128)(2,1)}, f32[32,1,768]{2,1,0:T(1,128)}, bf16[8,144]{1,0:T(8,128)(2,1)}, f32[4,1,1728]{2,1,0:T(1,128)}) custom-call(f32[32,1,768]{2,1,0:T(1,128)} %broadcast_in_dim.57.note_ref, bf16[144,1728]{1,0:T(8,128)(2,1)} %convert_element_type.86.ada_ref, bf16[144,1152]{1,0:T(8,128)(2,1)} %pad_maximum_fusion.1.block_ref), custom_call_target="tpu_custom_call" | custom-call | bytes 10616832 | tf_op jit(solution)/shard_map/first_gather/pallas_call | solution.py:373
  84.8 13.6 %project_qkv.1 = (bf16[512,1152]{1,0:T(8,128)(2,1)}, bf16[512,1152]{1,0:T(8,128)(2,1)}, bf16[512,2304]{1,0:T(8,128)(2,1)}) custom-call(bf16[512,1152]{1,0:T(8,128)(2,1)} %x_ref.3, f32[1,1152]{1,0:T(1,128)} %get-tuple-element.185.shift_ref, f32[1,1152]{1,0:T(1,128)} %get-tuple-element.186.scale_ref, f32[1,3456]{1,0:T(1,128)} %fusion.20.bias_ref, ...), custom_call_target="tpu_custom_call" | custom-call | flops 4076863488 | bytes 10616832 | tf_op jit(solution)/shard_map/project_qkv/pallas_call | solution.py:872
  110.2 129.2 %second_gather.1 = (bf16[2,2,2,2,2,144,1152]{6,5,4,3,2,1,0:T(8,128)(2,1)}, bf16[2,2,2,2,2,144,1152]{6,5,4,3,2,1,0:T(8,128)(2,1)}, bf16[2,2,512,2304]{3,2,1,0:T(8,128)(2,1)}) custom-call(bf16[144,1152]{1,0:T(8,128)(2,1)} %convert_element_type.90.up_ref, bf16[144,1152]{1,0:T(8,128)(2,1)} %all_to_all.27.down_ref, bf16[512,2304]{1,0:T(8,128)(2,1)} %get-tuple-element.68.kv_ref), custom_call_target="tpu_custom_call" | custom-call | bytes 21233664 | tf_op jit(solution)/shard_map/second_gather/pallas_call | solution.py:459
  239.4 19.8 %attend.1 = (bf16[512,1152]{1,0:T(8,128)(2,1)}, f32[16,512]{1,0:T(8,128)}) custom-call(s32[1,8]{1,0:T(1,128)} %len_ref.3, bf16[512,1152]{1,0:T(8,128)(2,1)} %get-tuple-element.67.q_ref, f32[1,1152]{1,0:T(1,128)} %broadcast_in_dim_reshape.3.hm_ref, bf16[2048,2304]{1,0:T(8,128)(2,1)} %bitcast.54), custom_call_target="tpu_custom_call" | custom-call | flops 9663676416 | bytes 23592960 | tf_op jit(solution)/shard_map/attend/pallas_call | solution.py:963
  259.2 10.1 %project_out.1 = (f32[512,1152]{1,0:T(8,128)}, f32[512,1152]{1,0:T(8,128)}, bf16[512,1152]{1,0:T(8,128)(2,1)}) custom-call(bf16[512,1152]{1,0:T(8,128)(2,1)} %get-tuple-element.70.ob_ref, bf16[4,1152,1152]{2,1,0:T(8,128)(2,1)} %bitcast.34, f32[1,1152]{1,0:T(1,128)} %get-tuple-element.175.bias_ref, bf16[512,1152]{1,0:T(8,128)(2,1)} %x_ref.3, ...), custom_call_target="tpu_custom_call" | custom-call | flops 1358954496 | bytes 9732096 | tf_op jit(solution)/shard_map/project_out/pallas_call | solution.py:1006
  269.3 2.6 reduce_sum.177
  273.0 49.7 %feed_forward.1 = (f32[512,1152]{1,0:T(8,128)}, f32[512,1152]{1,0:T(8,128)}, bf16[16,144,1152]{2,1,0:T(8,128)(2,1)}, bf16[16,144,1152]{2,1,0:T(8,128)(2,1)}, bf1...) custom-call(bf16[512,1152]{1,0:T(8,128)(2,1)} %get-tuple-element.72.a_ref, ...), custom_call_target="tpu_custom_call" | custom-call | flops 32614907904 | bytes 42467328 | tf_op jit(solution)/shard_map/feed_forward/pallas_call | solution.py:1129
  322.7 3.2 multiply_reduce_fusion
  332.2 3.4 pad.22.dr_ref
  335.6 9.2 %back_out.1 = (bf16[512,1152]{1,0:T(8,128)(2,1)}, f32[16,512]{1,0:T(8,128)}) custom-call(bf16[4,512,384]{2,1,0:T(8,128)(2,1)} %pad.22.dr_ref, bf16[4,1152,1152]{2,1,0:T(8,128)(2,1)} %bitcast.35, f32[1,1152]{1,0:T(1,128)} %broadcast_in_dim_reshape.3.hm_ref, bf16[512,1152]{1,0:T(8,128)(2,1)} %get-tuple-element.70.ob_ref), custom_call_target="tpu_custom_call" | custom-call | flops 1358954496 | bytes 2654208 | tf_op jit(solution)/shard_map/back_out/pallas_call | solution.py:1200
  344.8 33.1 %attend_back.1 = (bf16[512,1152]{1,0:T(8,128)(2,1)}, bf16[2,512,2304]{2,1,0:T(8,128)(2,1)}, bf16[2,512,2304]{2,1,0:T(8,128)(2,1)}) custom-call(s32[1,8]{1,0:T(1,128)} %len_ref.3, bf16[512,1152]{1,0:T(8,128)(2,1)} %get-tuple-element.67.q_ref, bf16[512,1152]{1,0:T(8,128)(2,1)} %get-tuple-element.78.do_ref, f32[16,512]{1,0:T(8,128)} %get-tuple-element.79.log_ref, ...), custom_call_target="tpu_custom_call" | custom-call | flops 24159191040 | bytes 47185920 | tf_op jit(solution)/shard_map/attend_back/pallas_call | solution.py:1275
  379.9 133.0 %first_scatter.1 = (bf16[512,2304]{1,0:T(8,128)(2,1)}, f32[144,1152]{1,0:T(8,128)}, f32[144,1152]{1,0:T(8,128)}) custom-call(bf16[2,512,2304]{2,1,0:T(8,128)(2,1)} %get-tuple-element.82.kv_far, bf16[2,512,2304]{2,1,0:T(8,128)(2,1)} %get-tuple-element.83.kv_near, bf16[2,2,2,2,144,1152]{5,4,3,2,1,0:T(8,128)(2,1)} %bitcast.42, ...), custom_call_target="tpu_custom_call" | custom-call | bytes 21233664 | tf_op jit(solution)/shard_map/first_scatter/pallas_call | solution.py:680
  512.9 3.9 pad_maximum_fusion
  517.7 5.7 copy.69
  523.4 6.0 copy.70
  529.5 4.1 pad.23.dy_ref
  533.6 23.3 %back_qkv.1 = (f32[512,1152]{1,0:T(8,128)}, bf16[16,144,1152]{2,1,0:T(8,128)(2,1)}, bf16[16,144,1152]{2,1,0:T(8,128)(2,1)}) custom-call(bf16[512,1152]{1,0:T(8,128)(2,1)} %get-tuple-element.77.a_ref, bf16[512,1152]{1,0:T(8,128)(2,1)} %get-tuple-element.70.ob_ref, bf16[4,512,896]{2,1,0:T(8,128)(2,1)} %pad.23.dy_ref, bf16[4,512,384]{2,1,0:T(8,128)(2,1)} %pad.22.dr_ref, ...), custom_call_target="tpu_custom_call" | custom-call | flops 9512681472 | bytes 21233664 | tf_op jit(solution)/shard_map/back_qkv/pallas_call | solution.py:1335
  562.0 5.2 fusion.12
  572.1 62.8 %last_scatter.1 = (f32[144,1152]{1,0:T(8,128)}, f32[8,1728]{1,0:T(8,128)}, f32[1,512]{1,0:T(1,128)}, f32[8,1,256]{2,1,0:T(1,128)}) custom-call(f32[32,1,2304]{2,1,0:T(1,128)} %broadcast_in_dim.69.note_ref, bf16[144,1728]{1,0:T(8,128)(2,1)} %convert_element_type.86.ada_ref, bf16[2,2,2,2,144,1152]{5,4,3,2,1,0:T(8,128)(2,1)} %bitcast.40, ...), custom_call_target="tpu_custom_call" | custom-call | bytes 10616832 | tf_op jit(solution)/shard_map/last_scatter/pallas_call | solution.py:816
  637.8 4.4 all-to-all-start.1
  642.3 3.0 multiply_add_fusion.7
  648.5 3.4 multiply_add_fusion.2
  654.8 3.3 multiply_add_fusion.4
  (229 shorter events, 59.4 us)
Async XLA Ops:
  0.7 6.6 copy-start.54
  0.7 6.8 %copy-start.58 = (f32[504]{0:T(512)S(1)}, f32[504]{0:T(512)}, u32[]{:S(2)}) copy-start(f32[504]{0:T(512)} %param.60) | copy-start | bytes 6052
  0.7 7.5 %copy-start.13 = (f32[144,1728]{1,0:T(8,128)S(1)}, f32[144,1728]{1,0:T(8,128)}, u32[]{:S(2)}) copy-start(f32[144,1728]{1,0:T(8,128)} %param.40) | copy-start | bytes 2985988
  2.2 6.8 %copy-start.27 = (f32[144,288]{1,0:T(8,128)S(1)}, f32[144,288]{1,0:T(8,128)}, u32[]{:S(2)}) copy-start(f32[144,288]{1,0:T(8,128)} %param.48) | copy-start | bytes 497668
  2.2 6.8 %copy-start.22 = (f32[144,864]{1,0:T(8,128)S(1)}, f32[144,864]{1,0:T(8,128)}, u32[]{:S(2)}) copy-start(f32[144,864]{1,0:T(8,128)} %param.44) | copy-start | bytes 1492996
  3.1 104.9 %all-to-all-start = ((bf16[4,144,288]{2,1,0:T(8,128)(2,1)}), bf16[4,144,288]{2,1,0:T(8,128)(2,1)}, u32[]{:S(2)}, u32[]{:S(2)}) async-start(bf16[4,144,288]{2,1,0:T(8,128)(2,1)} %bitcast.3), calls=%async_computation | async-start | bytes 884736 | tf_op jit(solution)/shard_map/all_to_all | solution.py:1395
  9.1 73.3 %copy-start.1 = (bf16[512,1152]{1,0:T(8,128)(2,1)S(1)}, bf16[512,1152]{1,0:T(8,128)(2,1)}, u32[]{:S(2)}) copy-start(bf16[512,1152]{1,0:T(8,128)(2,1)} %x_ref.3) | copy-start | bytes 3538948
  9.1 73.5 %copy-start.38 = (s32[10,4608]{1,0:T(8,128)S(1)}, s32[10,4608]{1,0:T(8,128)}, u32[]{:S(2)}) copy-start(s32[10,4608]{1,0:T(8,128)} %param.39) | copy-start | bytes 552964
  10.0 73.4 %copy-start.6 = (bf16[512,1152]{1,0:T(8,128)(2,1)S(1)}, bf16[512,1152]{1,0:T(8,128)(2,1)}, u32[]{:S(2)}) copy-start(bf16[512,1152]{1,0:T(8,128)(2,1)} %param.34) | copy-start | bytes 3538948
  82.4 16.0 %copy-start.56 = (f32[512]{0:T(512)}, f32[512]{0:T(512)S(1)}, u32[]{:S(2)}) copy-start(f32[512]{0:T(512)S(1)} %convert_element_type.92) | copy-start | bytes 6148
  84.8 13.6 %copy-start.60 = (s32[10,16]{1,0:T(8,128)S(1)}, s32[10,16]{1,0:T(8,128)}, u32[]{:S(2)}) copy-start(s32[10,16]{1,0:T(8,128)} %param.38) | copy-start | bytes 1924
  84.8 14.5 %copy-start.20 = (f32[144,1152]{1,0:T(8,128)S(1)}, f32[144,1152]{1,0:T(8,128)}, u32[]{:S(2)}) copy-start(f32[144,1152]{1,0:T(8,128)} %param.52) | copy-start | bytes 1990660
  273.0 49.7 %copy-start.42 = (f32[1152]{0:T(1024)S(1)}, f32[1152]{0:T(1024)}, u32[]{:S(2)}) copy-start(f32[1152]{0:T(1024)} %get-tuple-element.191) | copy-start | bytes 13828
  379.9 133.0 %copy-start.12 = (bf16[512,1152]{1,0:T(8,128)(2,1)S(1)}, bf16[512,1152]{1,0:T(8,128)(2,1)}, u32[]{:S(2)}) copy-start(bf16[512,1152]{1,0:T(8,128)(2,1)} %get-tuple-element.81) | copy-start | bytes 3538948
  533.6 23.3 %copy-start.2 = (bf16[512,1152]{1,0:T(8,128)(2,1)S(1)}, bf16[512,1152]{1,0:T(8,128)(2,1)}, u32[]{:S(2)}) copy-start(bf16[512,1152]{1,0:T(8,128)(2,1)} %x_ref.3) | copy-start | bytes 3538948
  533.6 23.3 %copy-start.44 = (f32[512]{0:T(512)S(1)}, f32[512]{0:T(512)}, u32[]{:S(2)}) copy-start(f32[512]{0:T(512)} %broadcast_multiply_fusion) | copy-start | bytes 6148
  572.1 63.8 %copy-start.55 = (f32[1,1152]{1,0:T(1,128)S(1)}, f32[1,1152]{1,0:T(1,128)}, u32[]{:S(2)}) copy-start(f32[1,1152]{1,0:T(1,128)} %param.33) | copy-start | bytes 13828
  572.1 64.4 %copy-start.36 = (f32[144,1152]{1,0:T(8,128)S(1)}, f32[144,1152]{1,0:T(8,128)}, u32[]{:S(2)}) copy-start(f32[144,1152]{1,0:T(8,128)} %get-tuple-element.99) | copy-start | bytes 1990660
  634.9 7.3 %copy-start.23 = (f32[144,864]{1,0:T(8,128)S(1)}, f32[144,864]{1,0:T(8,128)}, u32[]{:S(2)}) copy-start(f32[144,864]{1,0:T(8,128)} %param.44) | copy-start | bytes 1492996
  634.9 7.3 %copy-start.29 = (f32[144,1152]{1,0:T(8,128)S(1)}, f32[144,1152]{1,0:T(8,128)}, u32[]{:S(2)}) copy-start(f32[144,1152]{1,0:T(8,128)} %get-tuple-element.97) | copy-start | bytes 1990660
  634.9 7.3 %copy-start.37 = (f32[144,864]{1,0:T(8,128)S(1)}, f32[144,864]{1,0:T(8,128)}, u32[]{:S(2)}) copy-start(f32[144,864]{1,0:T(8,128)} %param.47) | copy-start | bytes 1492996
  637.8 17.0 %all-to-all-start.1 = ((bf16[144,4,288]{2,0,1:T(8,128)(2,1)}), bf16[144,4,288]{2,0,1:T(8,128)(2,1)}, u32[]{:S(2)}, u32[]{:S(2)}) async-start(bf16[144,4,288]{2,0,1:T(8,128)(2,1)} %copy.74), calls=%async_computation.1 | async-start | bytes 884736 | tf_op jit(solution)/shard_map/all_to_all | solution.py:1562
  648.5 6.3 copy-start.16
  648.5 6.3 copy-start.17
  (44 other events, 162.7 us)

commit v2 on v1

--- a/solution.py
+++ b/solution.py
@@ -188,9 +188,11 @@
             self.hop(phase + 1).start()
         self.across(phase + 1).start()
 
-    def finish(self):
+    def collect(self):
         for phase in range(5):
             self.across(phase).wait_recv()
+
+    def finish(self):
         for phase in range(4):
             self.hop(phase).wait_send()
         for phase in range(5):
@@ -198,63 +200,75 @@
 
 
 GATHER_SEMS = 10
-PAIR_SHARES = (32, 32, 32, 32, 16)
-REST_SHARES = (48, 48, 48)
+SHARES = (32, 32, 32, 32, 16)
 PAIR_PARTS = (
+    (Z1, Z0, Y, X),
     (Z1, Y, X, Z0),
-    (Z1, X, Y, Z0),
     (Z1, Z0, X, Y),
-    (Z1, Z0, Y, X),
-    (Z1, Z0, X, Y),
-)
-PAIR_EVENTS = (
-    (0, 0), (1, 0), (2, 0), (0, 1), (3, 0), (1, 1), (4, 0), (2, 1), (0, 2), (3, 1),
-    (1, 2), (2, 2), (4, 1), (3, 2), (4, 2), (2, 3), (0, 3), (3, 3), (4, 3), (1, 3),
+    (Z0, Z1, Y, X),
+    (Z0, Z1, X, Y),
 )
 UP_PARTS = (
     (Z1, Y, Z0, X),
-    (Z1, Y, X, Z0),
-    (Z1, X, Z0, Y),
+    (Z1, Y, Z0, X),
+    (Z1, X, Y, Z0),
+    (Z1, Y, Z0, X),
+    (Z1, Y, Z0, X),
 )
 DOWN_PARTS = (
-    (Z1, Z0, Y, X),
-    (Z0, Z1, Y, X),
-    (Y, Z1, X, Z0),
+    (Z1, Y, X, Z0),
+    (Z1, Y, X, Z0),
+    (Z1, Z0, X, Y),
+    (Z1, Y, Z0, X),
+    (X, Z1, Y, Z0),
 )
-REST_EVENTS = (
-    (5, 0), (0, 0), (1, 0), (0, 1), (2, 0), (1, 1), (3, 0), (4, 0), (2, 1), (5, 1),
-    (1, 2), (0, 2), (5, 2), (3, 1), (4, 1), (3, 2), (0, 3), (2, 2), (4, 2), (3, 3),
-    (1, 3), (2, 3), (4, 3), (5, 3),
+BEGIN, PLANE, KV = -1, -2, -3
+GATHER_STEPS = (
+    (0, 0), (1, 0), (2, 0), (3, 0), (4, 0), (1, 1), (0, 1), (2, 1), (1, 2), (3, 1),
+    (0, 2), (4, 1), (-1, 0), (2, 2), (3, 2), (1, 3), (0, 3), (5, 0), (4, 2), (14, 0),
+    (6, 0), (2, 3), (7, 0), (5, 1), (8, 0), (9, 0), (4, 3), (10, 0), (3, 3), (-2, 0),
+    (6, 1), (11, 0), (7, 1), (8, 1), (-2, 1), (12, 0), (9, 1), (13, 0), (10, 1), (-2, 2),
+    (14, 1), (11, 1), (-2, 3), (-3, 0), (-3, 1), (-3, 2), (-3, 3), (5, 2), (7, 2), (10, 2),
+    (13, 1), (6, 2), (14, 2), (11, 2), (8, 2), (12, 1), (9, 2), (5, 3), (7, 3), (6, 3),
+    (10, 3), (8, 3), (13, 2), (12, 2), (14, 3), (9, 3), (11, 3), (12, 3), (13, 3),
+)
+NOTE = -4
+DOWN_SUM_PARTS = (
+    (X, Z0, Y, Z1),
+    (Z0, X, Z1, Y),
+    (X, Z0, Y, Z1),
+    (Z0, X, Y, Z1),
+    (X, Z0, Y, Z1),
+)
+FIRST_SUM_STEPS = (
+    (-3, 0), (-3, 1), (-3, 2), (-3, 3), (0, -1), (1, -1), (2, -1), (3, -1), (4, -1), (0, 0),
+    (1, 0), (2, 0), (3, 0), (4, 0), (0, 1), (1, 1), (2, 1), (4, 1), (3, 1), (0, 2),
+    (2, 2), (1, 2), (4, 2), (0, 3), (3, 2), (1, 3), (2, 3), (4, 3), (3, 3),
+)
+UP_SUM_PARTS = (
+    (Z0, X, Z1, Y),
+    (X, Z0, Z1, Y),
+    (Y, X, Z0, Z1),
+    (Z0, Y, X, Z1),
+    (Y, X, Z1, Z0),
 )
 PAIR_SUM_PARTS = (
     (Y, X, Z0, Z1),
-    (X, Z0, Y, Z1),
-    (Z0, X, Y, Z1),
-    (Y, Z0, X, Z1),
     (Y, X, Z0, Z1),
+    (X, Y, Z0, Z1),
+    (Y, X, Z0, Z1),
+    (Z0, Y, X, Z1),
 )
-PAIR_SUM_EVENTS = (
-    (0, -1), (1, -1), (2, -1), (3, -1), (4, -1), (0, 0), (1, 0), (2, 0), (0, 1), (1, 1),
-    (3, 0), (2, 1), (0, 2), (4, 0), (1, 2), (3, 1), (4, 1), (2, 2), (0, 3), (1, 3),
-    (3, 2), (4, 2), (2, 3), (3, 3), (4, 3),
+LAST_SUM_STEPS = (
+    (-2, 0), (0, -1), (1, -1), (2, -1), (-2, 1), (3, -1), (4, -1), (-2, 2), (0, 0), (-2, 3),
+    (5, -1), (6, -1), (7, -1), (1, 0), (2, 0), (8, -1), (9, -1), (4, 0), (0, 1), (3, 0),
+    (-4, 0), (1, 1), (5, 0), (7, 0), (9, 0), (2, 1), (0, 2), (4, 1), (6, 0), (1, 2),
+    (5, 1), (2, 2), (4, 2), (6, 1), (5, 2), (8, 0), (2, 3), (4, 3), (3, 1), (6, 2),
+    (8, 1), (5, 3), (7, 1), (3, 2), (6, 3), (9, 1), (8, 2), (0, 3), (1, 3), (7, 2),
+    (9, 2), (3, 3), (8, 3), (7, 3), (9, 3),
 )
-UP_SUM_PARTS = (
-    (X, Y, Z0, Z1),
-    (Z0, X, Y, Z1),
-    (X, Y, Z0, Z1),
-)
-DOWN_SUM_PARTS = (
-    (Z0, X, Y, Z1),
-    (Z0, X, Y, Z1),
-    (X, Y, Z0, Z1),
-)
-REST_SUM_EVENTS = (
-    (0, -1), (1, -1), (2, -1), (3, -1), (4, -1), (5, -1), (0, 0), (1, 0), (0, 1), (2, 0),
-    (3, 0), (2, 1), (5, 0), (4, 0), (0, 2), (1, 1), (2, 2), (5, 1), (0, 3), (1, 2),
-    (3, 1), (2, 3), (5, 2), (3, 2), (4, 1), (1, 3), (5, 3), (4, 2), (3, 3), (4, 3),
-)
-NOTE_EVENT = 5
-KV_EVENTS = (2, 6, 10, 14)
+NOTE_STEP = 5
+KV_PIECES = 4
 
 
 def split_gatherings(block_ref, out_ref, layout, shares, orders, send, recv, base):
@@ -267,24 +281,39 @@
     return moving
 
 
-def first_gather_kernel(
+def gather_kernel(
     note_ref,
     ada_ref,
-    block_ref,
-    out_ref,
-    inbox_ref,
+    pair_ref,
+    up_ref,
+    down_ref,
+    x_ref,
+    pair_out,
+    up_out,
+    down_out,
+    kv_out,
     silu_ref,
     mod_ref,
+    bias_ref,
+    a_ref,
+    q_ref,
+    inbox,
     parts,
     returns,
+    row,
+    weights,
+    acc,
+    kv,
     note_send,
     note_recv,
     mod_send,
     mod_recv,
+    weight_sem,
     send,
     recv,
 ):
     bucket, seq = lax.axis_index("bucket"), lax.axis_index("seq")
+    place = my_coords()
     me = bucket * PLANES + seq
     count = BLOCKS * PLANES
     barrier = pltpu.get_barrier_semaphore()
@@ -298,8 +327,8 @@
     def note(distance):
         peer = peer_at(distance)
         return pltpu.make_async_remote_copy(
-            src_ref=note_ref.at[peer[0] * PLANES + peer[1]],
-            dst_ref=inbox_ref.at[me],
+            src_ref=note_ref.at[peer[0]],
+            dst_ref=inbox.at[me],
             send_sem=note_send.at[distance],
             recv_sem=note_recv.at[distance],
             device_id=peer,
@@ -321,44 +350,144 @@
     def _(distance):
         note(distance).start()
 
-    inbox_ref[me] = note_ref[me]
-    moving = split_gatherings(
-        block_ref, out_ref, "planes", PAIR_SHARES, PAIR_PARTS, send, recv, 0
-    )
-    for part in moving:
+    inbox[me] = note_ref[bucket]
+    base = len(PAIR_PARTS) * GATHER_SEMS
+    pairs = split_gatherings(pair_ref, pair_out, "planes", SHARES, PAIR_PARTS, send, recv, 0)
+    rest = split_gatherings(up_ref, up_out, "planes", SHARES, UP_PARTS, send, recv, base)
+    base += len(UP_PARTS) * GATHER_SEMS
+    rest += split_gatherings(down_ref, down_out, "rows", SHARES, DOWN_PARTS, send, recv, base)
+    base += len(DOWN_PARTS) * GATHER_SEMS
+    moving = pairs + rest
+    for part in pairs:
         part.begin()
 
-    for part, phase in PAIR_EVENTS[:NOTE_EVENT]:
-        moving[part].advance(phase)
-
-    @pl.loop(1, count)
-    def _(distance):
-        note(distance).wait_recv()
-
-    rows = ada_ref.shape[0]
-    heard = jnp.concatenate([inbox_ref[PLANES * g, :, :] for g in range(BLOCKS)])
-    silu = jax.nn.silu(heard[:, :rows]).astype(bfloat)
-    silu_ref[...] = silu
-    mods = dot_nn(silu, ada_ref[...])
-    for group in range(BLOCKS):
-        parts[group] = mods[group : group + 1, :]
-    returns[me] = parts[bucket]
-
-    @pl.loop(1, count)
-    def _(distance):
-        answer(distance).start()
-
-    for part, phase in PAIR_EVENTS[NOTE_EVENT:]:
-        moving[part].advance(phase)
-
-    @pl.loop(1, count)
-    def _(distance):
-        answer(distance).wait_recv()
-
-    for plane in range(PLANES):
-        mod_ref[plane] = sum(returns[PLANES * g + plane] for g in range(BLOCKS))
+    rows, width = ada_ref.shape[0], x_ref.shape[1]
+    cols = 3 * width // PLANES
+    local = x_ref.shape[0] // KV_PIECES
+
+    def kv_copy(source, target, slot, bit):
+        return pltpu.make_async_remote_copy(
+            src_ref=source,
+            dst_ref=target,
+            send_sem=send.at[base + slot],
+            recv_sem=recv.at[base + slot],
+            device_id=partner(bit),
+            device_id_type=MESH,
+        )
+
+    def kv_step(piece, kind):
+        span = pl.ds(piece * local, local)
+        mine = kv_out.at[place[Y], place[CORE], span, :]
+        other = kv_out.at[1 - place[Y], place[CORE], span, :]
+        if kind == "over":
+            return kv_copy(kv.at[span, :], mine, 4 * piece, Y)
+        if kind == "near":
+            return kv_copy(kv.at[span, :], mine, 4 * piece + 1, CORE)
+        if kind == "far":
+            return kv_copy(other, other, 4 * piece + 2, CORE)
+        return pltpu.make_async_copy(kv.at[span, :], mine, send.at[base + 4 * piece + 3])
+
+    def load(plane):
+        source = pair_out.at[plane // 2, plane % 2, :, :, :, :, pl.ds(0, weights.shape[5])]
+        return pltpu.make_async_copy(source, weights.at[plane % 2], weight_sem.at[plane % 2])
+
+    def modulations():
+        @pl.loop(1, count)
+        def _(distance):
+            note(distance).wait_recv()
+
+        head = jnp.concatenate(
+            [inbox[PLANES * g, NOTE_ROWS - 2 : NOTE_ROWS - 1, :] for g in range(BLOCKS)]
+        )
+        tail = jnp.concatenate(
+            [inbox[PLANES * g, NOTE_ROWS - 1 : NOTE_ROWS, :] for g in range(BLOCKS)]
+        )
+        head, tail = jax.nn.silu(head).astype(bfloat), jax.nn.silu(tail).astype(bfloat)
+        silu_ref[:, :LANES] = head
+        silu_ref[:, LANES:] = tail
+        mods = dot_nn(head, ada_ref[:LANES, :]) + dot_nn(
+            tail[:, : rows - LANES], ada_ref[LANES:, :]
+        )
+        for group in range(BLOCKS):
+            parts[group] = mods[group : group + 1, :]
+        returns[me] = parts[bucket]
+
+        @pl.loop(1, count)
+        def _(distance):
+            answer(distance).start()
+
+    def biases():
+        each = width // count
+        lane = lax.broadcasted_iota(jnp.int32, (LANES, width), 1)
+        entry = lax.broadcasted_iota(jnp.int32, (LANES, width), 0)
+        copies = (lane % each == entry).astype(single).astype(bfloat)
+        owner = lax.broadcasted_iota(jnp.int32, (NOTE_ROWS, width), 1) // each
+        total = jnp.zeros((NOTE_ROWS, width), single)
+        for device in range(count):
+            spread = dot_nn(inbox[device].astype(bfloat), copies)
+            total = jnp.where(owner == device, spread, total)
+        bias_ref[...] = total
+
+    def projection(plane):
+        if plane == 0:
+            for part in pairs:
+                part.collect()
+            load(0).start()
+            load(1).start()
+
+            @pl.loop(1, count)
+            def _(distance):
+                answer(distance).wait_recv()
+
+            for index in range(PLANES):
+                wide = returns.shape[2]
+                row[:, index * wide : (index + 1) * wide] = sum(
+                    returns[PLANES * g + index] for g in range(BLOCKS)
+                )
+            for index in range(6):
+                mod_ref[index : index + 1, :] = (
+                    row[:, index * width : (index + 1) * width] + bias_ref[index : index + 1, :]
+                )
+            a_ref[...] = modulate(
+                x_ref[...].astype(single), mod_ref[0:1, :], mod_ref[1:2, :]
+            ).astype(bfloat)
+        load(plane).wait()
+        weight = weights[plane % 2].reshape(width, weights.shape[5])
+        acc[:, plane * cols : (plane + 1) * cols] = dot_nn(a_ref[...], weight)[:, :cols]
+        if plane + 2 < PLANES:
+            load(plane + 2).start()
+        if plane == PLANES - 1:
+            q_ref[...] = (acc[:, :width] + bias_ref[6:7, :]).astype(bfloat)
+            kv[:, :width] = acc[:, width : 2 * width].astype(bfloat)
+            kv[:, width:] = (acc[:, 2 * width :] + bias_ref[7:8, :]).astype(bfloat)
+
+    for step, (part, phase) in enumerate(GATHER_STEPS):
+        if step == NOTE_STEP:
+            modulations()
+            biases()
+        if part == BEGIN:
+            for moved in rest:
+                moved.begin()
+        elif part == PLANE:
+            projection(phase)
+        elif part == KV:
+            for kind in ("over", "near", "keep"):
+                kv_step(phase, kind).start()
+        else:
+            moving[part].advance(phase)
+    for piece in range(KV_PIECES):
+        kv_step(piece, "over").wait_recv()
+        kv_step(piece, "far").start()
+    for part in rest:
+        part.collect()
     for part in moving:
         part.finish()
+    for piece in range(KV_PIECES):
+        kv_step(piece, "near").wait_recv()
+        kv_step(piece, "far").wait_recv()
+        kv_step(piece, "keep").wait()
+        for kind in ("over", "near", "far"):
+            kv_step(piece, kind).wait_send()
 
     @pl.loop(1, count)
     def _(distance):
@@ -366,113 +495,61 @@
         answer(distance).wait_send()
 
 
-def first_gather(notes, ada_low, block):
-    rows, width = block.shape
+NOTE_ROWS = 16
+
+
+def gather(notes, ada_low, pair_block, up_block, down_block, tokens):
+    rows, width = pair_block.shape
+    local = tokens.shape[0]
     count = BLOCKS * PLANES
     cols = ada_low.shape[1]
-    out, inbox, silu, mods = pl.pallas_call(
-        first_gather_kernel,
+    wide = -(-3 * width // PLANES // LANES) * LANES
+    blocks = jax.ShapeDtypeStruct((2, 2, 2, 2, 2, rows, width), bfloat)
+    sems = 3 * len(SHARES) * GATHER_SEMS + 4 * KV_PIECES
+    pair, up, down, kv, silu, mods, biases, first_in, query = pl.pallas_call(
+        gather_kernel,
         out_shape=(
-            jax.ShapeDtypeStruct((2, 2, 2, 2, 2, rows, width), bfloat),
-            jax.ShapeDtypeStruct(notes.shape, single),
-            jax.ShapeDtypeStruct((BLOCKS, rows), bfloat),
-            jax.ShapeDtypeStruct((PLANES, 1, cols), single),
+            blocks,
+            blocks,
+            blocks,
+            jax.ShapeDtypeStruct((2, 2, local, 2 * width), bfloat),
+            jax.ShapeDtypeStruct((BLOCKS, 2 * LANES), bfloat),
+            jax.ShapeDtypeStruct((8, width), single),
+            jax.ShapeDtypeStruct((NOTE_ROWS, width), single),
+            jax.ShapeDtypeStruct((local, width), bfloat),
+            jax.ShapeDtypeStruct((local, width), bfloat),
         ),
-        in_specs=[IN_VMEM] * 3,
-        out_specs=(IN_HBM, IN_VMEM, IN_VMEM, IN_VMEM),
+        in_specs=[IN_VMEM] * 6,
+        out_specs=(IN_HBM,) * 4 + (IN_VMEM,) * 5,
         scratch_shapes=[
+            pltpu.VMEM((count, NOTE_ROWS, LANES), single),
             pltpu.VMEM((BLOCKS, 1, cols), single),
             pltpu.VMEM((count, 1, cols), single),
+            pltpu.VMEM((1, 6 * width), single),
+            pltpu.VMEM((2, 2, 2, 2, rows, wide), bfloat),
+            pltpu.VMEM((local, 3 * width), single),
+            pltpu.VMEM((local, 2 * width), bfloat),
         ]
         + [pltpu.SemaphoreType.DMA((count,))] * 4
-        + [pltpu.SemaphoreType.DMA((len(PAIR_PARTS) * GATHER_SEMS,))] * 2,
+        + [pltpu.SemaphoreType.DMA((2,))]
+        + [pltpu.SemaphoreType.DMA((sems,))] * 2,
         compiler_params=pltpu.CompilerParams(
             collective_id=1, has_side_effects=True, vmem_limit_bytes=VMEM_LIMIT
         ),
-        cost_estimate=cost(0, 64 * rows * width),
-        name="first_gather",
-    )(notes, ada_low, block)
-    return out.reshape(PLANES, BLOCKS * rows, width), inbox, silu, mods
-
-
-def second_gather_kernel(
-    up_ref, down_ref, kv_ref, up_out, down_out, kv_out, send, recv
-):
-    me = my_coords()
-    greet([partner(bit) for bit in (X, Z0, Z1, CORE, Y)])
-    base = len(UP_PARTS) * GATHER_SEMS
-    moving = split_gatherings(
-        up_ref, up_out, "planes", REST_SHARES, UP_PARTS, send, recv, 0
-    )
-    moving += split_gatherings(
-        down_ref, down_out, "rows", REST_SHARES, DOWN_PARTS, send, recv, base
-    )
-    base = len(moving) * GATHER_SEMS
-
-    def kv_copy(source, place, slot, bit):
-        return pltpu.make_async_remote_copy(
-            src_ref=source,
-            dst_ref=place,
-            send_sem=send.at[base + slot],
-            recv_sem=recv.at[base + slot],
-            device_id=partner(bit),
-            device_id_type=MESH,
-        )
-
-    count = kv_ref.shape[0] // len(KV_EVENTS)
-    overs, nears, fars, keeps = [], [], [], []
-    for index in range(len(KV_EVENTS)):
-        rows = pl.ds(index * count, count)
-        own = kv_ref.at[rows, :]
-        mine = kv_out.at[me[Y], me[CORE], rows, :]
-        other = kv_out.at[1 - me[Y], me[CORE], rows, :]
-        overs.append(kv_copy(own, mine, 4 * index, Y))
-        nears.append(kv_copy(own, mine, 4 * index + 1, CORE))
-        fars.append(kv_copy(other, other, 4 * index + 2, CORE))
-        keeps.append(pltpu.make_async_copy(own, mine, send.at[base + 4 * index + 3]))
-    for part in moving:
-        part.begin()
-    for copy in nears + keeps:
-        copy.start()
-    for index, (part, phase) in enumerate(REST_EVENTS):
-        for piece, event in enumerate(KV_EVENTS):
-            if index == event:
-                overs[piece].start()
-        moving[part].advance(phase)
-    for over, far in zip(overs, fars):
-        over.wait_recv()
-        far.start()
-    for part in moving:
-        part.finish()
-    for over, near, far, keep in zip(overs, nears, fars, keeps):
-        near.wait_recv()
-        far.wait_recv()
-        keep.wait()
-        for copy in (over, near, far):
-            copy.wait_send()
-
-
-def second_gather(up_block, down_block, key_value):
-    rows, width = up_block.shape
-    local, wide = key_value.shape
-    blocks = jax.ShapeDtypeStruct((2, 2, 2, 2, 2, rows, width), bfloat)
-    up, down, kv = pl.pallas_call(
-        second_gather_kernel,
-        out_shape=(blocks, blocks, jax.ShapeDtypeStruct((2, 2, local, wide), bfloat)),
-        in_specs=[IN_VMEM] * 3,
-        out_specs=(IN_HBM,) * 3,
-        scratch_shapes=[pltpu.SemaphoreType.DMA(((len(UP_PARTS) + len(DOWN_PARTS)) * GATHER_SEMS + 4 * len(KV_EVENTS),))] * 2,
-        compiler_params=pltpu.CompilerParams(
-            collective_id=2, has_side_effects=True, vmem_limit_bytes=VMEM_LIMIT
-        ),
-        cost_estimate=cost(0, 128 * rows * width),
-        name="second_gather",
-    )(up_block, down_block, key_value)
-    count = BLOCKS * PLANES * rows
+        cost_estimate=cost(6 * local * width * width, 200 * rows * width),
+        name="gather",
+    )(notes, ada_low, pair_block, up_block, down_block, tokens)
+    tall = BLOCKS * rows
     return (
-        up.reshape(PLANES, BLOCKS * rows, width),
-        down.reshape(count, width),
-        kv.reshape(PLANES * local, wide),
+        pair.reshape(PLANES, tall, width),
+        up.reshape(PLANES, tall, width),
+        down.reshape(PLANES * tall, width),
+        kv.reshape(PLANES * local, 2 * width),
+        silu[:, :rows],
+        mods,
+        biases,
+        first_in,
+        query,
     )
 
 
@@ -602,20 +679,14 @@
     return moving
 
 
-def first_scatter_kernel(
-    kv_far, kv_near, up_far, up_near, down_far, down_near, kv_out, up_out, down_out, *refs
-):
-    up_scratch, down_scratch, (kv_total, kv_arrival, send, recv) = refs[:5], refs[5:10], refs[10:]
+def first_scatter_kernel(kv_far, kv_near, down_far, down_near, kv_out, down_out, *refs):
+    scratch, (kv_total, kv_arrival, send, recv) = refs[:5], refs[5:]
     greet([partner(bit) for bit in (X, Z0, Z1, CORE, Y)])
-    base = len(UP_SUM_PARTS) * SCATTER_SEMS
     moving = split_scatterings(
-        up_far, up_near, up_scratch, up_out, REST_SHARES, UP_SUM_PARTS, send, recv, 0
-    ) + split_scatterings(
-        down_far, down_near, down_scratch, down_out, REST_SHARES, DOWN_SUM_PARTS, send, recv, base
+        down_far, down_near, scratch, down_out, SHARES, DOWN_SUM_PARTS, send, recv, 0
     )
     base = len(moving) * SCATTER_SEMS
-    local = kv_out.shape[0]
-    count = local // len(KV_EVENTS)
+    count = kv_out.shape[0] // KV_PIECES
 
     def kv_copy(source, place, slot, bit):
         return pltpu.make_async_remote_copy(
@@ -627,63 +698,59 @@
             device_id_type=MESH,
         )
 
-    nears, overs = [], []
-    for index in range(len(KV_EVENTS)):
-        rows = pl.ds(index * count, count)
-        nears.append(
-            kv_copy(kv_far.at[:, rows, :], kv_total.at[:, rows, :], 2 * index, CORE)
-        )
-        overs.append(
-            kv_copy(kv_total.at[1, rows, :], kv_arrival.at[rows, :], 2 * index + 1, Y)
-        )
-    nears[0].start()
-    for part in moving:
-        part.across().start()
-    for near in nears[1:]:
-        near.start()
-
-    def kv_add(index, side):
-        rows = pl.ds(index * count, count)
+    def near(piece):
+        rows = pl.ds(piece * count, count)
+        return kv_copy(kv_far.at[:, rows, :], kv_total.at[:, rows, :], 2 * piece, CORE)
+
+    def over(piece):
+        rows = pl.ds(piece * count, count)
+        return kv_copy(kv_total.at[1, rows, :], kv_arrival.at[rows, :], 2 * piece + 1, Y)
+
+    def kv_add(piece, side):
+        rows = pl.ds(piece * count, count)
         kv_total[side, rows, :] = (
             kv_total[side, rows, :].astype(single) + kv_near[side, rows, :].astype(single)
         ).astype(bfloat)
 
-    for index, (part, phase) in enumerate(REST_SUM_EVENTS):
-        for piece, event in enumerate(KV_SUM_EVENTS):
-            if index == event:
-                nears[piece].wait_recv()
-                kv_add(piece, 1)
-                overs[piece].start()
-                kv_add(piece, 0)
-        moving[part].advance(phase)
-    for index, over in enumerate(overs):
-        over.wait_recv()
-        rows = pl.ds(index * count, count)
+    for piece in range(KV_PIECES):
+        near(piece).start()
+    for part in moving:
+        part.across().start()
+    for part, phase in FIRST_SUM_STEPS:
+        if part == KV:
+            near(phase).wait_recv()
+            kv_add(phase, 1)
+            over(phase).start()
+            kv_add(phase, 0)
+        else:
+            moving[part].advance(phase)
+    for piece in range(KV_PIECES):
+        over(piece).wait_recv()
+        rows = pl.ds(piece * count, count)
         kv_out[rows, :] = (
             kv_total[0, rows, :].astype(single) + kv_arrival[rows, :].astype(single)
         ).astype(bfloat)
     for part in moving:
         part.finish()
-    for copy in nears + overs:
-        copy.wait_send()
-
-
-KV_SUM_EVENTS = (2, 9, 13, 17)
-
-
-def first_scatter(kv_far, kv_near, up_far, up_near, down_far, down_near):
-    rows, width = up_far.shape[1:]
+    for piece in range(KV_PIECES):
+        near(piece).wait_send()
+        over(piece).wait_send()
+
+
+def first_scatter(kv_far, kv_near, down_far, down_near):
+    rows, width = down_far.shape[1:]
     local, wide = kv_far.shape[1:]
     cube = (2, 2, 2, 2, rows, width)
-    mine = jax.ShapeDtypeStruct((rows, width), single)
-    sems = (len(UP_SUM_PARTS) + len(DOWN_SUM_PARTS)) * SCATTER_SEMS + 2 * len(KV_SUM_EVENTS)
+    sems = len(DOWN_SUM_PARTS) * SCATTER_SEMS + 2 * KV_PIECES
     return pl.pallas_call(
         first_scatter_kernel,
-        out_shape=(jax.ShapeDtypeStruct((local, wide), bfloat), mine, mine),
-        in_specs=[IN_HBM, IN_VMEM] * 3,
-        out_specs=(IN_VMEM,) * 3,
+        out_shape=(
+            jax.ShapeDtypeStruct((local, wide), bfloat),
+            jax.ShapeDtypeStruct((rows, width), single),
+        ),
+        in_specs=[IN_HBM, IN_VMEM] * 2,
+        out_specs=(IN_VMEM,) * 2,
         scratch_shapes=scatter_scratch(rows, width)
-        + scatter_scratch(rows, width)
         + [pltpu.VMEM((2, local, wide), bfloat), pltpu.VMEM((local, wide), bfloat)]
         + [pltpu.SemaphoreType.DMA((sems,))] * 2,
         compiler_params=pltpu.CompilerParams(
@@ -691,29 +758,48 @@
         ),
         cost_estimate=cost(0, 128 * rows * width),
         name="first_scatter",
-    )(
-        kv_far,
-        kv_near,
-        up_far.reshape(cube),
-        up_near.reshape(cube),
-        down_far.reshape(cube),
-        down_near.reshape(cube),
-    )
+    )(kv_far, kv_near, down_far.reshape(cube), down_near.reshape(cube))
+
+
+def norm_back(values, grad, scale_row):
+    centre = values - jnp.mean(values, axis=-1, keepdims=True)
+    root = lax.rsqrt(jnp.mean(centre * centre, axis=-1, keepdims=True) + EPSILON)
+    normed = centre * root
+    scaled = grad * (1.0 + scale_row)
+    inner = jnp.mean(scaled * normed, axis=-1, keepdims=True)
+    return root * (scaled - jnp.mean(scaled, axis=-1, keepdims=True) - normed * inner), normed
+
+
+def column_sum(values):
+    return jnp.sum(values, axis=0, keepdims=True)
 
 
 def last_scatter_kernel(
-    note_ref,
+    up_far,
+    up_near,
+    a_ref,
+    ob_ref,
+    dq_ref,
+    dkv_ref,
+    dr_ref,
+    w_ref,
+    x_ref,
+    dmid_ref,
+    mod_ref,
+    row_ref,
     ada_ref,
-    far_ref,
-    near_ref,
-    out_ref,
-    mod_ref,
+    up_out,
+    pair_out,
+    grad_ref,
+    mods_ref,
     bias_ref,
     silu_ref,
     *refs,
 ):
-    scratch, refs = refs[:5], refs[5:]
-    inbox, parts, returns, note_send, note_recv, back_send, back_recv, send, recv = refs
+    up_scratch, pair_scratch, refs = refs[:5], refs[5:10], refs[10:]
+    far, near, weights, dy, table, line, bias_notes, mod_notes, bias_box, mod_box = refs[:10]
+    parts, returns, weight_sem = refs[10:13]
+    bias_send, bias_recv, mod_send, mod_recv, back_send, back_recv, send, recv = refs[13:]
     bucket, seq = lax.axis_index("bucket"), lax.axis_index("seq")
     me = bucket * PLANES + seq
     count = BLOCKS * PLANES
@@ -725,70 +811,200 @@
 
     pl.semaphore_wait(barrier, count - 1)
 
-    def note(distance):
+    def message(source, target, out_sem, in_sem, distance):
+        return pltpu.make_async_remote_copy(
+            src_ref=source,
+            dst_ref=target,
+            send_sem=out_sem.at[distance],
+            recv_sem=in_sem.at[distance],
+            device_id=peer_at(distance),
+            device_id_type=MESH,
+        )
+
+    def bias_note(distance):
         peer = peer_at(distance)
-        return pltpu.make_async_remote_copy(
-            src_ref=note_ref.at[peer[0] * PLANES + peer[1]],
-            dst_ref=inbox.at[me],
-            send_sem=note_send.at[distance],
-            recv_sem=note_recv.at[distance],
-            device_id=peer,
-            device_id_type=MESH,
-        )
+        source = bias_notes.at[peer[0] * PLANES + peer[1]]
+        return message(source, bias_box.at[me], bias_send, bias_recv, distance)
+
+    def mod_note(distance):
+        source = mod_notes.at[peer_at(distance)[1]]
+        return message(source, mod_box.at[me], mod_send, mod_recv, distance)
 
     def answer(distance):
-        peer = peer_at(distance)
-        return pltpu.make_async_remote_copy(
-            src_ref=parts.at[peer[0]],
-            dst_ref=returns.at[me],
-            send_sem=back_send.at[distance],
-            recv_sem=back_recv.at[distance],
-            device_id=peer,
-            device_id_type=MESH,
-        )
-
-    moving = split_scatterings(
-        far_ref, near_ref, scratch, out_ref, PAIR_SHARES, PAIR_SUM_PARTS, send, recv, 0
-    )
-    for part in moving:
+        source = parts.at[peer_at(distance)[0]]
+        return message(source, returns.at[me], back_send, back_recv, distance)
+
+    base = len(UP_SUM_PARTS) * SCATTER_SEMS
+    ups = split_scatterings(
+        up_far, up_near, up_scratch, up_out, SHARES, UP_SUM_PARTS, send, recv, 0
+    )
+    pairs = split_scatterings(
+        far, near, pair_scratch, pair_out, SHARES, PAIR_SUM_PARTS, send, recv, base
+    )
+    moving = ups + pairs
+    for part in ups:
         part.across().start()
+
+    width = x_ref.shape[1]
+    rows = up_out.shape[0]
+    cols = 3 * width // PLANES
+    wide = dy.shape[1]
+    below = wide - LANES
+    order = (1, 3, 0, 2)
+
+    def load(step):
+        plane = seq ^ order[step]
+        return pltpu.make_async_copy(
+            w_ref.at[plane, :, pl.ds(0, wide)], weights.at[step % 2], weight_sem.at[step % 2]
+        )
+
+    def gather_dy(index):
+        low, high = index * cols, (index + 1) * cols
+        pieces = []
+        if low < width:
+            pieces.append(dq_ref[:, low : min(high, width)])
+        if high > width:
+            pieces.append(dkv_ref[:, max(low - width, 0) : high - width])
+        first = 0
+        for piece in pieces:
+            dy[:, first : first + piece.shape[1]] = piece
+            first += piece.shape[1]
+
+    def project(step):
+        bits = order[step]
+        plane = seq ^ bits
+        if step == 0:
+            load(0).start()
+            dy[:, cols:] = jnp.zeros((dy.shape[0], wide - cols), bfloat)
+            grad_ref[...] = jnp.zeros_like(grad_ref)
+        if step + 1 < PLANES:
+            load(step + 1).start()
+        for index in range(PLANES):
+
+            @pl.when(plane == index)
+            def _():
+                gather_dy(index)
+
+        target = far if bits % 2 else near
+        place = my_coords()
+
+        def store(values, first_col):
+            for block in range(BLOCKS):
+                spot = (
+                    bits // 2,
+                    (block % 2) ^ place[X],
+                    (block // 4) ^ place[Z1],
+                    (block // 2 % 2) ^ place[Z0],
+                    slice(None),
+                    slice(first_col, first_col + values.shape[1]),
+                )
+                target[spot] = values[block * rows : (block + 1) * rows, :].astype(bfloat)
+
+        store(dot_tn(a_ref[...], dy[:, :below]), 0)
+        edge = dot_tn(ob_ref[...], dr_ref[plane])
+        store(dot_tn(a_ref[...], dy[:, below:]) + edge[:, :LANES], below)
+        store(edge[:, LANES:], wide)
+        load(step).wait()
+        grad_ref[...] += dot_nt(dy[...], weights[step % 2])
+
+    def notes():
+        shift_sum, scale_sum = jnp.zeros((1, width), single), jnp.zeros((1, width), single)
+        scale_row = mod_ref[1:2, :]
+        for tile in range(0, x_ref.shape[0], LANES):
+            span = slice(tile, tile + LANES)
+            grad = grad_ref[span, :]
+            back, normed = norm_back(x_ref[span, :].astype(single), grad, scale_row)
+            shift_sum += column_sum(grad)
+            scale_sum += column_sum(grad * normed)
+            grad_ref[span, :] = dmid_ref[span, :] + back
+        line[:, :width] = shift_sum
+        line[:, width : 2 * width] = scale_sum
+        table[0:1, :] = shift_sum
+        table[1:2, :] = scale_sum
+        for index in range(4):
+            line[:, (2 + index) * width : (3 + index) * width] = row_ref[index : index + 1, :]
+        table[2:6, :] = row_ref[0:4, :]
+        table[6:7, :] = column_sum(dq_ref[...].astype(single))
+        table[7:8, :] = column_sum(dkv_ref[:, width:].astype(single))
+        table[8:14, :] = row_ref[4:10, :]
+        table[14:16, :] = jnp.zeros((2, width), single)
+        each = width // count
+        lane = lax.broadcasted_iota(jnp.int32, (LANES, width), 1)
+        entry = lax.broadcasted_iota(jnp.int32, (LANES, width), 0)
+        copies = (lane % each == entry).astype(single)
+        owner = lax.broadcasted_iota(jnp.int32, (NOTE_ROWS, width), 1) // each
+
+        @pl.loop(0, count)
+        def _(device):
+            mine = jnp.where(owner == device, table[...], 0.0)
+            bias_notes[device] = lax.dot_general(
+                mine,
+                copies,
+                (((1,), (1,)), ((), ())),
+                preferred_element_type=single,
+                precision=HIGHEST,
+            )
+
+        part = mod_notes.shape[2]
+        for index in range(PLANES):
+            mod_notes[index] = line[:, index * part : (index + 1) * part]
+        bias_box[me] = bias_notes[me]
+        mod_box[me] = mod_notes[seq]
+
+        @pl.loop(1, count)
+        def _(distance):
+            mod_note(distance).start()
+            bias_note(distance).start()
+
+    def answers():
+        @pl.loop(1, count)
+        def _(distance):
+            mod_note(distance).wait_recv()
+
+        sums = [sum(mod_box[PLANES * g + s] for s in range(PLANES)) for g in range(BLOCKS)]
+        mods = jnp.concatenate(sums)
+        mods_ref[...] = mods
+        silu = lax.dot_general(
+            mods,
+            ada_ref[...].astype(single),
+            (((1,), (1,)), ((), ())),
+            preferred_element_type=single,
+            precision=HIGHEST,
+        )
+        for group in range(BLOCKS):
+            parts[group, :, :rows] = silu[group : group + 1, :]
+            parts[group, :, rows:] = jnp.zeros((1, parts.shape[2] - rows), single)
+        returns[me] = parts[bucket]
+
+        @pl.loop(1, count)
+        def _(distance):
+            answer(distance).start()
+
+    since = 0
+    for part, phase in LAST_SUM_STEPS:
+        if part == PLANE:
+            project(phase)
+            if phase == 1:
+                for moved in pairs:
+                    moved.across().start()
+        elif part == NOTE:
+            notes()
+            since = 1
+        else:
+            moving[part].advance(phase)
+            since += since > 0
+            if since == ANSWER_AFTER:
+                answers()
 
     @pl.loop(1, count)
     def _(distance):
-        note(distance).start()
-
-    inbox[me] = note_ref[me]
-    for part, phase in PAIR_SUM_EVENTS[:SUM_NOTE_EVENT]:
-        moving[part].advance(phase)
-
-    @pl.loop(1, count)
-    def _(distance):
-        note(distance).wait_recv()
-
-    rows, cols = ada_ref.shape
-    spot = bias_ref.shape[1]
-    sums = [sum(inbox[PLANES * g + s] for s in range(PLANES)) for g in range(BLOCKS)]
-    bias_ref[...] = sum(sums)[:, :spot]
-    mods = jnp.concatenate(sums)[:, spot : spot + cols]
-    mod_ref[...] = mods
-    silu = lax.dot_general(
-        mods,
-        ada_ref[...].astype(single),
-        (((1,), (1,)), ((), ())),
-        preferred_element_type=single,
-        precision=HIGHEST,
-    )
-    for group in range(BLOCKS):
-        parts[group, :, :rows] = silu[group : group + 1, :]
-        parts[group, :, rows:] = jnp.zeros((1, parts.shape[2] - rows), single)
-    returns[me] = parts[bucket]
-
-    @pl.loop(1, count)
-    def _(distance):
-        answer(distance).start()
-
-    for part, phase in PAIR_SUM_EVENTS[SUM_NOTE_EVENT:]:
-        moving[part].advance(phase)
+        bias_note(distance).wait_recv()
+
+    bias_ref[...] = jnp.zeros_like(bias_ref)
+
+    @pl.loop(0, count)
+    def _(device):
+        bias_ref[...] += bias_box[device]
 
     @pl.loop(1, count)
     def _(distance):
@@ -801,42 +1017,86 @@
 
     @pl.loop(1, count)
     def _(distance):
-        note(distance).wait_send()
+        bias_note(distance).wait_send()
+        mod_note(distance).wait_send()
         answer(distance).wait_send()
 
 
-SUM_NOTE_EVENT = 9
-
-
-def last_scatter(notes, ada_low, far, near, spot):
-    rows, width = far.shape[1:]
+ANSWER_AFTER = 12
+
+
+def last_scatter(
+    up_far,
+    up_near,
+    first_in,
+    branch,
+    query_grad,
+    kv_grad,
+    dr_planes,
+    weight,
+    tokens,
+    middle_grad,
+    mods,
+    row_grads,
+    ada_low,
+):
+    rows, width = up_far.shape[1:]
     cube = (2, 2, 2, 2, rows, width)
     count = BLOCKS * PLANES
     cols = ada_low.shape[1]
+    local = tokens.shape[0]
+    wide = -(-3 * width // PLANES // LANES) * LANES
+    mine = jax.ShapeDtypeStruct((rows, width), single)
     return pl.pallas_call(
         last_scatter_kernel,
         out_shape=(
-            jax.ShapeDtypeStruct((rows, width), single),
+            mine,
+            mine,
+            jax.ShapeDtypeStruct((local, width), single),
             jax.ShapeDtypeStruct((BLOCKS, cols), single),
-            jax.ShapeDtypeStruct((1, spot), single),
+            jax.ShapeDtypeStruct((NOTE_ROWS, LANES), single),
             jax.ShapeDtypeStruct((BLOCKS, 1, 2 * LANES), single),
         ),
-        in_specs=[IN_VMEM, IN_VMEM, IN_HBM, IN_VMEM],
-        out_specs=(IN_VMEM,) * 4,
+        in_specs=[IN_HBM] + [IN_VMEM] * 6 + [IN_HBM] + [IN_VMEM] * 5,
+        out_specs=(IN_VMEM,) * 6,
         scratch_shapes=scatter_scratch(rows, width)
+        + scatter_scratch(rows, width)
+        + [pltpu.VMEM(cube, bfloat)] * 2
         + [
-            pltpu.VMEM(notes.shape, single),
+            pltpu.VMEM((2, width, wide), bfloat),
+            pltpu.VMEM((local, wide), bfloat),
+            pltpu.VMEM((NOTE_ROWS, width), single),
+            pltpu.VMEM((1, 6 * width), single),
+            pltpu.VMEM((count, NOTE_ROWS, LANES), single),
+            pltpu.VMEM((PLANES, 1, cols), single),
+            pltpu.VMEM((count, NOTE_ROWS, LANES), single),
+            pltpu.VMEM((count, 1, cols), single),
             pltpu.VMEM((BLOCKS, 1, 2 * LANES), single),
             pltpu.VMEM((count, 1, 2 * LANES), single),
+            pltpu.SemaphoreType.DMA((2,)),
         ]
-        + [pltpu.SemaphoreType.DMA((count,))] * 4
-        + [pltpu.SemaphoreType.DMA((len(PAIR_SUM_PARTS) * SCATTER_SEMS,))] * 2,
+        + [pltpu.SemaphoreType.DMA((count,))] * 6
+        + [pltpu.SemaphoreType.DMA((2 * len(SHARES) * SCATTER_SEMS,))] * 2,
         compiler_params=pltpu.CompilerParams(
-            collective_id=4, has_side_effects=True, vmem_limit_bytes=VMEM_LIMIT
+            collective_id=4, has_side_effects=True, vmem_limit_bytes=63 * 1024 * 1024
         ),
-        cost_estimate=cost(0, 64 * rows * width),
+        cost_estimate=cost(14 * local * width * width, 200 * rows * width),
         name="last_scatter",
-    )(notes, ada_low, far.reshape(cube), near.reshape(cube))
+    )(
+        up_far.reshape(cube),
+        up_near.reshape(cube),
+        first_in,
+        branch,
+        query_grad,
+        kv_grad,
+        dr_planes,
+        weight,
+        tokens,
+        middle_grad,
+        mods,
+        row_grads,
+        ada_low,
+    )
 
 
 def whole(shape):
@@ -976,55 +1236,53 @@
     )(lengths, query, head_row, kv)
 
 
-def out_kernel(
-    ob_ref, w_ref, bias_ref, x_ref, gate_ref, shift_ref, scale_ref, r_ref, mid_ref, a_ref
-):
+def out_kernel(ob_ref, w_ref, bias_ref, x_ref, c_ref, keep_ref, mod_ref, r_ref, mid_ref, a_ref, df_ref):
     step = pl.program_id(0)
     width = x_ref.shape[1]
-    steps = pl.num_programs(0)
-    cols = width // 4
+    cols = width // PLANES
     part = dot_nn(ob_ref[...], w_ref[0])[:, -cols:]
-    for index in range(4):
+    for index in range(PLANES):
 
         @pl.when(step == index)
         def _():
             r_ref[:, index * cols : (index + 1) * cols] = part
 
-    @pl.when(step == steps - 1)
+    @pl.when(step == PLANES - 1)
     def _():
         result = r_ref[...] + bias_ref[...]
         r_ref[...] = result
-        middle = x_ref[...].astype(single) + gate_ref[...] * result
+        middle = x_ref[...].astype(single) + mod_ref[2:3, :] * result
         mid_ref[...] = middle
-        a_ref[...] = modulate(middle, shift_ref[...], scale_ref[...]).astype(bfloat)
-
-
-def project_out(branch, weight, bias_row, tokens, gate_row, shift_row, scale_row):
+        a_ref[...] = modulate(middle, mod_ref[3:4, :], mod_ref[4:5, :]).astype(bfloat)
+        df_ref[...] = (mod_ref[5:6, :] * keep_ref[...] * c_ref[...].astype(single)).astype(bfloat)
+
+
+def project_out(branch, weight, bias_row, tokens, upstream, keep, mods):
     rows, width = tokens.shape
-    planes = weight.shape[0]
-    row = whole((1, width))
+    row, square = whole((1, width)), whole((rows, width))
     return pl.pallas_call(
         out_kernel,
-        grid=(planes,),
+        grid=(PLANES,),
         out_shape=(
             jax.ShapeDtypeStruct((rows, width), single),
             jax.ShapeDtypeStruct((rows, width), single),
             jax.ShapeDtypeStruct((rows, width), bfloat),
+            jax.ShapeDtypeStruct((rows, width), bfloat),
         ),
         in_specs=[
-            whole((rows, width)),
+            square,
             pl.BlockSpec((1, width, 3 * LANES), lambda s: (s, 0, 2)),
             row,
-            whole((rows, width)),
-            row,
-            row,
-            row,
+            square,
+            square,
+            whole((rows, 1)),
+            whole(mods.shape),
         ],
-        out_specs=(whole((rows, width)),) * 3,
+        out_specs=(square,) * 4,
         compiler_params=params("arbitrary"),
-        cost_estimate=cost(2 * rows * width * width, 2 * width * width + 12 * rows * width),
+        cost_estimate=cost(2 * rows * width * width, 2 * width * width + 16 * rows * width),
         name="project_out",
-    )(branch, weight, bias_row, tokens, gate_row, shift_row, scale_row)
+    )(branch, weight, bias_row, tokens, upstream, keep, mods)
 
 
 def out_copies(source, layout, plane, buffer, seq_bits, far_ref, near_ref, sem):
@@ -1163,21 +1421,68 @@
     return result
 
 
-def back_out_kernel(heads, dr_ref, w_ref, hm_ref, ob_ref, do_ref, delta_ref, acc):
+def back_out_kernel(
+    heads,
+    f_ref,
+    da_ref,
+    mid_ref,
+    r_ref,
+    c_ref,
+    keep_ref,
+    mod_ref,
+    bias_ref,
+    df_ref,
+    w_ref,
+    hm_ref,
+    ob_ref,
+    out_ref,
+    dmid_ref,
+    dr_ref,
+    row_ref,
+    do_ref,
+    delta_ref,
+    acc,
+):
     step = pl.program_id(0)
-    part = dot_nt(dr_ref[0], w_ref[0])
+    width = acc.shape[1]
+    cols = width // PLANES
+    edge = dr_ref.shape[2] - cols
 
     @pl.when(step == 0)
     def _():
-        acc[...] = part
-
-    @pl.when(step > 0)
+        row_ref[...] = jnp.zeros_like(row_ref)
+        acc[...] = jnp.zeros_like(acc)
+        gate_one, scale, gate_two = mod_ref[2:3, :], mod_ref[4:5, :], mod_ref[5:6, :]
+
+        @pl.loop(0, acc.shape[0], step=LANES)
+        def _(tile):
+            span = pl.ds(pl.multiple_of(tile, LANES), LANES)
+            keep = keep_ref[span, :]
+            upstream = c_ref[span, :].astype(single)
+            middle = mid_ref[span, :]
+            mlp = f_ref[span, :] + bias_ref[...]
+            out_ref[span, :] = (middle + gate_two * keep * mlp).astype(bfloat)
+            grad = da_ref[span, :]
+            back, normed = norm_back(middle, grad, scale)
+            dmid = upstream + back
+            dmid_ref[span, :] = dmid
+            branch = (gate_one * dmid).astype(bfloat).astype(single)
+            for plane in range(PLANES):
+                dr_ref[plane, span, :edge] = jnp.zeros((LANES, edge), bfloat)
+                dr_ref[plane, span, edge:] = branch[:, plane * cols : (plane + 1) * cols].astype(
+                    bfloat
+                )
+            row_ref[0:1, :] += column_sum(dmid * r_ref[span, :])
+            row_ref[1:2, :] += column_sum(grad)
+            row_ref[2:3, :] += column_sum(grad * normed)
+            row_ref[3:4, :] += column_sum(keep * upstream * mlp)
+            row_ref[4:5, :] += column_sum(branch)
+            row_ref[5:6, :] += column_sum(df_ref[span, :].astype(single))
+
+    acc[...] += dot_nt(dr_ref[step], w_ref[0])
+
+    @pl.when(step == PLANES - 1)
     def _():
-        acc[...] += part
-
-    @pl.when(step == pl.num_programs(0) - 1)
-    def _():
-        width = acc.shape[1]
         size = width // heads
         grad = (acc[...] * hm_ref[...]).astype(bfloat)
         do_ref[...] = grad
@@ -1194,28 +1499,74 @@
         )
 
 
-def back_out(dr_planes, weight, head_row, branch, heads):
+def back_out(
+    mlp_sum,
+    second_grad,
+    middle,
+    attn_out,
+    upstream,
+    keep,
+    mods,
+    bias_row,
+    mlp_grad,
+    weight,
+    head_row,
+    branch,
+    heads,
+):
     rows, width = branch.shape
-    planes = weight.shape[0]
+    row, square = whole((1, width)), whole((rows, width))
     return pl.pallas_call(
         functools.partial(back_out_kernel, heads),
-        grid=(planes,),
+        grid=(PLANES,),
         out_shape=(
+            jax.ShapeDtypeStruct((rows, width), bfloat),
+            jax.ShapeDtypeStruct((rows, width), single),
+            jax.ShapeDtypeStruct((PLANES, rows, 3 * LANES), bfloat),
+            jax.ShapeDtypeStruct((8, width), single),
             jax.ShapeDtypeStruct((rows, width), bfloat),
             jax.ShapeDtypeStruct((heads, rows), single),
         ),
         in_specs=[
-            pl.BlockSpec((1, rows, 3 * LANES), lambda s: (s, 0, 0)),
+            square,
+            square,
+            square,
+            square,
+            square,
+            whole((rows, 1)),
+            whole(mods.shape),
+            row,
+            square,
             pl.BlockSpec((1, width, 3 * LANES), lambda s: (s, 0, 2)),
-            whole((1, width)),
-            whole((rows, width)),
+            row,
+            square,
         ],
-        out_specs=(whole((rows, width)), whole((heads, rows))),
+        out_specs=(
+            square,
+            square,
+            whole((PLANES, rows, 3 * LANES)),
+            whole((8, width)),
+            square,
+            whole((heads, rows)),
+        ),
         scratch_shapes=[pltpu.VMEM((rows, width), single)],
         compiler_params=params("arbitrary"),
-        cost_estimate=cost(2 * rows * width * width, 2 * width * width),
+        cost_estimate=cost(2 * rows * width * width, 2 * width * width + 30 * rows * width),
         name="back_out",
-    )(dr_planes, weight, head_row, branch)
+    )(
+        mlp_sum,
+        second_grad,
+        middle,
+        attn_out,
+        upstream,
+        keep,
+        mods,
+        bias_row,
+        mlp_grad,
+        weight,
+        head_row,
+        branch,
+    )
 
 
 def attend_back_kernel(
@@ -1398,15 +1749,31 @@
     up_block = up_master.astype(bfloat)
     ada_low = ada_master.astype(bfloat)
     if cube_path():
-        count = bias_master.shape[0]
-        spots = (LANES * 2, LANES * 4)
-        slices = jnp.pad(condition.reshape(buckets, block_rows), ((0, 0), (0, spots[0] - block_rows)))
-        told = jnp.broadcast_to(
-            jnp.pad(bias_master, (0, spots[1] - count)), (buckets * seqs, spots[1])
-        )
-        notes = jnp.concatenate([jnp.repeat(slices, seqs, axis=0), told], axis=1)[:, None, :]
-        pair_weight, inbox, silu_rows, mod_row = first_gather(notes, ada_low, pair_block)
-        bias_low = inbox[:, 0, spots[0] : spots[0] + count].astype(bfloat).reshape(-1)
+        each = width // (buckets * seqs)
+        table = bias_master.reshape(each, table_cols).T
+        slices = jnp.pad(
+            condition.reshape(buckets, block_rows), ((0, 0), (0, 2 * LANES - block_rows))
+        )
+        notes = jnp.concatenate(
+            [
+                jnp.broadcast_to(
+                    jnp.pad(table, ((0, 0), (0, LANES - each))), (buckets, table_cols, LANES)
+                ),
+                slices.reshape(buckets, 2, LANES),
+            ],
+            axis=1,
+        )
+        (
+            pair_weight,
+            up_weight,
+            down_weight,
+            near,
+            silu_rows,
+            mods,
+            bias_table,
+            first_in,
+            query,
+        ) = gather(notes, ada_low, pair_block, up_block, down_block, tokens)
     else:
         pair_weight = gather_all(pair_block, "planes")
         bias_low = lax.all_gather(
@@ -1419,123 +1786,108 @@
             dot_nn(silu_rows, ada_low), "bucket", scatter_dimension=0, tiled=True
         )
         mod_row = lax.all_gather(mod_part, "seq", axis=1, tiled=True)
-
-    bias_table = bias_low.astype(single).reshape(width, table_cols).T
-    modulation = mod_row.reshape(6, 1, width) + bias_table[:6, None, :]
-    shift_one, scale_one, gate_one, shift_two, scale_two, gate_two = modulation
-    value_bias = bias_table[7:8]
-    qkv_bias = jnp.concatenate([bias_table[6:7], jnp.zeros_like(value_bias), value_bias], axis=1)
+        bias_table = bias_low.astype(single).reshape(width, table_cols).T
+        mods = jnp.pad(mod_row.reshape(6, width) + bias_table[:6], ((0, 2), (0, 0)))
+        value_bias = bias_table[7:8]
+        qkv_bias = jnp.concatenate(
+            [bias_table[6:7], jnp.zeros_like(value_bias), value_bias], axis=1
+        )
+        first_in, query, key_value = project_qkv(
+            tokens, mods[0:1], mods[1:2], qkv_bias, pair_weight
+        )
+        up_weight = gather_all(up_block, "planes")
+        down_weight = gather_all(down_block, "rows")
+        near = lax.all_gather(key_value, "seq", axis=0, tiled=True)
+
     out_bias = bias_table[8:9]
     up_bias = bias_table[9 : table_cols - 1].T.reshape(1, hidden_width)
-    down_bias = bias_table[table_cols - 1 :]
+    down_bias = bias_table[table_cols - 1 : table_cols]
     selector = (
         jnp.arange(head_table.shape[0], dtype=jnp.int32)[:, None] == bucket_ids[None, :]
     ).astype(single)
     head_row = jnp.repeat(jnp.sum(selector * head_table.astype(single), axis=0), head_size)[None]
     chan_row = jnp.sum(selector * chan_table.astype(single), axis=0)[None]
     keep_float = keep_flags.astype(single)[:, None]
-    upstream = cotangent.astype(single)
-    mlp_grad = (gate_two * keep_float * upstream).astype(bfloat)
-
-    first_in, query, key_value = project_qkv(tokens, shift_one, scale_one, qkv_bias, pair_weight)
-    if cube_path():
-        up_weight, down_weight, near = second_gather(up_block, down_block, key_value)
-    else:
-        up_weight = gather_all(up_block, "planes")
-        down_weight = gather_all(down_block, "rows")
-        near = lax.all_gather(key_value, "seq", axis=0, tiled=True)
     branch_in, logs = attend(lengths, query, near, head_row, heads)
-    attn_out, middle, second_in = project_out(
-        branch_in, pair_weight, out_bias, tokens, gate_one, shift_two, scale_two
+    attn_out, middle, second_in, mlp_grad = project_out(
+        branch_in, pair_weight, out_bias, tokens, cotangent, keep_float, mods
     )
     mlp_sum, second_grad, up_far, up_near, down_far, down_near, up_bias_grad = feed_forward(
         second_in, mlp_grad, chan_row, up_bias, up_weight, down_weight
     )
-    mlp_out = mlp_sum + down_bias
-    output = (middle + gate_two * keep_float * mlp_out).astype(bfloat)
-    gate_two_grad = jnp.sum(keep_float * upstream * mlp_out, axis=0)
-    down_bias_grad = jnp.sum(mlp_grad, axis=0, dtype=single)
-    _, norm_two_back = jax.vjp(modulate, middle, shift_two[0], scale_two[0])
-    middle_norm_grad, shift_two_grad, scale_two_grad = norm_two_back(second_grad)
-    middle_grad = upstream + middle_norm_grad
-    branch_grad = (gate_one * middle_grad).astype(bfloat)
-    gate_one_grad = jnp.sum(middle_grad * attn_out, axis=0)
-    out_bias_grad = jnp.sum(branch_grad, axis=0, dtype=single)
-    out_cols = width // seqs
-    dr_planes = jnp.pad(
-        branch_grad.reshape(local_rows, seqs, out_cols).transpose(1, 0, 2),
-        ((0, 0), (0, 0), (3 * LANES - out_cols, 0)),
-    )
-    attended_grad, delta = back_out(dr_planes, pair_weight, head_row, branch_in, heads)
+    output, middle_grad, dr_planes, row_grads, attended_grad, delta = back_out(
+        mlp_sum,
+        second_grad,
+        middle,
+        attn_out,
+        cotangent,
+        keep_float,
+        mods,
+        down_bias,
+        mlp_grad,
+        pair_weight,
+        head_row,
+        branch_in,
+        heads,
+    )
+    up_bias_rows = up_bias_grad.reshape(width, hidden_ratio).T
     query_grad, kv_far, kv_near = attend_back(
         lengths, query, attended_grad, logs, delta, near, heads
     )
+    qkv_cols = 3 * width // seqs
     if cube_path():
-        kv_grad, up_new_grad, down_new_grad = first_scatter(
-            kv_far, kv_near, up_far, up_near, down_far, down_near
-        )
+        kv_grad, down_new_grad = first_scatter(kv_far, kv_near, down_far, down_near)
+        rows_all = jnp.concatenate([row_grads[:5], up_bias_rows, row_grads[5:6]])
+        rows_all = jnp.pad(rows_all, ((0, 16 - rows_all.shape[0]), (0, 0)))
+        up_new_grad, pair_new_grad, token_grad, mod_all, bias_sum, silu_sum = last_scatter(
+            up_far,
+            up_near,
+            first_in,
+            branch_in,
+            query_grad,
+            kv_grad,
+            dr_planes,
+            pair_weight,
+            tokens,
+            middle_grad,
+            mods,
+            rows_all,
+            ada_low,
+        )
+        bias_new_grad = bias_sum[:table_cols, : width // (buckets * seqs)].T.reshape(-1)
+        silu_grad = silu_sum[:, 0, :block_rows].reshape(1, width)
     else:
         terms = jnp.stack([kv_near[0], kv_far[0], kv_near[1], kv_far[1]])
         kv_grad = lax.psum_scatter(terms, "seq", scatter_dimension=0)
+        projected_grad = jnp.concatenate([query_grad, kv_grad], axis=1)
+        dy_planes = jnp.pad(
+            projected_grad.reshape(local_rows, seqs, qkv_cols).transpose(1, 0, 2),
+            ((0, 0), (0, 0), (0, -qkv_cols % LANES)),
+        )
+        first_grad, pair_far, pair_near = back_qkv(
+            first_in, branch_in, dy_planes, dr_planes, pair_weight
+        )
+        back, normed = norm_back(tokens.astype(single), first_grad, mods[1:2])
+        token_grad = middle_grad + back
         up_new_grad = natural_sum(up_far, up_near, "planes")
         down_new_grad = natural_sum(down_far, down_near, "rows")
-    projected_grad = jnp.concatenate([query_grad, kv_grad], axis=1)
-    qkv_cols = 3 * width // seqs
-    dy_planes = jnp.pad(
-        projected_grad.reshape(local_rows, seqs, qkv_cols).transpose(1, 0, 2),
-        ((0, 0), (0, 0), (0, -qkv_cols % LANES)),
-    )
-    first_grad, pair_far, pair_near = back_qkv(
-        first_in, branch_in, dy_planes, dr_planes, pair_weight
-    )
-    query_bias_grad = jnp.sum(projected_grad[:, :width], axis=0, dtype=single)
-    value_bias_grad = jnp.sum(projected_grad[:, 2 * width :], axis=0, dtype=single)
-    inputs_float = tokens.astype(single)
-    _, norm_one_back = jax.vjp(modulate, inputs_float, shift_one[0], scale_one[0])
-    input_norm_grad, shift_one_grad, scale_one_grad = norm_one_back(first_grad)
-    token_grad = middle_grad + input_norm_grad
-    mod_grads = jnp.stack(
-        [
-            shift_one_grad,
-            scale_one_grad,
-            gate_one_grad,
-            shift_two_grad,
-            scale_two_grad,
-            gate_two_grad,
-        ]
-    )
-    bias_grad = jnp.concatenate(
-        [
-            mod_grads.T,
-            query_bias_grad[:, None],
-            value_bias_grad[:, None],
-            out_bias_grad[:, None],
-            up_bias_grad.reshape(width, hidden_ratio),
-            down_bias_grad[:, None],
-        ],
-        axis=1,
-    ).reshape(width * table_cols)
-    mod_parts = mod_grads.reshape(seqs, 6 * width // seqs)
-    if cube_path():
-        count = bias_master.shape[0]
-        spot = -(-count // LANES) * LANES
-        notes = jnp.concatenate(
+        pair_new_grad = natural_sum(pair_far, pair_near, "planes")
+        mod_grads = jnp.concatenate(
+            [column_sum(first_grad), column_sum(first_grad * normed), row_grads[:4]]
+        )
+        bias_grad = jnp.concatenate(
             [
-                bias_grad.reshape(buckets * seqs, count),
-                jnp.zeros((buckets * seqs, spot - count), single),
-                jnp.tile(mod_parts, (buckets, 1)),
-            ],
-            axis=1,
-        )
-        notes = jnp.pad(notes, ((0, 0), (0, -notes.shape[1] % LANES)))[:, None, :]
-        pair_new_grad, mod_all, bias_sum, silu_sum = last_scatter(
-            notes, ada_low, pair_far, pair_near, spot
-        )
-        bias_new_grad = bias_sum[0, :count]
-        silu_grad = silu_sum[:, 0, :block_rows].reshape(1, width)
-    else:
-        pair_new_grad = natural_sum(pair_far, pair_near, "planes")
-        mod_mine = lax.psum_scatter(mod_parts, "seq", scatter_dimension=0, tiled=True)
+                mod_grads,
+                column_sum(query_grad.astype(single)),
+                column_sum(kv_grad[:, width:].astype(single)),
+                row_grads[4:5],
+                up_bias_rows,
+                row_grads[5:6],
+            ]
+        ).T.reshape(width * table_cols)
+        mod_mine = lax.psum_scatter(
+            mod_grads.reshape(seqs, 6 * width // seqs), "seq", scatter_dimension=0, tiled=True
+        )
         mod_all = lax.all_gather(mod_mine, "bucket", axis=0, tiled=True)
         silu_part = lax.dot_general(
             mod_all,

time: 674 us -> 585 us (0.87)
  Pallas kernels: 551 us -> 507 us
  other arithmetic: 48.3 us -> 21.7 us
  local copies, waits for them, and re-layouts: 51.5 us -> 35.2 us
    pallas_call x1, Pallas kernels: 133 us -> 80.3 us  [first_scatter(): pl.pallas_call(first_scatter_kernel, out_shape=(jax.ShapeDtypeStruct((loc...]
    reduce_sum x12 -> x0, other arithmetic: 22.6 us -> none  [the longest x1 5.16 us: on_device(): gate_two_grad = jnp.sum(keep_float * upstream * mlp_out, axis=0)]
    pallas_call x7 -> x4, Pallas kernels: 316 us -> 324 us  [the longest x1 176 us: gather(): pl.pallas_call(gather_kernel, out_shape=(blocks, blocks, blocks, jax.Shap...]
    concatenate x5 -> x0, local copies, waits for them, and re-layouts: 6.83 us -> none  [the longest x1 5.75 us: on_device(): projected_grad = jnp.concatenate([query_grad, kv_grad], axis=1)]
    unnamed x140 -> x78, local copies, waits for them, and re-layouts: 15 us -> 18.9 us
  transfers between devices with their start and end apart: 2 -> 2, of which waited for: 0 -> 0; matrix products, arithmetic and copies ran while one was open for 5% -> 6% of each run, Pallas kernels for 12% -> 21%
where the time goes in v2:
time: 585 us; the launch traced here: 577 us
  Pallas kernels  507 us (87%)
  local copies, waits for them, and re-layouts  35.2 us (6%)
  other arithmetic  21.7 us (4%)
  starting transfers between devices  8.48 us (1%)
    pallas_call x1, Pallas kernels, gather(): pl.pallas_call(gather_kernel, out_shape=(blocks, blocks, blocks, jax.Shap...  176 us
    pallas_call x1, Pallas kernels, last_scatter(): pl.pallas_call(last_scatter_kernel, out_shape=(mine, mine, jax.ShapeDtype...  119 us
    pallas_call x1, Pallas kernels, first_scatter(): pl.pallas_call(first_scatter_kernel, out_shape=(jax.ShapeDtypeStruct((loc...  80.3 us
    pallas_call x1, Pallas kernels, feed_forward(): pl.pallas_call(ffn_kernel, out_shape=(jax.ShapeDtypeStruct((rows, width),...  49.5 us
    pallas_call x1, Pallas kernels, attend_back(): pl.pallas_call(functools.partial(attend_back_kernel, heads), out_shape=(j...  33.2 us
    pallas_call x1, Pallas kernels, attend(): pl.pallas_call(functools.partial(attend_kernel, heads), out_shape=(jax.Sh...  19.6 us
    unnamed x78, local copies, waits for them, and re-layouts  18.9 us
    pallas_call x1, Pallas kernels, back_out(): pl.pallas_call(functools.partial(back_out_kernel, heads), grid=(PLANES,),...  17.4 us
  transfers between devices with their start and end apart: 2, of which 0 were waited for; matrix products, arithmetic and copies ran while one was open for 6% of the time, Pallas kernels for 21%

profile of v2, /device:TPU:0, one launch (start us, length us, event | category | flops | bytes accessed | tf_op | source)
XLA Modules:
  0.0 577.5 jit_solution(13920485304300205464)
XLA Ops:
  0.7 1.5 copy.63
  3.0 4.4 all-to-all-start
  13.8 1.7 multiply_reduce_fusion
  19.5 1.4 reshape_broadcast_in_dim.3.cm_ref
  20.8 1.3 copy.70
  22.2 2.3 copy.72
  27.8 176.0 %gather.1 = (bf16[2,2,2,2,2,144,1152]{6,5,4,3,2,1,0:T(8,128)(2,1)}, bf16[2,2,2,2,2,144,1152]{6,5,4,3,2,1,0:T(8,128)(2,1)}, bf16[2,2,2,2,2,144,1152]{6,5,4,3,2,1,...) custom-call(f32[8,16,128]{2,1,0:T(8,128)} %pad_maximum_fusion.1.note, ...), custom_call_target="tpu_custom_call" | custom-call | flops 4076863488 | bytes 33177600 | tf_op jit(solution)/shard_map/gather/pallas_call | solution.py:509
  203.9 1.4 fusion.16
  207.4 19.6 %attend.1 = (bf16[512,1152]{1,0:T(8,128)(2,1)}, f32[16,512]{1,0:T(8,128)}) custom-call(s32[1,8]{1,0:T(1,128)} %len_ref.3, bf16[512,1152]{1,0:T(8,128)(2,1)} %get-tuple-element.66.q_ref, f32[1,1152]{1,0:T(1,128)} %broadcast_in_dim_reshape.3.hm_ref, bf16[2048,2304]{1,0:T(8,128)(2,1)} %bitcast.41), custom_call_target="tpu_custom_call" | custom-call | flops 9663676416 | bytes 23592960 | tf_op jit(solution)/shard_map/attend/pallas_call | solution.py:1223
  227.0 11.2 %project_out.1 = (f32[512,1152]{1,0:T(8,128)}, f32[512,1152]{1,0:T(8,128)}, bf16[512,1152]{1,0:T(8,128)(2,1)}, bf16[512,1152]{1,0:T(8,128)(2,1)}) custom-call(bf16[512,1152]{1,0:T(8,128)(2,1)} %get-tuple-element.68.ob_ref, bf16[4,1152,1152]{2,1,0:T(8,128)(2,1)} %bitcast.28, f32[1,1152]{1,0:T(1,128)} %get-tuple-element.157.bias_ref, bf16[512,1152]{1,0:T(8,128)(2,1)} %x_ref.5, ...), custom_call_target="tpu_custom_call" | custom-call | flops 1358954496 | bytes 12091392 | tf_op jit(solution)/shard_map/project_out/pallas_call | solution.py:1263
  238.2 49.5 %feed_forward.1 = (f32[512,1152]{1,0:T(8,128)}, f32[512,1152]{1,0:T(8,128)}, bf16[16,144,1152]{2,1,0:T(8,128)(2,1)}, bf16[16,144,1152]{2,1,0:T(8,128)(2,1)}, bf1...) custom-call(bf16[512,1152]{1,0:T(8,128)(2,1)} %get-tuple-element.72.a_ref, ...), custom_call_target="tpu_custom_call" | custom-call | flops 32614907904 | bytes 42467328 | tf_op jit(solution)/shard_map/feed_forward/pallas_call | solution.py:1387
  287.7 17.4 %back_out.1 = (bf16[512,1152]{1,0:T(8,128)(2,1)}, f32[512,1152]{1,0:T(8,128)}, bf16[4,512,384]{2,1,0:T(8,128)(2,1)}, f32[8,1152]{1,0:T(8,128)}, bf16[512,1152]{1,0:T(8,128)(2,1)}, /*index=5*/f32[16,512]{1,0:T(8,128)}) custom-call(f32[512,1152]{1,0:T(8,128)} %get-tuple-element.76.f_ref, f32[512,1152]{1,0:T(8,128)} %get-tuple-element.77.da_ref, ...), custom_call_target="tpu_custom_call" | custom-call | flops 1358954496 | bytes 20348928 | tf_op jit(solution)/shard_map/back_out/pallas_call | solution.py:1519
  306.8 33.2 %attend_back.1 = (bf16[512,1152]{1,0:T(8,128)(2,1)}, bf16[2,512,2304]{2,1,0:T(8,128)(2,1)}, bf16[2,512,2304]{2,1,0:T(8,128)(2,1)}) custom-call(s32[1,8]{1,0:T(1,128)} %len_ref.3, bf16[512,1152]{1,0:T(8,128)(2,1)} %get-tuple-element.66.q_ref, bf16[512,1152]{1,0:T(8,128)(2,1)} %get-tuple-element.84.do_ref, f32[16,512]{1,0:T(8,128)} %get-tuple-element.85.log_ref, ...), custom_call_target="tpu_custom_call" | custom-call | flops 24159191040 | bytes 47185920 | tf_op jit(solution)/shard_map/attend_back/pallas_call | solution.py:1626
  340.0 80.3 %first_scatter.1 = (bf16[512,2304]{1,0:T(8,128)(2,1)}, f32[144,1152]{1,0:T(8,128)}) custom-call(bf16[2,512,2304]{2,1,0:T(8,128)(2,1)} %get-tuple-element.88.kv_far, bf16[2,512,2304]{2,1,0:T(8,128)(2,1)} %get-tuple-element.89.kv_near, bf16[2,2,2,2,144,1152]{5,4,3,2,1,0:T(8,128)(2,1)} %bitcast.31, bf16[2,2,2,2,144,1152]{5,4,3,2,1,0:T(8,128)(2,1)} %bitcast.32), custom_call_target="tpu_custom_call" | custom-call | bytes 21233664 | tf_op jit(solution)/shard_map/first_scatter/pallas_call | solution.py:745
  422.7 4.1 all-to-all-start.1
  427.5 119.3 %last_scatter.1 = (f32[144,1152]{1,0:T(8,128)}, f32[144,1152]{1,0:T(8,128)}, f32[512,1152]{1,0:T(8,128)}, f32[8,1728]{1,0:T(8,128)}, f32[16,128]{1,0:T(8,128)}, /*index=5*/f32[8,1,256]{2,1,0:T(1,128)}) custom-call(bf16[2,2,2,2,144,1152]{5,4,3,2,1,0:T(8,128)(2,1)} %bitcast.43, bf16[2,2,2,2,144,1152]{5,4,3,2,1,0:T(8,128)(2,1)} %bitcast.44, ...), custom_call_target="tpu_custom_call" | custom-call | flops 9512681472 | bytes 33177600 | tf_op jit(solution)/shard_map/last_scatter/pallas_call | solution.py:1050
  548.4 3.4 multiply_add_fusion.7
  551.8 2.1 multiply_add_fusion.9
  554.0 2.0 multiply_add_fusion.6
  557.1 3.4 multiply_add_fusion.2
  563.4 3.3 multiply_add_fusion.4
  566.7 2.5 copy.77
  569.1 2.3 copy.78
  573.8 3.2 copy.84
  (114 shorter events, 28.4 us)
Async XLA Ops:
  0.7 6.7 %copy-start.29 = (f32[504]{0:T(512)S(1)}, f32[504]{0:T(512)}, u32[]{:S(2)}) copy-start(f32[504]{0:T(512)} %param.60) | copy-start | bytes 6052
  0.7 15.5 %copy-start = (f32[144,1728]{1,0:T(8,128)S(1)}, f32[144,1728]{1,0:T(8,128)}, u32[]{:S(2)}) copy-start(f32[144,1728]{1,0:T(8,128)} %param.40) | copy-start | bytes 2985988
  2.2 14.8 %copy-start.9 = (f32[144,864]{1,0:T(8,128)S(1)}, f32[144,864]{1,0:T(8,128)}, u32[]{:S(2)}) copy-start(f32[144,864]{1,0:T(8,128)} %param.44) | copy-start | bytes 1492996
  3.0 14.1 %copy-start.7 = (f32[144,1152]{1,0:T(8,128)S(1)}, f32[144,1152]{1,0:T(8,128)}, u32[]{:S(2)}) copy-start(f32[144,1152]{1,0:T(8,128)} %param.52) | copy-start | bytes 1990660
  3.0 23.6 %all-to-all-start = ((bf16[4,144,288]{2,1,0:T(8,128)(2,1)}), bf16[4,144,288]{2,1,0:T(8,128)(2,1)S(1)}, u32[]{:S(2)}, u32[]{:S(2)}) async-start(bf16[4,144,288]{2,1,0:T(8,128)(2,1)} %bitcast.34), calls=%async_computation | async-start | bytes 884736 | tf_op jit(solution)/shard_map/all_to_all | solution.py:1746
  17.9 6.7 %copy-start.16 = (f32[576,288]{0,1:T(8,128)S(1)}, f32[576,288]{0,1:T(8,128)}, u32[]{:S(2)}) copy-start(f32[576,288]{0,1:T(8,128)} %param.59) | copy-start | bytes 1990660
  287.7 18.2 %copy-start.27 = (f32[4,1,1152]{2,1,0:T(1,128)S(1)}, f32[4,1,1152]{2,1,0:T(1,128)}, u32[]{:S(2)}) copy-start(f32[4,1,1152]{2,1,0:T(1,128)} %get-tuple-element.96) | copy-start | bytes 55300
  420.3 6.5 %copy-start.25 = (f32[8,1152]{1,0:T(8,128)S(1)}, f32[8,1152]{1,0:T(8,128)}, u32[]{:S(2)}) copy-start(f32[8,1152]{1,0:T(8,128)} %get-tuple-element.95) | copy-start | bytes 110596
  422.7 140.7 %all-to-all-start.1 = ((bf16[144,4,288]{2,0,1:T(8,128)(2,1)}), bf16[144,4,288]{2,0,1:T(8,128)(2,1)}, u32[]{:S(2)}, u32[]{:S(2)}) async-start(bf16[144,4,288]{2,0,1:T(8,128)(2,1)} %copy.71), calls=%async_computation.1 | async-start | bytes 884736 | tf_op jit(solution)/shard_map/all_to_all | solution.py:1914
  427.5 120.3 %copy-start.26 = (f32[1,1152]{1,0:T(1,128)S(1)}, f32[1,1152]{1,0:T(1,128)}, u32[]{:S(2)}) copy-start(f32[1,1152]{1,0:T(1,128)} %param.33) | copy-start | bytes 13828
  546.8 5.0 copy-start.14
  546.8 5.0 copy-start.21
  546.8 5.0 copy-start.22
  546.8 5.0 copy-start.23
  548.3 5.6 copy-start.8
  548.4 5.6 copy-start.17
  548.4 5.6 copy-start.18
  548.4 5.6 copy-start.19
  548.4 5.6 copy-start.20
  557.1 5.0 copy-start.32
  557.1 6.3 %copy-start.2 = (f32[576,288]{1,0:T(8,128)S(1)}, f32[576,288]{1,0:T(8,128)}, u32[]{:S(2)}) copy-start(f32[576,288]{1,0:T(8,128)} %copy.70) | copy-start | bytes 1990660
  557.1 6.3 %copy-start.3 = (f32[576,288]{1,0:T(8,128)S(1)}, f32[576,288]{1,0:T(8,128)}, u32[]{:S(2)}) copy-start(f32[576,288]{1,0:T(8,128)} %copy.72) | copy-start | bytes 1990660
  557.1 6.3 %copy-start.4 = (f32[576,288]{1,0:T(8,128)S(1)}, f32[576,288]{1,0:T(8,128)}, u32[]{:S(2)}) copy-start(f32[576,288]{1,0:T(8,128)} %copy.75) | copy-start | bytes 1990660
  566.7 6.0 %copy-start.5 = (f32[576,288]{1,0:T(8,128)S(1)}, f32[576,288]{1,0:T(8,128)}, u32[]{:S(2)}) copy-start(f32[576,288]{1,0:T(8,128)} %get-tuple-element.136) | copy-start | bytes 1990660
  (12 other events, 40.9 us)

commit v3 on v2

--- a/solution.py
+++ b/solution.py
@@ -82,6 +82,7 @@
 
 IN_VMEM = pl.BlockSpec(memory_space=pltpu.VMEM)
 IN_HBM = pl.BlockSpec(memory_space=pl.ANY)
+IN_SMEM = pl.BlockSpec(memory_space=pltpu.SMEM)
 
 
 def cube_path():
@@ -90,6 +91,7 @@
 
 BLOCKS, PLANES = 8, 4
 X, Z0, Z1, CORE, Y = ("bucket", 1), ("bucket", 2), ("bucket", 4), ("seq", 1), ("seq", 2)
+MIDDLE, FORWARD = ("bucket", 6), ("bucket", 2, "forward")
 
 
 def gather_all(block, layout):
@@ -120,7 +122,7 @@
 
 def partner(bit):
     bucket, seq = lax.axis_index("bucket"), lax.axis_index("seq")
-    axis, amount = bit
+    axis, amount = bit[:2]
     return (bucket ^ amount, seq) if axis == "bucket" else (bucket, seq ^ amount)
 
 
@@ -141,6 +143,7 @@
         self.own, self.out, self.dims, self.order = own, out, DIMS[layout], order
         self.first, self.rows, self.send, self.recv, self.base = first, rows, send, recv, base
         self.me = my_coords()
+        self.inner = self.me[Z0] != self.me[Z1]
 
     def view(self, free, flipped=None):
         index = tuple(
@@ -161,89 +164,124 @@
             device_id_type=MESH,
         )
 
+    def dim(self, phase):
+        return Z1 if self.order[phase] in (MIDDLE, FORWARD) else self.order[phase]
+
+    def had(self, phase):
+        return [self.dim(past) for past in range(phase) if self.order[past] != MIDDLE]
+
+    def arrived(self, phase):
+        return self.view(self.had(phase), self.dim(phase))
+
     def hop(self, phase):
-        place = self.view(self.order[:phase])
+        place = self.arrived(phase) if self.order[phase] == FORWARD else self.view(self.had(phase))
         source = self.own if phase == 0 else place
         return self.copy(source, place, phase, self.order[phase])
 
     def across(self, phase):
         if phase == 0:
-            return self.copy(self.own, self.view(()), 4, CORE)
-        place = self.view(self.order[: phase - 1], self.order[phase - 1])
-        return self.copy(place, place, 4 + phase, CORE)
+            return self.copy(self.own, self.view(()), 5, CORE)
+        place = self.arrived(phase - 1)
+        return self.copy(place, place, 5 + phase, CORE)
 
     def keep(self):
-        return pltpu.make_async_copy(self.own, self.view(()), self.send.at[self.base + 9])
+        return pltpu.make_async_copy(self.own, self.view(()), self.send.at[self.base + 11])
 
     def begin(self):
         self.hop(0).start()
         self.across(0).start()
         self.keep().start()
 
+    def sends(self, phase, act):
+        if self.order[phase] in (MIDDLE, FORWARD):
+            pl.when(self.inner)(act)
+        else:
+            act()
+
     def advance(self, phase):
         if phase == 0:
             self.keep().wait()
-        self.hop(phase).wait_recv()
-        if phase < 3:
-            self.hop(phase + 1).start()
+        kind = self.order[phase]
+        if kind == MIDDLE:
+
+            @pl.when(self.inner)
+            def _():
+                self.hop(phase).wait_recv()
+                self.hop(phase + 1).start()
+
+            return
+        if kind == FORWARD:
+
+            @pl.when(jnp.logical_not(self.inner))
+            def _():
+                self.hop(phase).wait_recv()
+
+        else:
+            self.hop(phase).wait_recv()
+        if phase < 4:
+            self.sends(phase + 1, lambda: self.hop(phase + 1).start())
         self.across(phase + 1).start()
 
     def collect(self):
+        for phase in range(6):
+            if phase == 0 or self.order[phase - 1] != MIDDLE:
+                self.across(phase).wait_recv()
+
+    def finish(self):
         for phase in range(5):
-            self.across(phase).wait_recv()
-
-    def finish(self):
-        for phase in range(4):
-            self.hop(phase).wait_send()
-        for phase in range(5):
-            self.across(phase).wait_send()
-
-
-GATHER_SEMS = 10
+            self.sends(phase, lambda phase=phase: self.hop(phase).wait_send())
+        for phase in range(6):
+            if phase == 0 or self.order[phase - 1] != MIDDLE:
+                self.across(phase).wait_send()
+
+
+GATHER_SEMS = 12
 SHARES = (32, 32, 32, 32, 16)
 PAIR_PARTS = (
-    (Z1, Z0, Y, X),
-    (Z1, Y, X, Z0),
-    (Z1, Z0, X, Y),
-    (Z0, Z1, Y, X),
-    (Z0, Z1, X, Y),
+    (X, Z0, Y, MIDDLE, FORWARD),
+    (Z0, MIDDLE, FORWARD, X, Y),
+    (Z0, Y, MIDDLE, FORWARD, X),
+    (Z0, MIDDLE, FORWARD, Y, X),
+    (Z0, MIDDLE, FORWARD, Y, X),
 )
 UP_PARTS = (
-    (Z1, Y, Z0, X),
-    (Z1, Y, Z0, X),
-    (Z1, X, Y, Z0),
-    (Z1, Y, Z0, X),
-    (Z1, Y, Z0, X),
+    (Z0, X, Y, MIDDLE, FORWARD),
+    (Z0, X, Y, MIDDLE, FORWARD),
+    (Y, Z0, MIDDLE, FORWARD, X),
+    (Y, Z0, MIDDLE, FORWARD, X),
+    (Z0, X, MIDDLE, FORWARD, Y),
 )
 DOWN_PARTS = (
-    (Z1, Y, X, Z0),
-    (Z1, Y, X, Z0),
-    (Z1, Z0, X, Y),
-    (Z1, Y, Z0, X),
-    (X, Z1, Y, Z0),
+    (Z0, MIDDLE, FORWARD, Y, X),
+    (Z0, Y, X, MIDDLE, FORWARD),
+    (Z0, MIDDLE, FORWARD, Y, X),
+    (Z0, X, Y, MIDDLE, FORWARD),
+    (Z0, MIDDLE, FORWARD, X, Y),
 )
 BEGIN, PLANE, KV = -1, -2, -3
 GATHER_STEPS = (
-    (0, 0), (1, 0), (2, 0), (3, 0), (4, 0), (1, 1), (0, 1), (2, 1), (1, 2), (3, 1),
-    (0, 2), (4, 1), (-1, 0), (2, 2), (3, 2), (1, 3), (0, 3), (5, 0), (4, 2), (14, 0),
-    (6, 0), (2, 3), (7, 0), (5, 1), (8, 0), (9, 0), (4, 3), (10, 0), (3, 3), (-2, 0),
-    (6, 1), (11, 0), (7, 1), (8, 1), (-2, 1), (12, 0), (9, 1), (13, 0), (10, 1), (-2, 2),
-    (14, 1), (11, 1), (-2, 3), (-3, 0), (-3, 1), (-3, 2), (-3, 3), (5, 2), (7, 2), (10, 2),
-    (13, 1), (6, 2), (14, 2), (11, 2), (8, 2), (12, 1), (9, 2), (5, 3), (7, 3), (6, 3),
-    (10, 3), (8, 3), (13, 2), (12, 2), (14, 3), (9, 3), (11, 3), (12, 3), (13, 3),
+    (0, 0), (1, 0), (2, 0), (3, 0), (4, 0), (1, 1), (0, 1), (2, 1), (3, 1), (4, 1),
+    (-1, 0), (1, 2), (3, 2), (0, 2), (2, 2), (4, 2), (7, 0), (5, 0), (8, 0), (6, 0),
+    (9, 0), (1, 3), (10, 0), (11, 0), (5, 1), (3, 3), (12, 0), (13, 0), (14, 0), (6, 1),
+    (4, 3), (9, 1), (0, 3), (2, 3), (10, 1), (7, 1), (12, 1), (14, 1), (8, 1), (1, 4),
+    (3, 4), (9, 2), (11, 1), (13, 1), (7, 2), (5, 2), (4, 4), (0, 4), (8, 2), (10, 2),
+    (6, 2), (12, 2), (14, 2), (13, 2), (9, 3), (2, 4), (-2, 0), (5, 3), (10, 3), (7, 3),
+    (11, 2), (-2, 1), (14, 3), (12, 3), (-2, 2), (8, 3), (-2, 3), (-3, 0), (-3, 1), (-3, 2),
+    (-3, 3), (6, 3), (9, 4), (10, 4), (14, 4), (5, 4), (13, 3), (7, 4), (6, 4), (11, 3),
+    (12, 4), (13, 4), (8, 4), (11, 4),
 )
 NOTE = -4
 DOWN_SUM_PARTS = (
     (X, Z0, Y, Z1),
-    (Z0, X, Z1, Y),
-    (X, Z0, Y, Z1),
+    (X, Y, Z0, Z1),
     (Z0, X, Y, Z1),
-    (X, Z0, Y, Z1),
+    (Z0, X, Y, Z1),
+    (X, Z0, Z1, Y),
 )
 FIRST_SUM_STEPS = (
     (-3, 0), (-3, 1), (-3, 2), (-3, 3), (0, -1), (1, -1), (2, -1), (3, -1), (4, -1), (0, 0),
-    (1, 0), (2, 0), (3, 0), (4, 0), (0, 1), (1, 1), (2, 1), (4, 1), (3, 1), (0, 2),
-    (2, 2), (1, 2), (4, 2), (0, 3), (3, 2), (1, 3), (2, 3), (4, 3), (3, 3),
+    (2, 0), (1, 0), (3, 0), (4, 0), (0, 1), (1, 1), (2, 1), (4, 1), (0, 2), (1, 2),
+    (3, 1), (2, 2), (4, 2), (0, 3), (3, 2), (4, 3), (1, 3), (2, 3), (3, 3),
 )
 UP_SUM_PARTS = (
     (Z0, X, Z1, Y),
@@ -281,12 +319,41 @@
     return moving
 
 
+def kv_needed(piece, act):
+    place = my_coords()
+    quarter = KV_PIECES // 2
+    last = jnp.logical_and(place[Y] == 1, place[CORE] == 1)
+    first = jnp.logical_and(place[Y] == 0, place[CORE] == 0)
+    skipped = first if piece < quarter else last
+    pl.when(jnp.logical_not(skipped))(act)
+
+
+def kv_expected(piece, act):
+    place = my_coords()
+    quarter = KV_PIECES // 2
+    last = jnp.logical_and(place[Y] == 0, place[CORE] == 1)
+    first = jnp.logical_and(place[Y] == 1, place[CORE] == 0)
+    skipped = first if piece < quarter else last
+    pl.when(jnp.logical_not(skipped))(act)
+
+
+def kv_relayed(piece, act):
+    place = my_coords()
+    quarter = KV_PIECES // 2
+    last = jnp.logical_and(place[Y] == 0, place[CORE] == 0)
+    first = jnp.logical_and(place[Y] == 1, place[CORE] == 1)
+    skipped = first if piece < quarter else last
+    pl.when(jnp.logical_not(skipped))(act)
+
+
 def gather_kernel(
-    note_ref,
+    cond_ref,
+    table_ref,
     ada_ref,
-    pair_ref,
-    up_ref,
-    down_ref,
+    qkv_master,
+    out_master,
+    up_master,
+    cut_ref,
     x_ref,
     pair_out,
     up_out,
@@ -297,6 +364,11 @@
     bias_ref,
     a_ref,
     q_ref,
+    note_ref,
+    pair_ref,
+    up_ref,
+    down_ref,
+    cuts,
     inbox,
     parts,
     returns,
@@ -308,6 +380,8 @@
     note_recv,
     mod_send,
     mod_recv,
+    cut_send,
+    cut_recv,
     weight_sem,
     send,
     recv,
@@ -322,7 +396,30 @@
     def _(distance):
         pl.semaphore_signal(barrier, inc=1, device_id=peer_at(distance), device_id_type=MESH)
 
+    rows, width = ada_ref.shape[0], x_ref.shape[1]
+    cols = 3 * width // PLANES
+    pair_ref[:, :cols] = qkv_master[...].astype(bfloat)
+    pair_ref[:, cols:] = out_master[...].astype(bfloat)
+    up_ref[...] = up_master[...].astype(bfloat)
+    note_ref[...] = jnp.zeros_like(note_ref)
+    for index in range(BLOCKS):
+        start = index * rows
+        note_ref[index, : NOTE_ROWS - 2, : table_ref.shape[1]] = table_ref[...]
+        note_ref[index, NOTE_ROWS - 2 : NOTE_ROWS - 1, :] = cond_ref[:, start : start + LANES]
+        note_ref[index, NOTE_ROWS - 1 :, : rows - LANES] = cond_ref[
+            :, start + LANES : start + rows
+        ]
     pl.semaphore_wait(barrier, count - 1)
+
+    def cut(distance):
+        return pltpu.make_async_remote_copy(
+            src_ref=cut_ref.at[seq ^ distance],
+            dst_ref=cuts.at[seq],
+            send_sem=cut_send.at[distance],
+            recv_sem=cut_recv.at[distance],
+            device_id=(bucket, seq ^ distance),
+            device_id_type=MESH,
+        )
 
     def note(distance):
         peer = peer_at(distance)
@@ -351,6 +448,7 @@
         note(distance).start()
 
     inbox[me] = note_ref[bucket]
+    cuts[seq] = cut_ref[seq]
     base = len(PAIR_PARTS) * GATHER_SEMS
     pairs = split_gatherings(pair_ref, pair_out, "planes", SHARES, PAIR_PARTS, send, recv, 0)
     rest = split_gatherings(up_ref, up_out, "planes", SHARES, UP_PARTS, send, recv, base)
@@ -360,9 +458,9 @@
     moving = pairs + rest
     for part in pairs:
         part.begin()
-
-    rows, width = ada_ref.shape[0], x_ref.shape[1]
-    cols = 3 * width // PLANES
+    for distance in range(1, PLANES):
+        cut(distance).start()
+
     local = x_ref.shape[0] // KV_PIECES
 
     def kv_copy(source, target, slot, bit):
@@ -405,8 +503,8 @@
         head, tail = jax.nn.silu(head).astype(bfloat), jax.nn.silu(tail).astype(bfloat)
         silu_ref[:, :LANES] = head
         silu_ref[:, LANES:] = tail
-        mods = dot_nn(head, ada_ref[:LANES, :]) + dot_nn(
-            tail[:, : rows - LANES], ada_ref[LANES:, :]
+        mods = dot_nn(head, ada_ref[:LANES, :].astype(bfloat)) + dot_nn(
+            tail[:, : rows - LANES], ada_ref[LANES:, :].astype(bfloat)
         )
         for group in range(BLOCKS):
             parts[group] = mods[group : group + 1, :]
@@ -466,28 +564,41 @@
             modulations()
             biases()
         if part == BEGIN:
+            for distance in range(1, PLANES):
+                cut(distance).wait_recv()
+            for index in range(PLANES):
+                each = cuts.shape[2]
+                down_ref[:, index * each : (index + 1) * each] = cuts[index]
             for moved in rest:
                 moved.begin()
         elif part == PLANE:
             projection(phase)
         elif part == KV:
-            for kind in ("over", "near", "keep"):
+            kv_needed(phase, lambda: kv_step(phase, "over").start())
+            for kind in ("near", "keep"):
                 kv_step(phase, kind).start()
         else:
             moving[part].advance(phase)
-    for piece in range(KV_PIECES):
+    def relay(piece):
         kv_step(piece, "over").wait_recv()
         kv_step(piece, "far").start()
+
+    for piece in range(KV_PIECES):
+        kv_expected(piece, functools.partial(relay, piece))
     for part in rest:
         part.collect()
     for part in moving:
         part.finish()
     for piece in range(KV_PIECES):
         kv_step(piece, "near").wait_recv()
-        kv_step(piece, "far").wait_recv()
+        kv_relayed(piece, lambda piece=piece: kv_step(piece, "far").wait_recv())
         kv_step(piece, "keep").wait()
-        for kind in ("over", "near", "far"):
-            kv_step(piece, kind).wait_send()
+        kv_step(piece, "near").wait_send()
+        kv_needed(piece, lambda piece=piece: kv_step(piece, "over").wait_send())
+        kv_expected(piece, lambda piece=piece: kv_step(piece, "far").wait_send())
+
+    for distance in range(1, PLANES):
+        cut(distance).wait_send()
 
     @pl.loop(1, count)
     def _(distance):
@@ -498,11 +609,12 @@
 NOTE_ROWS = 16
 
 
-def gather(notes, ada_low, pair_block, up_block, down_block, tokens):
-    rows, width = pair_block.shape
+def gather(condition, table, ada_master, qkv_master, out_master, up_master, cut, tokens):
+    rows, width = up_master.shape
     local = tokens.shape[0]
     count = BLOCKS * PLANES
-    cols = ada_low.shape[1]
+    cols = ada_master.shape[1]
+    block = pltpu.VMEM((rows, width), bfloat)
     wide = -(-3 * width // PLANES // LANES) * LANES
     blocks = jax.ShapeDtypeStruct((2, 2, 2, 2, 2, rows, width), bfloat)
     sems = 3 * len(SHARES) * GATHER_SEMS + 4 * KV_PIECES
@@ -519,9 +631,14 @@
             jax.ShapeDtypeStruct((local, width), bfloat),
             jax.ShapeDtypeStruct((local, width), bfloat),
         ),
-        in_specs=[IN_VMEM] * 6,
+        in_specs=[IN_VMEM] * 8,
         out_specs=(IN_HBM,) * 4 + (IN_VMEM,) * 5,
         scratch_shapes=[
+            pltpu.VMEM((BLOCKS, NOTE_ROWS, LANES), single),
+            block,
+            block,
+            block,
+            pltpu.VMEM(cut.shape, bfloat),
             pltpu.VMEM((count, NOTE_ROWS, LANES), single),
             pltpu.VMEM((BLOCKS, 1, cols), single),
             pltpu.VMEM((count, 1, cols), single),
@@ -531,6 +648,7 @@
             pltpu.VMEM((local, 2 * width), bfloat),
         ]
         + [pltpu.SemaphoreType.DMA((count,))] * 4
+        + [pltpu.SemaphoreType.DMA((PLANES,))] * 2
         + [pltpu.SemaphoreType.DMA((2,))]
         + [pltpu.SemaphoreType.DMA((sems,))] * 2,
         compiler_params=pltpu.CompilerParams(
@@ -538,7 +656,7 @@
         ),
         cost_estimate=cost(6 * local * width * width, 200 * rows * width),
         name="gather",
-    )(notes, ada_low, pair_block, up_block, down_block, tokens)
+    )(condition, table, ada_master, qkv_master, out_master, up_master, cut, tokens)
     tall = BLOCKS * rows
     return (
         pair.reshape(PLANES, tall, width),
@@ -712,6 +830,17 @@
             kv_total[side, rows, :].astype(single) + kv_near[side, rows, :].astype(single)
         ).astype(bfloat)
 
+    def pass_over(piece):
+        kv_add(piece, 1)
+        over(piece).start()
+
+    def take(piece):
+        over(piece).wait_recv()
+        rows = pl.ds(piece * count, count)
+        kv_total[0, rows, :] = (
+            kv_total[0, rows, :].astype(single) + kv_arrival[rows, :].astype(single)
+        ).astype(bfloat)
+
     for piece in range(KV_PIECES):
         near(piece).start()
     for part in moving:
@@ -719,22 +848,18 @@
     for part, phase in FIRST_SUM_STEPS:
         if part == KV:
             near(phase).wait_recv()
-            kv_add(phase, 1)
-            over(phase).start()
+            kv_expected(phase, functools.partial(pass_over, phase))
             kv_add(phase, 0)
         else:
             moving[part].advance(phase)
     for piece in range(KV_PIECES):
-        over(piece).wait_recv()
-        rows = pl.ds(piece * count, count)
-        kv_out[rows, :] = (
-            kv_total[0, rows, :].astype(single) + kv_arrival[rows, :].astype(single)
-        ).astype(bfloat)
+        kv_needed(piece, functools.partial(take, piece))
+    kv_out[...] = kv_total[0]
     for part in moving:
         part.finish()
     for piece in range(KV_PIECES):
         near(piece).wait_send()
-        over(piece).wait_send()
+        kv_expected(piece, lambda piece=piece: over(piece).wait_send())
 
 
 def first_scatter(kv_far, kv_near, down_far, down_near):
@@ -788,15 +913,18 @@
     mod_ref,
     row_ref,
     ada_ref,
+    down_ref,
     up_out,
     pair_out,
     grad_ref,
     mods_ref,
     bias_ref,
     silu_ref,
+    cuts,
     *refs,
 ):
     up_scratch, pair_scratch, refs = refs[:5], refs[5:10], refs[10:]
+    cut_send, cut_recv, cut_ref, refs = refs[0], refs[1], refs[2], refs[3:]
     far, near, weights, dy, table, line, bias_notes, mod_notes, bias_box, mod_box = refs[:10]
     parts, returns, weight_sem = refs[10:13]
     bias_send, bias_recv, mod_send, mod_recv, back_send, back_recv, send, recv = refs[13:]
@@ -844,6 +972,23 @@
     moving = ups + pairs
     for part in ups:
         part.across().start()
+
+    def cut(distance):
+        return pltpu.make_async_remote_copy(
+            src_ref=cut_ref.at[seq ^ distance],
+            dst_ref=cuts.at[seq],
+            send_sem=cut_send.at[distance],
+            recv_sem=cut_recv.at[distance],
+            device_id=(bucket, seq ^ distance),
+            device_id_type=MESH,
+        )
+
+    for index in range(PLANES):
+        each = cuts.shape[2]
+        cut_ref[index] = down_ref[:, index * each : (index + 1) * each].astype(bfloat)
+    cuts[seq] = cut_ref[seq]
+    for distance in range(1, PLANES):
+        cut(distance).start()
 
     width = x_ref.shape[1]
     rows = up_out.shape[0]
@@ -966,7 +1111,7 @@
         mods_ref[...] = mods
         silu = lax.dot_general(
             mods,
-            ada_ref[...].astype(single),
+            ada_ref[...].astype(bfloat).astype(single),
             (((1,), (1,)), ((), ())),
             preferred_element_type=single,
             precision=HIGHEST,
@@ -1014,6 +1159,9 @@
         silu_ref[group] = sum(returns[PLANES * group + s] for s in range(PLANES))
     for part in moving:
         part.finish()
+    for distance in range(1, PLANES):
+        cut(distance).wait_recv()
+        cut(distance).wait_send()
 
     @pl.loop(1, count)
     def _(distance):
@@ -1038,12 +1186,14 @@
     middle_grad,
     mods,
     row_grads,
-    ada_low,
+    ada_master,
+    down_grad,
 ):
     rows, width = up_far.shape[1:]
     cube = (2, 2, 2, 2, rows, width)
     count = BLOCKS * PLANES
-    cols = ada_low.shape[1]
+    cols = ada_master.shape[1]
+    cuts = (PLANES, rows, width // PLANES)
     local = tokens.shape[0]
     wide = -(-3 * width // PLANES // LANES) * LANES
     mine = jax.ShapeDtypeStruct((rows, width), single)
@@ -1056,11 +1206,14 @@
             jax.ShapeDtypeStruct((BLOCKS, cols), single),
             jax.ShapeDtypeStruct((NOTE_ROWS, LANES), single),
             jax.ShapeDtypeStruct((BLOCKS, 1, 2 * LANES), single),
+            jax.ShapeDtypeStruct(cuts, bfloat),
         ),
-        in_specs=[IN_HBM] + [IN_VMEM] * 6 + [IN_HBM] + [IN_VMEM] * 5,
-        out_specs=(IN_VMEM,) * 6,
+        in_specs=[IN_HBM] + [IN_VMEM] * 6 + [IN_HBM] + [IN_VMEM] * 6,
+        out_specs=(IN_VMEM,) * 7,
         scratch_shapes=scatter_scratch(rows, width)
         + scatter_scratch(rows, width)
+        + [pltpu.SemaphoreType.DMA((PLANES,))] * 2
+        + [pltpu.VMEM(cuts, bfloat)]
         + [pltpu.VMEM(cube, bfloat)] * 2
         + [
             pltpu.VMEM((2, width, wide), bfloat),
@@ -1095,7 +1248,8 @@
         middle_grad,
         mods,
         row_grads,
-        ada_low,
+        ada_master,
+        down_grad,
     )
 
 
@@ -1177,7 +1331,18 @@
 LONG, SHORT = 1024, 256
 
 
-def attend_kernel(heads, len_ref, q_ref, hm_ref, kv, ob_ref, log_ref, out):
+def head_row(table_ref, bucket_ref, width):
+    heads = table_ref.shape[1]
+    size = width // heads
+    lane = lax.broadcasted_iota(jnp.int32, (1, width), 1)
+    row = jnp.zeros((1, width), jnp.int32)
+    for head in range(heads):
+        inside = jnp.logical_and(lane >= head * size, lane < (head + 1) * size)
+        row = jnp.where(inside, table_ref[bucket_ref[0], head], row)
+    return row.astype(single)
+
+
+def attend_kernel(heads, len_ref, table_ref, bucket_ref, q_ref, kv, ob_ref, log_ref, out):
     rows, width = q_ref.shape
     size = width // heads
     my_seq = lax.axis_index("seq")
@@ -1214,10 +1379,10 @@
         def _():
             run(tile_start, start, SHORT)
 
-    ob_ref[...] = (out[...] * hm_ref[...]).astype(bfloat)
-
-
-def attend(lengths, query, kv, head_row, heads):
+    ob_ref[...] = (out[...] * head_row(table_ref, bucket_ref, width)).astype(bfloat)
+
+
+def attend(lengths, head_table, bucket_ids, query, kv, heads):
     rows, width = query.shape
     group = kv.shape[0]
     return pl.pallas_call(
@@ -1226,14 +1391,13 @@
             jax.ShapeDtypeStruct((rows, width), bfloat),
             jax.ShapeDtypeStruct((heads, rows), single),
         ),
-        in_specs=[pl.BlockSpec(memory_space=pltpu.SMEM)]
-        + [IN_VMEM] * 3,
+        in_specs=[IN_SMEM] * 3 + [IN_VMEM] * 2,
         out_specs=(IN_VMEM,) * 2,
         scratch_shapes=[pltpu.VMEM((rows, width), single)],
         compiler_params=params(),
         cost_estimate=cost(16 * rows * LONG * width, 10 * group * width, heads * rows * LONG),
         name="attend",
-    )(lengths, query, head_row, kv)
+    )(lengths, head_table, bucket_ids, query, kv)
 
 
 def out_kernel(ob_ref, w_ref, bias_ref, x_ref, c_ref, keep_ref, mod_ref, r_ref, mid_ref, a_ref, df_ref):
@@ -1312,7 +1476,7 @@
     return seq_bits[1]
 
 
-def ffn_kernel(a_ref, df_ref, cm_ref, b_ref, up_ref, down_ref, *refs):
+def ffn_kernel(bucket_ref, a_ref, df_ref, cm_ref, b_ref, up_ref, down_ref, *refs):
     f_ref, da_ref, up_far, up_near, down_far, down_near, db_ref = refs[:7]
     up, down, up_grad, down_grad, up_sem, down_sem, up_out, down_out = refs[7:]
     width = a_ref.shape[1]
@@ -1335,7 +1499,7 @@
     def one(plane, low, high, buffer):
         first, grad = a_ref[...], df_ref[...]
         hidden_rows = pl.ds(pl.multiple_of(plane * width + low, LANES), high - low)
-        keep = cm_ref[plane, :, low:high]
+        keep = cm_ref[pl.ds(bucket_ref[0], 1), hidden_rows].astype(single)
         pre = dot_nn(first, up[plane, :, low:high]) + b_ref[plane, :, low:high]
         root = math.sqrt(2.0 / math.pi)
         square = pre * pre
@@ -1380,9 +1544,9 @@
             copy.wait()
 
 
-def feed_forward(first, grad, chan_row, bias_row, up_weight, down_weight):
+def feed_forward(bucket_ids, first, grad, chan_table, bias_row, up_weight, down_weight):
     rows, width = first.shape
-    hidden = chan_row.shape[1]
+    hidden = chan_table.shape[1]
     blocks = jax.ShapeDtypeStruct((BLOCKS * PLANES // 2, width // BLOCKS, width), bfloat)
     result = pl.pallas_call(
         ffn_kernel,
@@ -1395,7 +1559,7 @@
             blocks,
             jax.ShapeDtypeStruct((PLANES, 1, width), single),
         ),
-        in_specs=[IN_VMEM] * 4 + [IN_HBM] * 2,
+        in_specs=[IN_SMEM] + [IN_VMEM] * 4 + [IN_HBM] * 2,
         out_specs=(IN_VMEM, IN_VMEM) + (IN_HBM,) * 4 + (IN_VMEM,),
         scratch_shapes=[
             pltpu.VMEM((PLANES, width, width), bfloat),
@@ -1411,9 +1575,10 @@
         cost_estimate=cost(12 * rows * width * hidden, 8 * width * hidden, rows * hidden),
         name="feed_forward",
     )(
+        bucket_ids,
         first,
         grad,
-        chan_row.reshape(PLANES, 1, width),
+        chan_table,
         bias_row.reshape(PLANES, 1, width),
         up_weight,
         down_weight,
@@ -1433,7 +1598,8 @@
     bias_ref,
     df_ref,
     w_ref,
-    hm_ref,
+    table_ref,
+    bucket_ref,
     ob_ref,
     out_ref,
     dmid_ref,
@@ -1484,7 +1650,7 @@
     @pl.when(step == PLANES - 1)
     def _():
         size = width // heads
-        grad = (acc[...] * hm_ref[...]).astype(bfloat)
+        grad = (acc[...] * head_row(table_ref, bucket_ref, width)).astype(bfloat)
         do_ref[...] = grad
         terms = grad.astype(single) * ob_ref[...].astype(single)
         head = lax.broadcasted_iota(jnp.int32, (heads, width), 0)
@@ -1510,7 +1676,8 @@
     bias_row,
     mlp_grad,
     weight,
-    head_row,
+    head_table,
+    bucket_ids,
     branch,
     heads,
 ):
@@ -1538,7 +1705,8 @@
             row,
             square,
             pl.BlockSpec((1, width, 3 * LANES), lambda s: (s, 0, 2)),
-            row,
+            IN_SMEM,
+            IN_SMEM,
             square,
         ],
         out_specs=(
@@ -1564,7 +1732,8 @@
         bias_row,
         mlp_grad,
         weight,
-        head_row,
+        head_table,
+        bucket_ids,
         branch,
     )
 
@@ -1742,27 +1911,9 @@
     buckets, seqs = lax.axis_size("bucket"), lax.axis_size("seq")
     group_rows = local_rows * seqs
     block_rows = qkv_master.shape[0]
-    pair_block = jnp.concatenate([qkv_master, out_master], axis=1).astype(bfloat)
-    down_block = lax.all_to_all(
-        down_master.astype(bfloat), "seq", split_axis=0, concat_axis=1, tiled=True
-    )
-    up_block = up_master.astype(bfloat)
-    ada_low = ada_master.astype(bfloat)
     if cube_path():
-        each = width // (buckets * seqs)
-        table = bias_master.reshape(each, table_cols).T
-        slices = jnp.pad(
-            condition.reshape(buckets, block_rows), ((0, 0), (0, 2 * LANES - block_rows))
-        )
-        notes = jnp.concatenate(
-            [
-                jnp.broadcast_to(
-                    jnp.pad(table, ((0, 0), (0, LANES - each))), (buckets, table_cols, LANES)
-                ),
-                slices.reshape(buckets, 2, LANES),
-            ],
-            axis=1,
-        )
+        table = bias_master.reshape(-1, table_cols).T
+        cut = down_master.astype(bfloat).reshape(seqs, -1, down_master.shape[1])
         (
             pair_weight,
             up_weight,
@@ -1773,8 +1924,16 @@
             bias_table,
             first_in,
             query,
-        ) = gather(notes, ada_low, pair_block, up_block, down_block, tokens)
+        ) = gather(
+            condition, table, ada_master, qkv_master, out_master, up_master, cut, tokens
+        )
     else:
+        pair_block = jnp.concatenate([qkv_master, out_master], axis=1).astype(bfloat)
+        down_block = lax.all_to_all(
+            down_master.astype(bfloat), "seq", split_axis=0, concat_axis=1, tiled=True
+        )
+        up_block = up_master.astype(bfloat)
+        ada_low = ada_master.astype(bfloat)
         pair_weight = gather_all(pair_block, "planes")
         bias_low = lax.all_gather(
             bias_master.astype(bfloat), ("bucket", "seq"), axis=0, tiled=True
@@ -1802,18 +1961,13 @@
     out_bias = bias_table[8:9]
     up_bias = bias_table[9 : table_cols - 1].T.reshape(1, hidden_width)
     down_bias = bias_table[table_cols - 1 : table_cols]
-    selector = (
-        jnp.arange(head_table.shape[0], dtype=jnp.int32)[:, None] == bucket_ids[None, :]
-    ).astype(single)
-    head_row = jnp.repeat(jnp.sum(selector * head_table.astype(single), axis=0), head_size)[None]
-    chan_row = jnp.sum(selector * chan_table.astype(single), axis=0)[None]
     keep_float = keep_flags.astype(single)[:, None]
-    branch_in, logs = attend(lengths, query, near, head_row, heads)
+    branch_in, logs = attend(lengths, head_table, bucket_ids, query, near, heads)
     attn_out, middle, second_in, mlp_grad = project_out(
         branch_in, pair_weight, out_bias, tokens, cotangent, keep_float, mods
     )
     mlp_sum, second_grad, up_far, up_near, down_far, down_near, up_bias_grad = feed_forward(
-        second_in, mlp_grad, chan_row, up_bias, up_weight, down_weight
+        bucket_ids, second_in, mlp_grad, chan_table, up_bias, up_weight, down_weight
     )
     output, middle_grad, dr_planes, row_grads, attended_grad, delta = back_out(
         mlp_sum,
@@ -1826,7 +1980,8 @@
         down_bias,
         mlp_grad,
         pair_weight,
-        head_row,
+        head_table,
+        bucket_ids,
         branch_in,
         heads,
     )
@@ -1839,7 +1994,15 @@
         kv_grad, down_new_grad = first_scatter(kv_far, kv_near, down_far, down_near)
         rows_all = jnp.concatenate([row_grads[:5], up_bias_rows, row_grads[5:6]])
         rows_all = jnp.pad(rows_all, ((0, 16 - rows_all.shape[0]), (0, 0)))
-        up_new_grad, pair_new_grad, token_grad, mod_all, bias_sum, silu_sum = last_scatter(
+        (
+            up_new_grad,
+            pair_new_grad,
+            token_grad,
+            mod_all,
+            bias_sum,
+            silu_sum,
+            down_cuts,
+        ) = last_scatter(
             up_far,
             up_near,
             first_in,
@@ -1852,8 +2015,10 @@
             middle_grad,
             mods,
             rows_all,
-            ada_low,
-        )
+            ada_master,
+            down_new_grad,
+        )
+        down_mine = down_cuts.reshape(down_master.shape)
         bias_new_grad = bias_sum[:table_cols, : width // (buckets * seqs)].T.reshape(-1)
         silu_grad = silu_sum[:, 0, :block_rows].reshape(1, width)
     else:
@@ -1902,6 +2067,9 @@
         bias_new_grad = lax.psum_scatter(
             bias_grad, ("bucket", "seq"), scatter_dimension=0, tiled=True
         )
+        down_mine = lax.all_to_all(
+            down_new_grad.astype(bfloat), "seq", split_axis=1, concat_axis=0, tiled=True
+        )
     ada_new_grad = lax.dot_general(
         silu_rows.astype(single),
         mod_all,
@@ -1911,9 +2079,6 @@
     )
     _, silu_back = jax.vjp(jax.nn.silu, condition)
     condition_grad = silu_back(silu_grad)[0]
-    down_mine = lax.all_to_all(
-        down_new_grad.astype(bfloat), "seq", split_axis=1, concat_axis=0, tiled=True
-    ).astype(single)
     out_rate = (group_rows / (16.0 * width)) ** 0.5
     ada_new = adam_update(
         ada_master, ada_first, ada_second, ada_average, ada_new_grad, width ** (-0.5), MATRIX_DECAY
@@ -1940,14 +2105,15 @@
         up_master, up_first, up_second, up_average, up_new_grad, width ** (-0.5), MATRIX_DECAY
     )
     down_new = adam_update(
-        down_master,
-        down_first,
-        down_second,
-        down_average,
-        down_mine,
+        down_master.T,
+        down_first.T,
+        down_second.T,
+        down_average.T,
+        down_mine.T.astype(single),
         hidden_width ** (-0.5),
         MATRIX_DECAY,
     )
+    down_new = [value.T for value in down_new]
     bias_new = adam_update(
         bias_master, bias_first, bias_second, bias_average, bias_new_grad, 0.3, 0.0
     )

time: 585 us -> 524 us (0.90)
  Pallas kernels: 507 us -> 482 us
  local copies, waits for them, and re-layouts: 35.2 us -> 12.5 us
  starting transfers between devices: 8.48 us -> 0 us
  other arithmetic: 21.7 us -> 14.5 us
    pallas_call x1, Pallas kernels: 176 us -> 158 us  [gather(): pl.pallas_call(gather_kernel, out_shape=(blocks, blocks, blocks, jax.Shap...]
    unnamed x78 -> x55, local copies, waits for them, and re-layouts: 18.9 us -> 2.88 us
    all_to_all x2 -> x0, starting transfers between devices: 8.48 us -> none  [the longest x1 4.37 us: on_device(): lax.all_to_all(down_master.astype(bfloat), 'seq', split_axis=0, concat_ax...]
    pallas_call x1, Pallas kernels: 33.2 us -> 27 us  [attend_back(): pl.pallas_call(functools.partial(attend_back_kernel, heads), out_shape=(j...]
  transfers between devices with their start and end apart: 2 -> 0, of which waited for: 0 -> 0; matrix products, arithmetic and copies ran while one was open for 6% -> 0% of each run, Pallas kernels for 21% -> 0%
where the time goes in v3:
time: 524 us; the launch traced here: 514 us
  Pallas kernels  482 us (92%)
  other arithmetic  14.5 us (3%)
  local copies, waits for them, and re-layouts  12.5 us (2%)
    pallas_call x1, Pallas kernels, gather(): pl.pallas_call(gather_kernel, out_shape=(blocks, blocks, blocks, jax.Shap...  158 us
    pallas_call x1, Pallas kernels, last_scatter(): pl.pallas_call(last_scatter_kernel, out_shape=(mine, mine, jax.ShapeDtype...  121 us
    pallas_call x1, Pallas kernels, first_scatter(): pl.pallas_call(first_scatter_kernel, out_shape=(jax.ShapeDtypeStruct((loc...  84.1 us
    pallas_call x1, Pallas kernels, feed_forward(): pl.pallas_call(ffn_kernel, out_shape=(jax.ShapeDtypeStruct((rows, width),...  49.5 us
    pallas_call x1, Pallas kernels, attend_back(): pl.pallas_call(functools.partial(attend_back_kernel, heads), out_shape=(j...  27 us
    pallas_call x1, Pallas kernels, back_out(): pl.pallas_call(functools.partial(back_out_kernel, heads), grid=(PLANES,),...  17.4 us
    pallas_call x1, Pallas kernels, attend(): pl.pallas_call(functools.partial(attend_kernel, heads), out_shape=(jax.Sh...  14.4 us
    pallas_call x1, Pallas kernels, project_out(): pl.pallas_call(out_kernel, grid=(PLANES,), out_shape=(jax.ShapeDtypeStruc...  10.7 us

profile of v3, /device:TPU:0, one launch (start us, length us, event | category | flops | bytes accessed | tf_op | source)
XLA Modules:
  0.0 514.5 jit_solution(15642726316573404883)
XLA Ops:
  2.0 0.8 reshape.93
  3.5 0.9 copy.66.keep_ref
  4.3 1.2 convert_element_type.19
  5.5 1.0 copy.65
  6.5 158.1 %gather.1 = (bf16[2,2,2,2,2,144,1152]{6,5,4,3,2,1,0:T(8,128)(2,1)}, bf16[2,2,2,2,2,144,1152]{6,5,4,3,2,1,0:T(8,128)(2,1)}, bf16[2,2,2,2,2,144,1152]{6,5,4,3,2,1,...) custom-call(f32[1,1152]{1,0:T(1,128)} %cond_ref.1, ...), custom_call_target="tpu_custom_call" | custom-call | flops 4076863488 | bytes 33177600 | tf_op jit(solution)/shard_map/gather/pallas_call | solution.py:621
  164.6 1.4 fusion.22
  166.0 0.8 slice_bitcast_fusion
  167.1 1.0 reshape_reshape.4.b_ref
  168.1 14.4 %attend.1 = (bf16[512,1152]{1,0:T(8,128)(2,1)}, f32[16,512]{1,0:T(8,128)}) custom-call(s32[1,8]{1,0:T(1,128)} %len_ref.3, s32[10,16]{1,0:T(8,128)} %table_ref.3, s32[1]{0:T(128)S(6)} %copy.76.bucket_ref, bf16[512,1152]{1,0:T(8,128)(2,1)} %get-tuple-element.67.q_ref, bf16[2048,2304]{1,0:T(8,128)(2,1)} %bitcast.33), custom_call_target="tpu_custom_call" | custom-call | flops 9663676416 | bytes 23592960 | tf_op jit(solution)/shard_map/attend/pallas_call | solution.py:1388
  182.5 10.7 %project_out.1 = (f32[512,1152]{1,0:T(8,128)}, f32[512,1152]{1,0:T(8,128)}, bf16[512,1152]{1,0:T(8,128)(2,1)}, bf16[512,1152]{1,0:T(8,128)(2,1)}) custom-call(bf16[512,1152]{1,0:T(8,128)(2,1)} %get-tuple-element.69.ob_ref, bf16[4,1152,1152]{2,1,0:T(8,128)(2,1)} %bitcast.21, f32[1,1152]{1,0:T(1,128)} %get-tuple-element.132.bias_ref, bf16[512,1152]{1,0:T(8,128)(2,1)} %x_ref.5, ...), custom_call_target="tpu_custom_call" | custom-call | flops 1358954496 | bytes 12091392 | tf_op jit(solution)/shard_map/project_out/pallas_call | solution.py:1427
  193.3 49.5 %feed_forward.1 = (f32[512,1152]{1,0:T(8,128)}, f32[512,1152]{1,0:T(8,128)}, bf16[16,144,1152]{2,1,0:T(8,128)(2,1)}, bf16[16,144,1152]{2,1,0:T(8,128)(2,1)}, bf1...) custom-call(s32[1]{0:T(128)S(6)} %copy.76.bucket_ref, ...), custom_call_target="tpu_custom_call" | custom-call | flops 32614907904 | bytes 42467328 | tf_op jit(solution)/shard_map/feed_forward/pallas_call | solution.py:1551
  242.8 17.4 %back_out.1 = (bf16[512,1152]{1,0:T(8,128)(2,1)}, f32[512,1152]{1,0:T(8,128)}, bf16[4,512,384]{2,1,0:T(8,128)(2,1)}, f32[8,1152]{1,0:T(8,128)}, bf16[512,1152]{1,0:T(8,128)(2,1)}, /*index=5*/f32[16,512]{1,0:T(8,128)}) custom-call(f32[512,1152]{1,0:T(8,128)} %get-tuple-element.77.f_ref, f32[512,1152]{1,0:T(8,128)} %get-tuple-element.78.da_ref, ...), custom_call_target="tpu_custom_call" | custom-call | flops 1358954496 | bytes 20348928 | tf_op jit(solution)/shard_map/back_out/pallas_call | solution.py:1686
  260.2 27.0 %attend_back.1 = (bf16[512,1152]{1,0:T(8,128)(2,1)}, bf16[2,512,2304]{2,1,0:T(8,128)(2,1)}, bf16[2,512,2304]{2,1,0:T(8,128)(2,1)}) custom-call(s32[1,8]{1,0:T(1,128)} %len_ref.3, bf16[512,1152]{1,0:T(8,128)(2,1)} %get-tuple-element.67.q_ref, bf16[512,1152]{1,0:T(8,128)(2,1)} %get-tuple-element.85.do_ref, f32[16,512]{1,0:T(8,128)} %get-tuple-element.86.log_ref, ...), custom_call_target="tpu_custom_call" | custom-call | flops 24159191040 | bytes 47185920 | tf_op jit(solution)/shard_map/attend_back/pallas_call | solution.py:1795
  287.3 84.1 %first_scatter.1 = (bf16[512,2304]{1,0:T(8,128)(2,1)}, f32[144,1152]{1,0:T(8,128)}) custom-call(bf16[2,512,2304]{2,1,0:T(8,128)(2,1)} %get-tuple-element.89.kv_far, bf16[2,512,2304]{2,1,0:T(8,128)(2,1)} %get-tuple-element.90.kv_near, bf16[2,2,2,2,144,1152]{5,4,3,2,1,0:T(8,128)(2,1)} %bitcast.24, bf16[2,2,2,2,144,1152]{5,4,3,2,1,0:T(8,128)(2,1)} %bitcast.25), custom_call_target="tpu_custom_call" | custom-call | bytes 21233664 | tf_op jit(solution)/shard_map/first_scatter/pallas_call | solution.py:870
  373.0 120.7 %last_scatter.1 = (f32[144,1152]{1,0:T(8,128)}, f32[144,1152]{1,0:T(8,128)}, f32[512,1152]{1,0:T(8,128)}, f32[8,1728]{1,0:T(8,128)}, f32[16,128]{1,0:T(8,128)}, ...) custom-call(bf16[2,2,2,2,144,1152]{5,4,3,2,1,0:T(8,128)(2,1)} %bitcast.35, bf16[2,2,2,2,144,1152]{5,4,3,2,1,0:T(8,128)(2,1)} %bitcast.36, ...), custom_call_target="tpu_custom_call" | custom-call | flops 9512681472 | bytes 33177600 | tf_op jit(solution)/shard_map/last_scatter/pallas_call | solution.py:1200
  493.7 0.8 slice_reduce_fusion
  496.7 1.2 bitcast_convert_fusion
  498.2 2.3 multiply_add_fusion.9
  500.6 3.0 multiply_add_fusion.7
  503.6 2.2 multiply_add_fusion.5
  506.2 2.0 multiply_add_fusion.6
  508.2 0.8 copy-done.4
  509.3 3.4 multiply_add_fusion.2
  512.6 1.4 copy.77
  (68 shorter events, 6.4 us)
Async XLA Ops:
  287.3 84.1 %copy-start.19 = (f32[8,1152]{1,0:T(8,128)S(1)}, f32[8,1152]{1,0:T(8,128)}, u32[]{:S(2)}) copy-start(f32[8,1152]{1,0:T(8,128)} %get-tuple-element.96) | copy-start | bytes 110596
  287.3 84.1 %copy-start.20 = (f32[4,1,1152]{2,1,0:T(1,128)S(1)}, f32[4,1,1152]{2,1,0:T(1,128)}, u32[]{:S(2)}) copy-start(f32[4,1,1152]{2,1,0:T(1,128)} %get-tuple-element.97) | copy-start | bytes 55300
  372.9 121.6 %copy-start.22 = (f32[1,1152]{1,0:T(1,128)S(1)}, f32[1,1152]{1,0:T(1,128)}, u32[]{:S(2)}) copy-start(f32[1,1152]{1,0:T(1,128)} %cond_ref.1) | copy-start | bytes 13828
  373.0 123.1 %copy-start.21 = (f32[504]{0:T(512)S(1)}, f32[504]{0:T(512)}, u32[]{:S(2)}) copy-start(f32[504]{0:T(512)} %param.60) | copy-start | bytes 6052
  373.0 123.1 %copy-start.24 = (f32[504]{0:T(512)S(1)}, f32[504]{0:T(512)}, u32[]{:S(2)}) copy-start(f32[504]{0:T(512)} %param.63) | copy-start | bytes 6052
  373.0 123.2 %copy-start.25 = (f32[504]{0:T(512)S(1)}, f32[504]{0:T(512)}, u32[]{:S(2)}) copy-start(f32[504]{0:T(512)} %param.61) | copy-start | bytes 6052
  373.0 123.2 %copy-start.26 = (f32[504]{0:T(512)S(1)}, f32[504]{0:T(512)}, u32[]{:S(2)}) copy-start(f32[504]{0:T(512)} %param.62) | copy-start | bytes 6052
  493.6 4.6 copy-start.6
  493.6 4.6 copy-start.17
  496.7 3.8 copy-start.15
  496.7 3.8 copy-start.16
  500.5 3.0 copy-start
  500.5 3.0 copy-start.7
  500.5 3.0 copy-start.8
  500.5 3.0 copy-start.9
  503.6 2.3 copy-start.10
  503.6 2.3 copy-start.11
  503.6 2.3 copy-start.12
  503.6 2.5 copy-start.14
  506.2 2.8 copy-start.4
  506.2 3.1 copy-start.5
  506.2 3.1 copy-start.18
  506.2 3.1 copy-start.23
  509.3 3.4 copy-start.1
  (3 other events, 6.3 us)

commit v4 on v3

--- a/solution.py
+++ b/solution.py
@@ -270,40 +270,44 @@
     (-3, 3), (6, 3), (9, 4), (10, 4), (14, 4), (5, 4), (13, 3), (7, 4), (6, 4), (11, 3),
     (12, 4), (13, 4), (8, 4), (11, 4),
 )
-NOTE = -4
+NOTE, TAKE, ALL = -4, -5, -6
 DOWN_SUM_PARTS = (
+    (X, Z0, Z1, Y),
+    (Y, X, Z0, Z1),
+    (Z0, Y, Z1, X),
+    (X, Z0, Z1, Y),
+    (Y, Z0, Z1, X),
+)
+UP_SUM_PARTS = (
     (X, Z0, Y, Z1),
     (X, Y, Z0, Z1),
-    (Z0, X, Y, Z1),
-    (Z0, X, Y, Z1),
-    (X, Z0, Z1, Y),
+    (Y, X, Z0, Z1),
+    (X, Y, Z0, Z1),
+    (Z0, Y, X, Z1),
 )
-FIRST_SUM_STEPS = (
-    (-3, 0), (-3, 1), (-3, 2), (-3, 3), (0, -1), (1, -1), (2, -1), (3, -1), (4, -1), (0, 0),
-    (2, 0), (1, 0), (3, 0), (4, 0), (0, 1), (1, 1), (2, 1), (4, 1), (0, 2), (1, 2),
-    (3, 1), (2, 2), (4, 2), (0, 3), (3, 2), (4, 3), (1, 3), (2, 3), (3, 3),
-)
-UP_SUM_PARTS = (
-    (Z0, X, Z1, Y),
-    (X, Z0, Z1, Y),
-    (Y, X, Z0, Z1),
+OUT_SHARES = (80, 64)
+OUT_SUM_PARTS = (
+    (X, Y, Z0, Z1),
     (Z0, Y, X, Z1),
-    (Y, X, Z1, Z0),
 )
 PAIR_SUM_PARTS = (
-    (Y, X, Z0, Z1),
-    (Y, X, Z0, Z1),
+    (Z0, Y, X, Z1),
     (X, Y, Z0, Z1),
-    (Y, X, Z0, Z1),
-    (Z0, Y, X, Z1),
+    (X, Y, Z0, Z1),
+    (X, Y, Z0, Z1),
+    (X, Y, Z0, Z1),
 )
-LAST_SUM_STEPS = (
-    (-2, 0), (0, -1), (1, -1), (2, -1), (-2, 1), (3, -1), (4, -1), (-2, 2), (0, 0), (-2, 3),
-    (5, -1), (6, -1), (7, -1), (1, 0), (2, 0), (8, -1), (9, -1), (4, 0), (0, 1), (3, 0),
-    (-4, 0), (1, 1), (5, 0), (7, 0), (9, 0), (2, 1), (0, 2), (4, 1), (6, 0), (1, 2),
-    (5, 1), (2, 2), (4, 2), (6, 1), (5, 2), (8, 0), (2, 3), (4, 3), (3, 1), (6, 2),
-    (8, 1), (5, 3), (7, 1), (3, 2), (6, 3), (9, 1), (8, 2), (0, 3), (1, 3), (7, 2),
-    (9, 2), (3, 3), (8, 3), (7, 3), (9, 3),
+SUM_STEPS = (
+    (-3, 0), (-3, 1), (-3, 2), (-3, 3), (0, -1), (1, -1), (2, -1), (-5, 0), (3, -1), (4, -1),
+    (5, -1), (6, -1), (7, -1), (-5, 1), (8, -1), (0, 0), (9, -1), (10, -1), (11, -1), (2, 0),
+    (-5, 2), (0, 1), (3, 0), (9, 0), (-5, 3), (-2, 0), (-2, 1), (5, 0), (11, 0), (1, 0),
+    (0, 2), (4, 0), (6, 0), (3, 1), (-6, 0), (-2, 2), (5, 1), (-2, 3), (4, 1), (7, 0),
+    (8, 0), (12, -1), (13, -1), (14, -1), (15, -1), (16, -1), (3, 2), (2, 1), (-4, 0), (4, 2),
+    (9, 1), (10, 0), (11, 1), (0, 3), (12, 0), (1, 1), (6, 1), (2, 2), (7, 1), (5, 2),
+    (1, 2), (6, 2), (8, 1), (3, 3), (7, 2), (13, 0), (5, 3), (10, 1), (1, 3), (12, 1),
+    (6, 3), (14, 0), (8, 2), (13, 1), (7, 3), (10, 2), (14, 1), (15, 0), (8, 3), (13, 2),
+    (16, 0), (4, 3), (10, 3), (9, 2), (15, 1), (14, 2), (11, 2), (16, 1), (2, 3), (13, 3),
+    (9, 3), (12, 2), (15, 2), (14, 3), (11, 3), (16, 2), (12, 3), (15, 3), (16, 3),
 )
 NOTE_STEP = 5
 KV_PIECES = 4
@@ -516,15 +520,9 @@
 
     def biases():
         each = width // count
-        lane = lax.broadcasted_iota(jnp.int32, (LANES, width), 1)
-        entry = lax.broadcasted_iota(jnp.int32, (LANES, width), 0)
-        copies = (lane % each == entry).astype(single).astype(bfloat)
-        owner = lax.broadcasted_iota(jnp.int32, (NOTE_ROWS, width), 1) // each
-        total = jnp.zeros((NOTE_ROWS, width), single)
         for device in range(count):
-            spread = dot_nn(inbox[device].astype(bfloat), copies)
-            total = jnp.where(owner == device, spread, total)
-        bias_ref[...] = total
+            heard = inbox[device].astype(bfloat).astype(single)
+            bias_ref[:, device * each : (device + 1) * each] = heard[:, :each]
 
     def projection(plane):
         if plane == 0:
@@ -707,6 +705,7 @@
         self.out, self.order, self.first, self.rows = out, order, first, rows
         self.send, self.recv, self.base = send, recv, base
         self.span = (pl.ds(first, rows), slice(None))
+        self.near_span = None
 
     def copy(self, source, place, slot, bit):
         return pltpu.make_async_remote_copy(
@@ -731,7 +730,7 @@
         place = self.arrivals[phase].at[(slice(None),) * (3 - phase) + self.span]
         return self.copy(source, place, phase, self.order[phase])
 
-    def add(self, fixed, source, source_dims):
+    def add(self, fixed, source, source_dims, source_span=None):
         free = [dim for dim in SLOT_DIMS if dim not in fixed]
 
         def one(step):
@@ -739,7 +738,7 @@
             for place, dim in enumerate(free):
                 index[dim] = (step >> place) & 1
             spot = tuple(index[dim] for dim in SLOT_DIMS) + self.span
-            term = source[tuple(index[dim] for dim in source_dims) + self.span]
+            term = source[tuple(index[dim] for dim in source_dims) + (source_span or self.span)]
             self.total[spot] = (self.total[spot].astype(single) + term.astype(single)).astype(
                 bfloat
             )
@@ -750,9 +749,13 @@
             one(0)
 
     def advance(self, phase):
+        span = None
+        if phase < 0 and self.near is None:
+            self.hop(0).start()
+            return
         if phase < 0:
             self.across().wait_recv()
-            source, dims, fixed = self.near, SLOT_DIMS, {}
+            source, dims, fixed, span = self.near, SLOT_DIMS, {}, self.near_span
         else:
             self.hop(phase).wait_recv()
             done = self.order[: phase + 1]
@@ -765,9 +768,9 @@
             )
             return
         ahead = self.order[phase + 1]
-        self.add(fixed | {ahead: 1}, source, dims)
+        self.add(fixed | {ahead: 1}, source, dims, span)
         self.hop(phase + 1).start()
-        self.add(fixed | {ahead: 0}, source, dims)
+        self.add(fixed | {ahead: 0}, source, dims, span)
 
     def finish(self):
         self.across().wait_send()
@@ -797,95 +800,6 @@
     return moving
 
 
-def first_scatter_kernel(kv_far, kv_near, down_far, down_near, kv_out, down_out, *refs):
-    scratch, (kv_total, kv_arrival, send, recv) = refs[:5], refs[5:]
-    greet([partner(bit) for bit in (X, Z0, Z1, CORE, Y)])
-    moving = split_scatterings(
-        down_far, down_near, scratch, down_out, SHARES, DOWN_SUM_PARTS, send, recv, 0
-    )
-    base = len(moving) * SCATTER_SEMS
-    count = kv_out.shape[0] // KV_PIECES
-
-    def kv_copy(source, place, slot, bit):
-        return pltpu.make_async_remote_copy(
-            src_ref=source,
-            dst_ref=place,
-            send_sem=send.at[base + slot],
-            recv_sem=recv.at[base + slot],
-            device_id=partner(bit),
-            device_id_type=MESH,
-        )
-
-    def near(piece):
-        rows = pl.ds(piece * count, count)
-        return kv_copy(kv_far.at[:, rows, :], kv_total.at[:, rows, :], 2 * piece, CORE)
-
-    def over(piece):
-        rows = pl.ds(piece * count, count)
-        return kv_copy(kv_total.at[1, rows, :], kv_arrival.at[rows, :], 2 * piece + 1, Y)
-
-    def kv_add(piece, side):
-        rows = pl.ds(piece * count, count)
-        kv_total[side, rows, :] = (
-            kv_total[side, rows, :].astype(single) + kv_near[side, rows, :].astype(single)
-        ).astype(bfloat)
-
-    def pass_over(piece):
-        kv_add(piece, 1)
-        over(piece).start()
-
-    def take(piece):
-        over(piece).wait_recv()
-        rows = pl.ds(piece * count, count)
-        kv_total[0, rows, :] = (
-            kv_total[0, rows, :].astype(single) + kv_arrival[rows, :].astype(single)
-        ).astype(bfloat)
-
-    for piece in range(KV_PIECES):
-        near(piece).start()
-    for part in moving:
-        part.across().start()
-    for part, phase in FIRST_SUM_STEPS:
-        if part == KV:
-            near(phase).wait_recv()
-            kv_expected(phase, functools.partial(pass_over, phase))
-            kv_add(phase, 0)
-        else:
-            moving[part].advance(phase)
-    for piece in range(KV_PIECES):
-        kv_needed(piece, functools.partial(take, piece))
-    kv_out[...] = kv_total[0]
-    for part in moving:
-        part.finish()
-    for piece in range(KV_PIECES):
-        near(piece).wait_send()
-        kv_expected(piece, lambda piece=piece: over(piece).wait_send())
-
-
-def first_scatter(kv_far, kv_near, down_far, down_near):
-    rows, width = down_far.shape[1:]
-    local, wide = kv_far.shape[1:]
-    cube = (2, 2, 2, 2, rows, width)
-    sems = len(DOWN_SUM_PARTS) * SCATTER_SEMS + 2 * KV_PIECES
-    return pl.pallas_call(
-        first_scatter_kernel,
-        out_shape=(
-            jax.ShapeDtypeStruct((local, wide), bfloat),
-            jax.ShapeDtypeStruct((rows, width), single),
-        ),
-        in_specs=[IN_HBM, IN_VMEM] * 2,
-        out_specs=(IN_VMEM,) * 2,
-        scratch_shapes=scatter_scratch(rows, width)
-        + [pltpu.VMEM((2, local, wide), bfloat), pltpu.VMEM((local, wide), bfloat)]
-        + [pltpu.SemaphoreType.DMA((sems,))] * 2,
-        compiler_params=pltpu.CompilerParams(
-            collective_id=3, has_side_effects=True, vmem_limit_bytes=VMEM_LIMIT
-        ),
-        cost_estimate=cost(0, 128 * rows * width),
-        name="first_scatter",
-    )(kv_far, kv_near, down_far.reshape(cube), down_near.reshape(cube))
-
-
 def norm_back(values, grad, scale_row):
     centre = values - jnp.mean(values, axis=-1, keepdims=True)
     root = lax.rsqrt(jnp.mean(centre * centre, axis=-1, keepdims=True) + EPSILON)
@@ -899,35 +813,40 @@
     return jnp.sum(values, axis=0, keepdims=True)
 
 
-def last_scatter_kernel(
+def scatter_kernel(
+    kv_far,
+    kv_near,
+    down_far,
+    down_near,
     up_far,
     up_near,
-    a_ref,
-    ob_ref,
-    dq_ref,
-    dkv_ref,
-    dr_ref,
+    wo_far,
     w_ref,
     x_ref,
     dmid_ref,
+    wo_near,
+    a_ref,
+    dq_ref,
     mod_ref,
     row_ref,
     ada_ref,
-    down_ref,
     up_out,
+    wo_sum,
     pair_out,
     grad_ref,
     mods_ref,
     bias_ref,
     silu_ref,
     cuts,
+    far,
     *refs,
 ):
-    up_scratch, pair_scratch, refs = refs[:5], refs[5:10], refs[10:]
-    cut_send, cut_recv, cut_ref, refs = refs[0], refs[1], refs[2], refs[3:]
-    far, near, weights, dy, table, line, bias_notes, mod_notes, bias_box, mod_box = refs[:10]
-    parts, returns, weight_sem = refs[10:13]
-    bias_send, bias_recv, mod_send, mod_recv, back_send, back_recv, send, recv = refs[13:]
+    down_scratch, up_scratch, refs = refs[:5], refs[5:10], refs[10:]
+    wo_scratch, pair_scratch, refs = refs[:5], refs[5:10], refs[10:]
+    kv_total, kv_arrival, kv_stage, stage, down_sum, cut_ref, plane_stage, refs = refs[:7] + (refs[7:],)
+    x_tile, dmid_tile, weights, dy, table, line, bias_notes, mod_notes, bias_box, mod_box = refs[:10]
+    parts, returns, cut_send, cut_recv, local_sem, far_sem = refs[10:16]
+    bias_send, bias_recv, mod_send, mod_recv, back_send, back_recv, send, recv = refs[16:]
     bucket, seq = lax.axis_index("bucket"), lax.axis_index("seq")
     me = bucket * PLANES + seq
     count = BLOCKS * PLANES
@@ -962,16 +881,82 @@
         source = parts.at[peer_at(distance)[0]]
         return message(source, returns.at[me], back_send, back_recv, distance)
 
-    base = len(UP_SUM_PARTS) * SCATTER_SEMS
-    ups = split_scatterings(
-        up_far, up_near, up_scratch, up_out, SHARES, UP_SUM_PARTS, send, recv, 0
-    )
-    pairs = split_scatterings(
-        far, near, pair_scratch, pair_out, SHARES, PAIR_SUM_PARTS, send, recv, base
-    )
-    moving = ups + pairs
-    for part in ups:
+    place = my_coords()
+    base = 0
+
+    def streams(far_ref, near_ref, scratch, out, shares, orders):
+        nonlocal base
+        start, base = base, base + len(orders) * SCATTER_SEMS
+        return split_scatterings(far_ref, near_ref, scratch, out, shares, orders, send, recv, start)
+
+    downs = streams(down_far, down_near, down_scratch, down_sum, SHARES, DOWN_SUM_PARTS)
+    ups = streams(up_far, up_near, up_scratch, up_out, SHARES, UP_SUM_PARTS)
+    wos = streams(wo_far, wo_near, wo_scratch, wo_sum, OUT_SHARES, OUT_SUM_PARTS)
+    pairs = streams(far, None, pair_scratch, pair_out, SHARES, PAIR_SUM_PARTS)
+    moving = downs + ups + wos + pairs
+    piece_rows = kv_arrival.shape[0] // KV_PIECES
+
+    def kv_copy(source, target, slot, bit):
+        return pltpu.make_async_remote_copy(
+            src_ref=source,
+            dst_ref=target,
+            send_sem=send.at[base + slot],
+            recv_sem=recv.at[base + slot],
+            device_id=partner(bit),
+            device_id_type=MESH,
+        )
+
+    def kv_span(piece):
+        return pl.ds(piece * piece_rows, piece_rows)
+
+    def near_kv(piece):
+        span = kv_span(piece)
+        return kv_copy(kv_far.at[:, span, :], kv_total.at[:, span, :], 2 * piece, CORE)
+
+    def over(piece):
+        span = kv_span(piece)
+        return kv_copy(kv_total.at[1, span, :], kv_arrival.at[span, :], 2 * piece + 1, Y)
+
+    def kv_load(piece):
+        return pltpu.make_async_copy(
+            kv_near.at[:, kv_span(piece), :], kv_stage, local_sem.at[2]
+        )
+
+    def kv_add(piece, side):
+        span = kv_span(piece)
+        kv_total[side, span, :] = (
+            kv_total[side, span, :].astype(single) + kv_stage[side].astype(single)
+        ).astype(bfloat)
+
+    def pass_over(piece):
+        kv_add(piece, 1)
+        over(piece).start()
+
+    def take(piece):
+        over(piece).wait_recv()
+        span = kv_span(piece)
+        kv_total[0, span, :] = (
+            kv_total[0, span, :].astype(single) + kv_arrival[span, :].astype(single)
+        ).astype(bfloat)
+
+    staged = [part for part, phase in SUM_STEPS if phase < 0 and 0 <= part < len(downs + ups)]
+
+    def stage_load(turn):
+        part = moving[staged[turn]]
+        spot = (slice(None),) * 4
+        return pltpu.make_async_copy(
+            part.near.at[spot + part.span],
+            stage.at[(turn % 2,) + spot + (pl.ds(0, part.rows), slice(None))],
+            local_sem.at[turn % 2],
+        )
+
+    kv_load(0).start()
+    for piece in range(KV_PIECES):
+        near_kv(piece).start()
+    for part in downs + ups + wos:
         part.across().start()
+    for turn in range(2):
+        stage_load(turn).start()
 
     def cut(distance):
         return pltpu.make_async_remote_copy(
@@ -983,24 +968,24 @@
             device_id_type=MESH,
         )
 
-    for index in range(PLANES):
-        each = cuts.shape[2]
-        cut_ref[index] = down_ref[:, index * each : (index + 1) * each].astype(bfloat)
-    cuts[seq] = cut_ref[seq]
-    for distance in range(1, PLANES):
-        cut(distance).start()
-
-    width = x_ref.shape[1]
+    def cut_down():
+        for index in range(PLANES):
+            each = cuts.shape[2]
+            cut_ref[index] = down_sum[:, index * each : (index + 1) * each].astype(bfloat)
+        cuts[seq] = cut_ref[seq]
+        for distance in range(1, PLANES):
+            cut(distance).start()
+
+    local, width = dq_ref.shape
     rows = up_out.shape[0]
     cols = 3 * width // PLANES
     wide = dy.shape[1]
-    below = wide - LANES
     order = (1, 3, 0, 2)
 
     def load(step):
         plane = seq ^ order[step]
         return pltpu.make_async_copy(
-            w_ref.at[plane, :, pl.ds(0, wide)], weights.at[step % 2], weight_sem.at[step % 2]
+            w_ref.at[plane, :, pl.ds(0, wide)], weights, local_sem.at[3]
         )
 
     def gather_dy(index):
@@ -1009,86 +994,107 @@
         if low < width:
             pieces.append(dq_ref[:, low : min(high, width)])
         if high > width:
-            pieces.append(dkv_ref[:, max(low - width, 0) : high - width])
+            pieces.append(kv_total[0, :, max(low - width, 0) : high - width])
         first = 0
         for piece in pieces:
             dy[:, first : first + piece.shape[1]] = piece
             first += piece.shape[1]
+
+    def block_spot(block, bits):
+        return (
+            bits // 2,
+            (block % 2) ^ place[X],
+            (block // 4) ^ place[Z1],
+            (block // 2 % 2) ^ place[Z0],
+        )
+
+    def far_copy(block, bits):
+        return pltpu.make_async_copy(
+            plane_stage.at[pl.ds(block * rows, rows), :],
+            far.at[block_spot(block, bits)],
+            far_sem.at[block],
+        )
 
     def project(step):
         bits = order[step]
         plane = seq ^ bits
         if step == 0:
             load(0).start()
-            dy[:, cols:] = jnp.zeros((dy.shape[0], wide - cols), bfloat)
+            dy[:, cols:] = jnp.zeros((local, wide - cols), bfloat)
             grad_ref[...] = jnp.zeros_like(grad_ref)
-        if step + 1 < PLANES:
-            load(step + 1).start()
         for index in range(PLANES):
 
             @pl.when(plane == index)
             def _():
                 gather_dy(index)
 
-        target = far if bits % 2 else near
-        place = my_coords()
-
-        def store(values, first_col):
+        if step == 1:
             for block in range(BLOCKS):
-                spot = (
-                    bits // 2,
-                    (block % 2) ^ place[X],
-                    (block // 4) ^ place[Z1],
-                    (block // 2 % 2) ^ place[Z0],
-                    slice(None),
-                    slice(first_col, first_col + values.shape[1]),
-                )
-                target[spot] = values[block * rows : (block + 1) * rows, :].astype(bfloat)
-
-        store(dot_tn(a_ref[...], dy[:, :below]), 0)
-        edge = dot_tn(ob_ref[...], dr_ref[plane])
-        store(dot_tn(a_ref[...], dy[:, below:]) + edge[:, :LANES], below)
-        store(edge[:, LANES:], wide)
+                far_copy(block, order[0]).wait()
+        total = pair_scratch[0]
+        for low, high in ((0, 4 * LANES), (4 * LANES, wide)):
+            values = dot_tn(a_ref[...], dy[:, low:high])
+            if step < 2:
+                plane_stage[:, low:high] = values.astype(bfloat)
+                continue
+            for block in range(BLOCKS):
+                spot = block_spot(block, bits) + (slice(None), slice(low, high))
+                value = values[block * rows : (block + 1) * rows, :]
+                total[spot] = (total[spot].astype(single) + value).astype(bfloat)
+        if step < 2:
+            for block in range(BLOCKS):
+                far_copy(block, bits).start()
         load(step).wait()
-        grad_ref[...] += dot_nt(dy[...], weights[step % 2])
+        grad_ref[...] += dot_nt(dy[...], weights[...])
+        if step + 1 < PLANES:
+            load(step + 1).start()
+        if step == 1:
+            for block in range(BLOCKS):
+                far_copy(block, bits).wait()
+            for part in pairs:
+                part.across().start()
+
+    def tile_loads(tile):
+        span = pl.ds(tile * LANES, LANES)
+        return (
+            pltpu.make_async_copy(x_ref.at[span, :], x_tile.at[tile % 2], far_sem.at[tile % 2]),
+            pltpu.make_async_copy(
+                dmid_ref.at[span, :], dmid_tile.at[tile % 2], far_sem.at[2 + tile % 2]
+            ),
+        )
 
     def notes():
         shift_sum, scale_sum = jnp.zeros((1, width), single), jnp.zeros((1, width), single)
         scale_row = mod_ref[1:2, :]
-        for tile in range(0, x_ref.shape[0], LANES):
-            span = slice(tile, tile + LANES)
+        tiles = local // LANES
+        for copy in tile_loads(0):
+            copy.start()
+        for tile in range(tiles):
+            if tile + 1 < tiles:
+                for copy in tile_loads(tile + 1):
+                    copy.start()
+            for copy in tile_loads(tile):
+                copy.wait()
+            span = slice(tile * LANES, (tile + 1) * LANES)
             grad = grad_ref[span, :]
-            back, normed = norm_back(x_ref[span, :].astype(single), grad, scale_row)
+            back, normed = norm_back(x_tile[tile % 2].astype(single), grad, scale_row)
             shift_sum += column_sum(grad)
             scale_sum += column_sum(grad * normed)
-            grad_ref[span, :] = dmid_ref[span, :] + back
+            grad_ref[span, :] = dmid_tile[tile % 2] + back
+        table[...] = jnp.zeros_like(table)
         line[:, :width] = shift_sum
         line[:, width : 2 * width] = scale_sum
-        table[0:1, :] = shift_sum
-        table[1:2, :] = scale_sum
+        table[0:1, :width] = shift_sum
+        table[1:2, :width] = scale_sum
         for index in range(4):
             line[:, (2 + index) * width : (3 + index) * width] = row_ref[index : index + 1, :]
-        table[2:6, :] = row_ref[0:4, :]
-        table[6:7, :] = column_sum(dq_ref[...].astype(single))
-        table[7:8, :] = column_sum(dkv_ref[:, width:].astype(single))
-        table[8:14, :] = row_ref[4:10, :]
-        table[14:16, :] = jnp.zeros((2, width), single)
+        table[2:6, :width] = row_ref[0:4, :]
+        table[6:7, :width] = column_sum(dq_ref[...].astype(single))
+        table[7:8, :width] = column_sum(kv_total[0, :, width:].astype(single))
+        table[8:14, :width] = row_ref[4:10, :]
         each = width // count
-        lane = lax.broadcasted_iota(jnp.int32, (LANES, width), 1)
-        entry = lax.broadcasted_iota(jnp.int32, (LANES, width), 0)
-        copies = (lane % each == entry).astype(single)
-        owner = lax.broadcasted_iota(jnp.int32, (NOTE_ROWS, width), 1) // each
-
-        @pl.loop(0, count)
-        def _(device):
-            mine = jnp.where(owner == device, table[...], 0.0)
-            bias_notes[device] = lax.dot_general(
-                mine,
-                copies,
-                (((1,), (1,)), ((), ())),
-                preferred_element_type=single,
-                precision=HIGHEST,
-            )
+        for device in range(count):
+            bias_notes[device] = table[:, device * each : device * each + LANES]
 
         part = mod_notes.shape[2]
         for index in range(PLANES):
@@ -1125,18 +1131,41 @@
         def _(distance):
             answer(distance).start()
 
-    since = 0
-    for part, phase in LAST_SUM_STEPS:
-        if part == PLANE:
+    since, turn, left = 0, 0, len(downs)
+    for part, phase in SUM_STEPS:
+        if part == KV:
+            near_kv(phase).wait_recv()
+            kv_load(phase).wait()
+            kv_expected(phase, functools.partial(pass_over, phase))
+            kv_add(phase, 0)
+            if phase + 1 < KV_PIECES:
+                kv_load(phase + 1).start()
+        elif part == TAKE:
+            kv_needed(phase, functools.partial(take, phase))
+        elif part == ALL:
+            for moved in pairs:
+                moved.across().wait_recv()
+        elif part == PLANE:
             project(phase)
-            if phase == 1:
-                for moved in pairs:
-                    moved.across().start()
         elif part == NOTE:
             notes()
             since = 1
         else:
-            moving[part].advance(phase)
+            mover = moving[part]
+            if phase < 0 and part < len(downs + ups):
+                stage_load(turn).wait()
+                mover.near = stage.at[turn % 2]
+                mover.near_span = (pl.ds(0, mover.rows), slice(None))
+                mover.advance(phase)
+                if turn + 2 < len(staged):
+                    stage_load(turn + 2).start()
+                turn += 1
+            else:
+                mover.advance(phase)
+            if part < len(downs) and phase == 3:
+                left -= 1
+                if left == 0:
+                    cut_down()
             since += since > 0
             if since == ANSWER_AFTER:
                 answers()
@@ -1159,6 +1188,9 @@
         silu_ref[group] = sum(returns[PLANES * group + s] for s in range(PLANES))
     for part in moving:
         part.finish()
+    for piece in range(KV_PIECES):
+        near_kv(piece).wait_send()
+        kv_expected(piece, lambda piece=piece: over(piece).wait_send())
     for distance in range(1, PLANES):
         cut(distance).wait_recv()
         cut(distance).wait_send()
@@ -1173,52 +1205,65 @@
 ANSWER_AFTER = 12
 
 
-def last_scatter(
+def scatter(
+    kv_far,
+    kv_near,
+    down_far,
+    down_near,
     up_far,
     up_near,
+    wo_far,
+    wo_near,
     first_in,
-    branch,
     query_grad,
-    kv_grad,
-    dr_planes,
     weight,
     tokens,
     middle_grad,
     mods,
     row_grads,
     ada_master,
-    down_grad,
 ):
     rows, width = up_far.shape[1:]
-    cube = (2, 2, 2, 2, rows, width)
+    edge = wo_far.shape[2]
     count = BLOCKS * PLANES
     cols = ada_master.shape[1]
     cuts = (PLANES, rows, width // PLANES)
-    local = tokens.shape[0]
+    local, kv_wide = kv_far.shape[1:]
     wide = -(-3 * width // PLANES // LANES) * LANES
-    mine = jax.ShapeDtypeStruct((rows, width), single)
+    cube, wo_cube = (2, 2, 2, 2, rows, width), (2, 2, 2, 2, rows, edge)
+    sems = (3 * len(SHARES) + len(OUT_SHARES)) * SCATTER_SEMS + 2 * KV_PIECES
     return pl.pallas_call(
-        last_scatter_kernel,
+        scatter_kernel,
         out_shape=(
-            mine,
-            mine,
+            jax.ShapeDtypeStruct((rows, width), single),
+            jax.ShapeDtypeStruct((rows, edge), single),
+            jax.ShapeDtypeStruct((rows, wide), single),
             jax.ShapeDtypeStruct((local, width), single),
             jax.ShapeDtypeStruct((BLOCKS, cols), single),
             jax.ShapeDtypeStruct((NOTE_ROWS, LANES), single),
             jax.ShapeDtypeStruct((BLOCKS, 1, 2 * LANES), single),
             jax.ShapeDtypeStruct(cuts, bfloat),
+            jax.ShapeDtypeStruct((2, 2, 2, 2, rows, wide), bfloat),
         ),
-        in_specs=[IN_HBM] + [IN_VMEM] * 6 + [IN_HBM] + [IN_VMEM] * 6,
-        out_specs=(IN_VMEM,) * 7,
+        in_specs=[IN_HBM] * 10 + [IN_VMEM] * 6,
+        out_specs=(IN_VMEM,) * 8 + (IN_HBM,),
         scratch_shapes=scatter_scratch(rows, width)
         + scatter_scratch(rows, width)
-        + [pltpu.SemaphoreType.DMA((PLANES,))] * 2
-        + [pltpu.VMEM(cuts, bfloat)]
-        + [pltpu.VMEM(cube, bfloat)] * 2
+        + scatter_scratch(rows, edge)
+        + scatter_scratch(rows, wide)
         + [
-            pltpu.VMEM((2, width, wide), bfloat),
+            pltpu.VMEM((2, local, kv_wide), bfloat),
+            pltpu.VMEM((local, kv_wide), bfloat),
+            pltpu.VMEM((2, local // KV_PIECES, kv_wide), bfloat),
+            pltpu.VMEM((2, 2, 2, 2, 2, max(SHARES), width), bfloat),
+            pltpu.VMEM((rows, width), single),
+            pltpu.VMEM(cuts, bfloat),
+            pltpu.VMEM((width, wide), bfloat),
+            pltpu.VMEM((2, LANES, width), bfloat),
+            pltpu.VMEM((2, LANES, width), single),
+            pltpu.VMEM((width, wide), bfloat),
             pltpu.VMEM((local, wide), bfloat),
-            pltpu.VMEM((NOTE_ROWS, width), single),
+            pltpu.VMEM((NOTE_ROWS, width + LANES), single),
             pltpu.VMEM((1, 6 * width), single),
             pltpu.VMEM((count, NOTE_ROWS, LANES), single),
             pltpu.VMEM((PLANES, 1, cols), single),
@@ -1226,30 +1271,35 @@
             pltpu.VMEM((count, 1, cols), single),
             pltpu.VMEM((BLOCKS, 1, 2 * LANES), single),
             pltpu.VMEM((count, 1, 2 * LANES), single),
-            pltpu.SemaphoreType.DMA((2,)),
+            pltpu.SemaphoreType.DMA((PLANES,)),
+            pltpu.SemaphoreType.DMA((PLANES,)),
+            pltpu.SemaphoreType.DMA((4,)),
+            pltpu.SemaphoreType.DMA((BLOCKS,)),
         ]
         + [pltpu.SemaphoreType.DMA((count,))] * 6
-        + [pltpu.SemaphoreType.DMA((2 * len(SHARES) * SCATTER_SEMS,))] * 2,
+        + [pltpu.SemaphoreType.DMA((sems,))] * 2,
         compiler_params=pltpu.CompilerParams(
             collective_id=4, has_side_effects=True, vmem_limit_bytes=63 * 1024 * 1024
         ),
-        cost_estimate=cost(14 * local * width * width, 200 * rows * width),
-        name="last_scatter",
+        cost_estimate=cost(12 * local * width * width, 300 * rows * width),
+        name="scatter",
     )(
+        kv_far,
+        kv_near,
+        down_far.reshape(cube),
+        down_near.reshape(cube),
         up_far.reshape(cube),
         up_near.reshape(cube),
-        first_in,
-        branch,
-        query_grad,
-        kv_grad,
-        dr_planes,
+        wo_far.reshape(wo_cube),
         weight,
         tokens,
         middle_grad,
+        wo_near.reshape(wo_cube),
+        first_in,
+        query_grad,
         mods,
         row_grads,
         ada_master,
-        down_grad,
     )
 
 
@@ -1400,55 +1450,6 @@
     )(lengths, head_table, bucket_ids, query, kv)
 
 
-def out_kernel(ob_ref, w_ref, bias_ref, x_ref, c_ref, keep_ref, mod_ref, r_ref, mid_ref, a_ref, df_ref):
-    step = pl.program_id(0)
-    width = x_ref.shape[1]
-    cols = width // PLANES
-    part = dot_nn(ob_ref[...], w_ref[0])[:, -cols:]
-    for index in range(PLANES):
-
-        @pl.when(step == index)
-        def _():
-            r_ref[:, index * cols : (index + 1) * cols] = part
-
-    @pl.when(step == PLANES - 1)
-    def _():
-        result = r_ref[...] + bias_ref[...]
-        r_ref[...] = result
-        middle = x_ref[...].astype(single) + mod_ref[2:3, :] * result
-        mid_ref[...] = middle
-        a_ref[...] = modulate(middle, mod_ref[3:4, :], mod_ref[4:5, :]).astype(bfloat)
-        df_ref[...] = (mod_ref[5:6, :] * keep_ref[...] * c_ref[...].astype(single)).astype(bfloat)
-
-
-def project_out(branch, weight, bias_row, tokens, upstream, keep, mods):
-    rows, width = tokens.shape
-    row, square = whole((1, width)), whole((rows, width))
-    return pl.pallas_call(
-        out_kernel,
-        grid=(PLANES,),
-        out_shape=(
-            jax.ShapeDtypeStruct((rows, width), single),
-            jax.ShapeDtypeStruct((rows, width), single),
-            jax.ShapeDtypeStruct((rows, width), bfloat),
-            jax.ShapeDtypeStruct((rows, width), bfloat),
-        ),
-        in_specs=[
-            square,
-            pl.BlockSpec((1, width, 3 * LANES), lambda s: (s, 0, 2)),
-            row,
-            square,
-            square,
-            whole((rows, 1)),
-            whole(mods.shape),
-        ],
-        out_specs=(square,) * 4,
-        compiler_params=params("arbitrary"),
-        cost_estimate=cost(2 * rows * width * width, 2 * width * width + 16 * rows * width),
-        name="project_out",
-    )(branch, weight, bias_row, tokens, upstream, keep, mods)
-
-
 def out_copies(source, layout, plane, buffer, seq_bits, far_ref, near_ref, sem):
     my_bucket, my_seq = place_in_kernel()
     rows = far_ref.shape[1]
@@ -1476,11 +1477,61 @@
     return seq_bits[1]
 
 
-def ffn_kernel(bucket_ref, a_ref, df_ref, cm_ref, b_ref, up_ref, down_ref, *refs):
-    f_ref, da_ref, up_far, up_near, down_far, down_near, db_ref = refs[:7]
-    up, down, up_grad, down_grad, up_sem, down_sem, up_out, down_out = refs[7:]
-    width = a_ref.shape[1]
+def middle_kernel(
+    heads,
+    bucket_ref,
+    table_ref,
+    ob_ref,
+    x_ref,
+    c_ref,
+    keep_ref,
+    mod_ref,
+    out_bias,
+    down_bias,
+    chan_ref,
+    up_bias,
+    pair_ref,
+    up_ref,
+    down_ref,
+    out_ref,
+    mid_ref,
+    up_far,
+    up_near,
+    down_far,
+    down_near,
+    wo_far,
+    wo_near,
+    do_ref,
+    delta_ref,
+    row_ref,
+    db_ref,
+    up,
+    down,
+    up_grad,
+    down_grad,
+    total,
+    da,
+    result,
+    second,
+    df,
+    dr,
+    wo_sem,
+    up_sem,
+    down_sem,
+    up_out,
+    down_out,
+    wo_out,
+):
+    local, width = x_ref.shape
     my_seq = place_in_kernel()[1]
+    cols, edge = width // PLANES, dr.shape[2]
+
+    def wo_load(plane, target):
+        source = pair_ref.at[plane, :, pl.ds(width - edge, edge)]
+        return pltpu.make_async_copy(source, target, wo_sem.at[plane])
+
+    def wo_stage(plane):
+        return up_grad.at[plane % 2, :, pl.ds(plane // 2 * edge, edge)]
 
     def loads(bits):
         plane = my_seq ^ bits
@@ -1490,38 +1541,54 @@
             pltpu.make_async_copy(down_ref.at[rows, :], down.at[rows, :], down_sem.at[bits]),
         )
 
+    for plane in range(PLANES):
+        wo_load(plane, wo_stage(plane)).start()
     for bits in (1, 3, 0, 2):
         for copy in loads(bits):
             copy.start()
-    f_ref[...] = jnp.zeros_like(f_ref)
-    da_ref[...] = jnp.zeros_like(da_ref)
+    total[...] = jnp.zeros_like(total)
+    da[...] = jnp.zeros_like(da)
+    row_ref[...] = jnp.zeros_like(row_ref)
+    for plane in range(PLANES):
+        wo_load(plane, wo_stage(plane)).wait()
+        stage = up_grad[plane % 2, :, plane // 2 * edge : (plane // 2 + 1) * edge]
+        result[:, plane * cols : (plane + 1) * cols] = dot_nn(ob_ref[...], stage)[:, -cols:]
+
+    @pl.loop(0, local, step=LANES)
+    def _(tile):
+        span = pl.ds(pl.multiple_of(tile, LANES), LANES)
+        branch = result[span, :] + out_bias[...]
+        result[span, :] = branch
+        middle = x_ref[span, :].astype(single) + mod_ref[2:3, :] * branch
+        mid_ref[span, :] = middle
+        second[span, :] = modulate(middle, mod_ref[3:4, :], mod_ref[4:5, :]).astype(bfloat)
+        upstream = c_ref[span, :].astype(single)
+        df[span, :] = (mod_ref[5:6, :] * keep_ref[span, :] * upstream).astype(bfloat)
 
     def one(plane, low, high, buffer):
-        first, grad = a_ref[...], df_ref[...]
+        first, grad = second[...], df[...]
         hidden_rows = pl.ds(pl.multiple_of(plane * width + low, LANES), high - low)
-        keep = cm_ref[pl.ds(bucket_ref[0], 1), hidden_rows].astype(single)
-        pre = dot_nn(first, up[plane, :, low:high]) + b_ref[plane, :, low:high]
+        keep = chan_ref[pl.ds(bucket_ref[0], 1), hidden_rows].astype(single)
+        pre = dot_nn(first, up[plane, :, low:high]) + up_bias[plane, :, low:high]
         root = math.sqrt(2.0 / math.pi)
         square = pre * pre
-        bend = jnp.tanh(root * pre * (1.0 + 0.044715 * square))
-        half = 0.5 * (1.0 + bend)
-        hidden = (pre * half * keep).astype(bfloat)
-        slope = half + 0.5 * pre * (1.0 - bend * bend) * (root * (1.0 + 0.134145 * square))
-        back = (dot_nt(grad, down[hidden_rows, :]) * keep * slope).astype(bfloat)
-        f_ref[...] += dot_nn(hidden, down[hidden_rows, :])
-        da_ref[...] += dot_nt(back, up[plane, :, low:high])
+        half = 0.5 + 0.5 * jnp.tanh(pre * (root + (root * 0.044715) * square))
+        kept = half * keep
+        hidden = (pre * kept).astype(bfloat)
+        bend = pre * (1.0 - half) * (2.0 * root + (2.0 * root * 0.134145) * square)
+        back = (dot_nt(grad, down[hidden_rows, :]) * (kept + kept * bend)).astype(bfloat)
+        total[...] += dot_nn(hidden, down[hidden_rows, :])
+        da[...] += dot_nt(back, up[plane, :, low:high])
         up_grad[buffer, :, low:high] = dot_tn(first, back).astype(bfloat)
         down_grad[buffer, low:high, :] = dot_tn(hidden, grad).astype(bfloat)
-        db_ref[plane, :, low:high] = jnp.sum(back.astype(single), axis=0, keepdims=True)
+        db_ref[plane, :, low:high] = column_sum(back.astype(single))
 
     cut = -(-width // 2 // LANES) * LANES
 
     def sends(plane, buffer, side_bits, far_side):
         return out_copies(
             up_grad, "planes", plane, buffer, (side_bits, far_side), up_far, up_near, up_out
-        ) + out_copies(
-            down_grad, "rows", plane, buffer, None, down_far, down_near, down_out
-        )
+        ) + out_copies(down_grad, "rows", plane, buffer, None, down_far, down_near, down_out)
 
     for far_side in (1, 0):
 
@@ -1539,202 +1606,160 @@
             for copy in sends(plane, above, bits, far_side):
                 copy.start()
 
+    def wo_end(plane):
+        return down.at[pl.ds(plane * width, width), pl.ds(0, edge)]
+
+    for plane in range(PLANES):
+        wo_load(plane, wo_end(plane)).start()
+    gate_one, scale, gate_two = mod_ref[2:3, :], mod_ref[4:5, :], mod_ref[5:6, :]
+
+    @pl.loop(0, local, step=LANES)
+    def _(tile):
+        span = pl.ds(pl.multiple_of(tile, LANES), LANES)
+        keep = keep_ref[span, :]
+        upstream = c_ref[span, :].astype(single)
+        middle = mid_ref[span, :]
+        mlp = total[span, :] + down_bias[...]
+        out_ref[span, :] = (middle + gate_two * keep * mlp).astype(bfloat)
+        grad = da[span, :]
+        back, normed = norm_back(middle, grad, scale)
+        dmid = upstream + back
+        mid_ref[span, :] = dmid
+        branch = (gate_one * dmid).astype(bfloat).astype(single)
+        for plane in range(PLANES):
+            dr[plane, span, : edge - cols] = jnp.zeros((LANES, edge - cols), bfloat)
+            dr[plane, span, edge - cols :] = branch[:, plane * cols : (plane + 1) * cols].astype(
+                bfloat
+            )
+        row_ref[0:1, :] += column_sum(dmid * result[span, :])
+        row_ref[1:2, :] += column_sum(grad)
+        row_ref[2:3, :] += column_sum(grad * normed)
+        row_ref[3:4, :] += column_sum(keep * upstream * mlp)
+        row_ref[4:5, :] += column_sum(branch)
+        row_ref[5:6, :] += column_sum(df[span, :].astype(single))
+
     for above in range(2):
         for copy in sends(my_seq ^ (above * 2), above, above * 2, 0):
             copy.wait()
-
-
-def feed_forward(bucket_ids, first, grad, chan_table, bias_row, up_weight, down_weight):
-    rows, width = first.shape
-    hidden = chan_table.shape[1]
+    stage = up_grad.at[:, :, pl.ds(0, edge)]
+    for far_side in (1, 0):
+        for above in range(2):
+            bits = above * 2 + far_side
+            plane = my_seq ^ bits
+            copies = out_copies(
+                stage, "planes", plane, above, (bits, far_side), wo_far, wo_near, wo_out
+            )
+            if not far_side:
+                for copy in copies:
+                    copy.wait()
+            up_grad[above, :, :edge] = dot_tn(ob_ref[...], dr[plane]).astype(bfloat)
+            for copy in copies:
+                copy.start()
+    for plane in range(PLANES):
+        wo_load(plane, wo_end(plane)).wait()
+        part = dot_nt(dr[plane], down[plane * width : (plane + 1) * width, :edge])
+        if plane == 0:
+            total[...] = part
+        else:
+            total[...] += part
+    size = width // heads
+    grad = (total[...] * head_row(table_ref, bucket_ref, width)).astype(bfloat)
+    do_ref[...] = grad
+    terms = grad.astype(single) * ob_ref[...].astype(single)
+    head = lax.broadcasted_iota(jnp.int32, (heads, width), 0)
+    lane = lax.broadcasted_iota(jnp.int32, (heads, width), 1)
+    chosen = jnp.logical_and(lane >= head * size, lane < (head + 1) * size)
+    delta_ref[...] = lax.dot_general(
+        chosen.astype(single),
+        terms,
+        (((1,), (1,)), ((), ())),
+        preferred_element_type=single,
+        precision=HIGHEST,
+    )
+    for above in range(2):
+        for copy in out_copies(
+            stage, "planes", my_seq ^ (above * 2), above, (above * 2, 0), wo_far, wo_near, wo_out
+        ):
+            copy.wait()
+
+
+def middle(
+    bucket_ids,
+    head_table,
+    branch,
+    tokens,
+    upstream,
+    keep,
+    mods,
+    out_bias,
+    down_bias,
+    chan_table,
+    up_bias,
+    pair_weight,
+    up_weight,
+    down_weight,
+):
+    rows, width = branch.shape
+    heads, hidden = head_table.shape[1], chan_table.shape[1]
+    edge = 3 * LANES
     blocks = jax.ShapeDtypeStruct((BLOCKS * PLANES // 2, width // BLOCKS, width), bfloat)
-    result = pl.pallas_call(
-        ffn_kernel,
+    narrow = jax.ShapeDtypeStruct((BLOCKS * PLANES // 2, width // BLOCKS, edge), bfloat)
+    square = pltpu.VMEM((rows, width), single)
+    low_square = pltpu.VMEM((rows, width), bfloat)
+    return pl.pallas_call(
+        functools.partial(middle_kernel, heads),
         out_shape=(
-            jax.ShapeDtypeStruct((rows, width), single),
+            jax.ShapeDtypeStruct((rows, width), bfloat),
             jax.ShapeDtypeStruct((rows, width), single),
             blocks,
             blocks,
             blocks,
             blocks,
+            narrow,
+            narrow,
+            jax.ShapeDtypeStruct((rows, width), bfloat),
+            jax.ShapeDtypeStruct((heads, rows), single),
+            jax.ShapeDtypeStruct((8, width), single),
             jax.ShapeDtypeStruct((PLANES, 1, width), single),
         ),
-        in_specs=[IN_SMEM] + [IN_VMEM] * 4 + [IN_HBM] * 2,
-        out_specs=(IN_VMEM, IN_VMEM) + (IN_HBM,) * 4 + (IN_VMEM,),
+        in_specs=[IN_SMEM] * 2 + [IN_VMEM] * 9 + [IN_HBM] * 3,
+        out_specs=(IN_VMEM,) * 2 + (IN_HBM,) * 6 + (IN_VMEM,) * 4,
         scratch_shapes=[
             pltpu.VMEM((PLANES, width, width), bfloat),
             pltpu.VMEM((hidden, width), bfloat),
             pltpu.VMEM((2, width, width), bfloat),
             pltpu.VMEM((2, width, width), bfloat),
+            square,
+            square,
+            square,
+            low_square,
+            low_square,
+            pltpu.VMEM((PLANES, rows, edge), bfloat),
+            pltpu.SemaphoreType.DMA((PLANES,)),
             pltpu.SemaphoreType.DMA((PLANES,)),
             pltpu.SemaphoreType.DMA((PLANES,)),
             pltpu.SemaphoreType.DMA((2, BLOCKS)),
             pltpu.SemaphoreType.DMA((2, BLOCKS)),
+            pltpu.SemaphoreType.DMA((2, BLOCKS)),
         ],
-        compiler_params=params(),
+        compiler_params=pltpu.CompilerParams(vmem_limit_bytes=63 * 1024 * 1024),
         cost_estimate=cost(12 * rows * width * hidden, 8 * width * hidden, rows * hidden),
-        name="feed_forward",
+        name="middle",
     )(
         bucket_ids,
-        first,
-        grad,
-        chan_table,
-        bias_row.reshape(PLANES, 1, width),
-        up_weight,
-        down_weight,
-    )
-    return result
-
-
-def back_out_kernel(
-    heads,
-    f_ref,
-    da_ref,
-    mid_ref,
-    r_ref,
-    c_ref,
-    keep_ref,
-    mod_ref,
-    bias_ref,
-    df_ref,
-    w_ref,
-    table_ref,
-    bucket_ref,
-    ob_ref,
-    out_ref,
-    dmid_ref,
-    dr_ref,
-    row_ref,
-    do_ref,
-    delta_ref,
-    acc,
-):
-    step = pl.program_id(0)
-    width = acc.shape[1]
-    cols = width // PLANES
-    edge = dr_ref.shape[2] - cols
-
-    @pl.when(step == 0)
-    def _():
-        row_ref[...] = jnp.zeros_like(row_ref)
-        acc[...] = jnp.zeros_like(acc)
-        gate_one, scale, gate_two = mod_ref[2:3, :], mod_ref[4:5, :], mod_ref[5:6, :]
-
-        @pl.loop(0, acc.shape[0], step=LANES)
-        def _(tile):
-            span = pl.ds(pl.multiple_of(tile, LANES), LANES)
-            keep = keep_ref[span, :]
-            upstream = c_ref[span, :].astype(single)
-            middle = mid_ref[span, :]
-            mlp = f_ref[span, :] + bias_ref[...]
-            out_ref[span, :] = (middle + gate_two * keep * mlp).astype(bfloat)
-            grad = da_ref[span, :]
-            back, normed = norm_back(middle, grad, scale)
-            dmid = upstream + back
-            dmid_ref[span, :] = dmid
-            branch = (gate_one * dmid).astype(bfloat).astype(single)
-            for plane in range(PLANES):
-                dr_ref[plane, span, :edge] = jnp.zeros((LANES, edge), bfloat)
-                dr_ref[plane, span, edge:] = branch[:, plane * cols : (plane + 1) * cols].astype(
-                    bfloat
-                )
-            row_ref[0:1, :] += column_sum(dmid * r_ref[span, :])
-            row_ref[1:2, :] += column_sum(grad)
-            row_ref[2:3, :] += column_sum(grad * normed)
-            row_ref[3:4, :] += column_sum(keep * upstream * mlp)
-            row_ref[4:5, :] += column_sum(branch)
-            row_ref[5:6, :] += column_sum(df_ref[span, :].astype(single))
-
-    acc[...] += dot_nt(dr_ref[step], w_ref[0])
-
-    @pl.when(step == PLANES - 1)
-    def _():
-        size = width // heads
-        grad = (acc[...] * head_row(table_ref, bucket_ref, width)).astype(bfloat)
-        do_ref[...] = grad
-        terms = grad.astype(single) * ob_ref[...].astype(single)
-        head = lax.broadcasted_iota(jnp.int32, (heads, width), 0)
-        lane = lax.broadcasted_iota(jnp.int32, (heads, width), 1)
-        chosen = jnp.logical_and(lane >= head * size, lane < (head + 1) * size)
-        delta_ref[...] = lax.dot_general(
-            chosen.astype(single),
-            terms,
-            (((1,), (1,)), ((), ())),
-            preferred_element_type=single,
-            precision=HIGHEST,
-        )
-
-
-def back_out(
-    mlp_sum,
-    second_grad,
-    middle,
-    attn_out,
-    upstream,
-    keep,
-    mods,
-    bias_row,
-    mlp_grad,
-    weight,
-    head_table,
-    bucket_ids,
-    branch,
-    heads,
-):
-    rows, width = branch.shape
-    row, square = whole((1, width)), whole((rows, width))
-    return pl.pallas_call(
-        functools.partial(back_out_kernel, heads),
-        grid=(PLANES,),
-        out_shape=(
-            jax.ShapeDtypeStruct((rows, width), bfloat),
-            jax.ShapeDtypeStruct((rows, width), single),
-            jax.ShapeDtypeStruct((PLANES, rows, 3 * LANES), bfloat),
-            jax.ShapeDtypeStruct((8, width), single),
-            jax.ShapeDtypeStruct((rows, width), bfloat),
-            jax.ShapeDtypeStruct((heads, rows), single),
-        ),
-        in_specs=[
-            square,
-            square,
-            square,
-            square,
-            square,
-            whole((rows, 1)),
-            whole(mods.shape),
-            row,
-            square,
-            pl.BlockSpec((1, width, 3 * LANES), lambda s: (s, 0, 2)),
-            IN_SMEM,
-            IN_SMEM,
-            square,
-        ],
-        out_specs=(
-            square,
-            square,
-            whole((PLANES, rows, 3 * LANES)),
-            whole((8, width)),
-            square,
-            whole((heads, rows)),
-        ),
-        scratch_shapes=[pltpu.VMEM((rows, width), single)],
-        compiler_params=params("arbitrary"),
-        cost_estimate=cost(2 * rows * width * width, 2 * width * width + 30 * rows * width),
-        name="back_out",
-    )(
-        mlp_sum,
-        second_grad,
-        middle,
-        attn_out,
+        head_table,
+        branch,
+        tokens,
         upstream,
         keep,
         mods,
-        bias_row,
-        mlp_grad,
-        weight,
-        head_table,
-        bucket_ids,
-        branch,
+        out_bias,
+        down_bias,
+        chan_table,
+        up_bias.reshape(PLANES, 1, width),
+        pair_weight,
+        up_weight,
+        down_weight,
     )
 
 
@@ -1813,12 +1838,9 @@
     )(lengths, query, grad, logs, delta, kv)
 
 
-def back_qkv_kernel(
-    a_ref, ob_ref, dy_ref, dr_ref, w_ref, da_ref, far_ref, near_ref, stage, sem
-):
+def back_qkv_kernel(a_ref, dy_ref, w_ref, da_ref, far_ref, near_ref, stage, sem):
     my_seq = place_in_kernel()[1]
     wide = dy_ref.shape[2]
-    below = wide - LANES
     da_ref[...] = jnp.zeros_like(da_ref)
 
     def sends(plane, buffer, bits, far_side):
@@ -1836,11 +1858,7 @@
                 for copy in sends(plane, above, bits, far_side):
                     copy.wait()
             da_ref[...] += dot_nt(dy_ref[plane], w_ref[plane, :, :wide])
-            first = dot_tn(a_ref[...], dy_ref[plane])
-            second = dot_tn(ob_ref[...], dr_ref[plane])
-            stage[above, :, :below] = first[:, :below].astype(bfloat)
-            stage[above, :, below:wide] = (first[:, below:] + second[:, :LANES]).astype(bfloat)
-            stage[above, :, wide:] = second[:, LANES:].astype(bfloat)
+            stage[above] = dot_tn(a_ref[...], dy_ref[plane]).astype(bfloat)
             for copy in sends(plane, above, bits, far_side):
                 copy.start()
 
@@ -1849,22 +1867,23 @@
             copy.wait()
 
 
-def back_qkv(first_in, branch, dy_planes, dr_planes, weight):
+def back_qkv(first_in, dy_planes, weight):
     rows, width = first_in.shape
-    blocks = jax.ShapeDtypeStruct((BLOCKS * PLANES // 2, width // BLOCKS, width), bfloat)
+    wide = dy_planes.shape[2]
+    blocks = jax.ShapeDtypeStruct((BLOCKS * PLANES // 2, width // BLOCKS, wide), bfloat)
     return pl.pallas_call(
         back_qkv_kernel,
         out_shape=(jax.ShapeDtypeStruct((rows, width), single), blocks, blocks),
-        in_specs=[IN_VMEM] * 5,
+        in_specs=[IN_VMEM] * 3,
         out_specs=(IN_VMEM, IN_HBM, IN_HBM),
         scratch_shapes=[
-            pltpu.VMEM((2, width, width), bfloat),
+            pltpu.VMEM((2, width, wide), bfloat),
             pltpu.SemaphoreType.DMA((2, BLOCKS)),
         ],
         compiler_params=params(),
-        cost_estimate=cost(14 * rows * width * width, 4 * weight.size),
+        cost_estimate=cost(12 * rows * width * width, 4 * weight.size),
         name="back_qkv",
-    )(first_in, branch, dy_planes, dr_planes, weight)
+    )(first_in, dy_planes, weight)
 
 
 def on_device(
@@ -1963,27 +1982,34 @@
     down_bias = bias_table[table_cols - 1 : table_cols]
     keep_float = keep_flags.astype(single)[:, None]
     branch_in, logs = attend(lengths, head_table, bucket_ids, query, near, heads)
-    attn_out, middle, second_in, mlp_grad = project_out(
-        branch_in, pair_weight, out_bias, tokens, cotangent, keep_float, mods
-    )
-    mlp_sum, second_grad, up_far, up_near, down_far, down_near, up_bias_grad = feed_forward(
-        bucket_ids, second_in, mlp_grad, chan_table, up_bias, up_weight, down_weight
-    )
-    output, middle_grad, dr_planes, row_grads, attended_grad, delta = back_out(
-        mlp_sum,
-        second_grad,
-        middle,
-        attn_out,
+    (
+        output,
+        middle_grad,
+        up_far,
+        up_near,
+        down_far,
+        down_near,
+        wo_far,
+        wo_near,
+        attended_grad,
+        delta,
+        row_grads,
+        up_bias_grad,
+    ) = middle(
+        bucket_ids,
+        head_table,
+        branch_in,
+        tokens,
         cotangent,
         keep_float,
         mods,
+        out_bias,
         down_bias,
-        mlp_grad,
+        chan_table,
+        up_bias,
         pair_weight,
-        head_table,
-        bucket_ids,
-        branch_in,
-        heads,
+        up_weight,
+        down_weight,
     )
     up_bias_rows = up_bias_grad.reshape(width, hidden_ratio).T
     query_grad, kv_far, kv_near = attend_back(
@@ -1991,32 +2017,35 @@
     )
     qkv_cols = 3 * width // seqs
     if cube_path():
-        kv_grad, down_new_grad = first_scatter(kv_far, kv_near, down_far, down_near)
         rows_all = jnp.concatenate([row_grads[:5], up_bias_rows, row_grads[5:6]])
         rows_all = jnp.pad(rows_all, ((0, 16 - rows_all.shape[0]), (0, 0)))
         (
             up_new_grad,
+            out_new_grad,
             pair_new_grad,
             token_grad,
             mod_all,
             bias_sum,
             silu_sum,
             down_cuts,
-        ) = last_scatter(
+            _,
+        ) = scatter(
+            kv_far,
+            kv_near,
+            down_far,
+            down_near,
             up_far,
             up_near,
+            wo_far,
+            wo_near,
             first_in,
-            branch_in,
             query_grad,
-            kv_grad,
-            dr_planes,
             pair_weight,
             tokens,
             middle_grad,
             mods,
             rows_all,
             ada_master,
-            down_new_grad,
         )
         down_mine = down_cuts.reshape(down_master.shape)
         bias_new_grad = bias_sum[:table_cols, : width // (buckets * seqs)].T.reshape(-1)
@@ -2029,9 +2058,8 @@
             projected_grad.reshape(local_rows, seqs, qkv_cols).transpose(1, 0, 2),
             ((0, 0), (0, 0), (0, -qkv_cols % LANES)),
         )
-        first_grad, pair_far, pair_near = back_qkv(
-            first_in, branch_in, dy_planes, dr_planes, pair_weight
-        )
+        first_grad, pair_far, pair_near = back_qkv(first_in, dy_planes, pair_weight)
+        out_new_grad = natural_sum(wo_far, wo_near, "planes")
         back, normed = norm_back(tokens.astype(single), first_grad, mods[1:2])
         token_grad = middle_grad + back
         up_new_grad = natural_sum(up_far, up_near, "planes")
@@ -2097,7 +2125,7 @@
         out_first,
         out_second,
         out_average,
-        pair_new_grad[:, qkv_cols:],
+        out_new_grad[:, -out_master.shape[1] :],
         out_rate,
         MATRIX_DECAY,
     )

time: 524 us -> 503 us (0.960)
  Pallas kernels: 482 us -> 462 us
    pallas_call x5 -> x2, Pallas kernels: 282 us -> 271 us  [the longest x1 204 us: scatter(): pl.pallas_call(scatter_kernel, out_shape=(jax.ShapeDtypeStruct((rows, wid...]
where the time goes in v4:
time: 503 us; the launch traced here: 494 us
  Pallas kernels  462 us (92%)
  other arithmetic  14.6 us (3%)
  local copies, waits for them, and re-layouts  12.5 us (2%)
    pallas_call x1, Pallas kernels, scatter(): pl.pallas_call(scatter_kernel, out_shape=(jax.ShapeDtypeStruct((rows, wid...  204 us
    pallas_call x1, Pallas kernels, gather(): pl.pallas_call(gather_kernel, out_shape=(blocks, blocks, blocks, jax.Shap...  158 us
    pallas_call x1, Pallas kernels, middle(): pl.pallas_call(functools.partial(middle_kernel, heads), out_shape=(jax.Sh...  66.6 us
    pallas_call x1, Pallas kernels, attend_back(): pl.pallas_call(functools.partial(attend_back_kernel, heads), out_shape=(j...  23.5 us
    add x5, other arithmetic, adam_update(): average_new = average_decay * average + (1.0 - average_decay) * master_new  10.2 us

profile of v4, /device:TPU:0, one launch (start us, length us, event | category | flops | bytes accessed | tf_op | source)
XLA Modules:
  0.0 494.1 jit_solution(11576711976992230161)
XLA Ops:
  1.3 0.7 convert_element_type.20
  2.0 0.8 reshape.99
  2.8 0.7 copy.64
  3.5 0.9 copy.67.keep_ref
  4.3 1.2 convert_element_type.19
  5.5 1.0 copy.65
  6.5 157.7 %gather.1 = (bf16[2,2,2,2,2,144,1152]{6,5,4,3,2,1,0:T(8,128)(2,1)}, bf16[2,2,2,2,2,144,1152]{6,5,4,3,2,1,0:T(8,128)(2,1)}, bf16[2,2,2,2,2,144,1152]{6,5,4,3,2,1,...) custom-call(f32[1,1152]{1,0:T(1,128)} %cond_ref.1, ...), custom_call_target="tpu_custom_call" | custom-call | flops 4076863488 | bytes 33177600 | tf_op jit(solution)/shard_map/gather/pallas_call | solution.py:619
  164.2 1.4 fusion.22
  165.6 0.8 slice_bitcast_fusion
  166.6 1.0 reshape_reshape.4.up_bias
  167.6 9.8 %attend.1 = (bf16[512,1152]{1,0:T(8,128)(2,1)}, f32[16,512]{1,0:T(8,128)}) custom-call(s32[1,8]{1,0:T(1,128)} %len_ref.3, s32[10,16]{1,0:T(8,128)} %table_ref.3, s32[1]{0:T(128)S(6)} %copy.75.bucket_ref, bf16[512,1152]{1,0:T(8,128)(2,1)} %get-tuple-element.61.q_ref, bf16[2048,2304]{1,0:T(8,128)(2,1)} %bitcast.38), custom_call_target="tpu_custom_call" | custom-call | flops 9663676416 | bytes 23592960 | tf_op jit(solution)/shard_map/attend/pallas_call | solution.py:1438
  177.4 66.6 %middle.1 = (bf16[512,1152]{1,0:T(8,128)(2,1)}, f32[512,1152]{1,0:T(8,128)}, bf16[16,144,1152]{2,1,0:T(8,128)(2,1)}, bf16[16,144,1152]{2,1,0:T(8,128)(2,1)}, bf1...) custom-call(s32[1]{0:T(128)S(6)} %copy.75.bucket_ref, ...), custom_call_target="tpu_custom_call" | custom-call | flops 32614907904 | bytes 42467328 | tf_op jit(solution)/shard_map/middle/pallas_call | solution.py:1709
  244.1 23.5 %attend_back.1 = (bf16[512,1152]{1,0:T(8,128)(2,1)}, bf16[2,512,2304]{2,1,0:T(8,128)(2,1)}, bf16[2,512,2304]{2,1,0:T(8,128)(2,1)}) custom-call(s32[1,8]{1,0:T(1,128)} %len_ref.3, bf16[512,1152]{1,0:T(8,128)(2,1)} %get-tuple-element.61.q_ref, bf16[512,1152]{1,0:T(8,128)(2,1)} %get-tuple-element.70.do_ref, f32[16,512]{1,0:T(8,128)} %get-tuple-element.71.log_ref, ...), custom_call_target="tpu_custom_call" | custom-call | flops 24159191040 | bytes 47185920 | tf_op jit(solution)/shard_map/attend_back/pallas_call | solution.py:1820
  269.2 204.0 %scatter.1 = (f32[144,1152]{1,0:T(8,128)}, f32[144,384]{1,0:T(8,128)}, f32[144,896]{1,0:T(8,128)}, f32[512,1152]{1,0:T(8,128)}, f32[8,1728]{1,0:T(8,128)}, /*ind...) custom-call(bf16[2,512,2304]{2,1,0:T(8,128)(2,1)} %get-tuple-element, ...), custom_call_target="tpu_custom_call" | custom-call | flops 8153726976 | bytes 49766400 | tf_op jit(solution)/shard_map/scatter/pallas_call | solution.py:1235
  473.2 0.8 slice_reduce_fusion
  474.7 0.7 slice_bitcast_fusion.1
  476.3 1.2 bitcast_convert_fusion
  477.8 2.4 multiply_add_fusion.9
  480.2 3.0 multiply_add_fusion.7
  483.3 2.2 multiply_add_fusion.5
  485.9 2.0 multiply_add_fusion.6
  487.9 0.8 copy-done.4
  489.0 3.4 multiply_add_fusion.2
  492.3 1.4 copy.76
  (65 shorter events, 4.4 us)
Async XLA Ops:
  244.1 23.5 %copy-start.19 = (f32[8,1152]{1,0:T(8,128)S(1)}, f32[8,1152]{1,0:T(8,128)}, u32[]{:S(2)}) copy-start(f32[8,1152]{1,0:T(8,128)} %get-tuple-element.84) | copy-start | bytes 110596
  244.1 23.5 %copy-start.20 = (f32[4,1,1152]{2,1,0:T(1,128)S(1)}, f32[4,1,1152]{2,1,0:T(1,128)}, u32[]{:S(2)}) copy-start(f32[4,1,1152]{2,1,0:T(1,128)} %get-tuple-element.85) | copy-start | bytes 55300
  269.1 204.9 %copy-start.22 = (f32[1,1152]{1,0:T(1,128)S(1)}, f32[1,1152]{1,0:T(1,128)}, u32[]{:S(2)}) copy-start(f32[1,1152]{1,0:T(1,128)} %cond_ref.1) | copy-start | bytes 13828
  269.1 206.5 %copy-start.21 = (f32[504]{0:T(512)S(1)}, f32[504]{0:T(512)}, u32[]{:S(2)}) copy-start(f32[504]{0:T(512)} %param.60) | copy-start | bytes 6052
  269.1 206.5 %copy-start.24 = (f32[504]{0:T(512)S(1)}, f32[504]{0:T(512)}, u32[]{:S(2)}) copy-start(f32[504]{0:T(512)} %param.63) | copy-start | bytes 6052
  269.1 206.5 %copy-start.25 = (f32[504]{0:T(512)S(1)}, f32[504]{0:T(512)}, u32[]{:S(2)}) copy-start(f32[504]{0:T(512)} %param.61) | copy-start | bytes 6052
  269.1 206.5 %copy-start.26 = (f32[504]{0:T(512)S(1)}, f32[504]{0:T(512)}, u32[]{:S(2)}) copy-start(f32[504]{0:T(512)} %param.62) | copy-start | bytes 6052
  473.2 4.6 copy-start.17
  476.3 4.0 copy-start.14
  476.3 4.0 copy-start.15
  476.3 4.0 copy-start.16
  480.2 3.0 copy-start.1
  480.2 3.0 copy-start.6
  480.2 3.0 copy-start.7
  480.2 3.0 copy-start.8
  483.2 2.3 copy-start.9
  483.3 2.3 copy-start.10
  483.3 2.3 copy-start.11
  483.3 2.6 copy-start.13
  485.9 2.8 copy-start.4
  485.9 3.1 copy-start.5
  485.9 3.1 copy-start.18
  485.9 3.1 copy-start.23
  489.0 3.4 copy-start.2
  (3 other events, 6.3 us)

commit v5 on v4

--- a/solution.py
+++ b/solution.py
@@ -272,42 +272,42 @@
 )
 NOTE, TAKE, ALL = -4, -5, -6
 DOWN_SUM_PARTS = (
+    (X, Z0, Y, Z1),
+    (Z0, X, Y, Z1),
+    (Z0, X, Y, Z1),
+    (Y, Z0, Z1, X),
+    (X, Z0, Z1, Y),
+)
+UP_SUM_PARTS = (
     (X, Z0, Z1, Y),
     (Y, X, Z0, Z1),
-    (Z0, Y, Z1, X),
-    (X, Z0, Z1, Y),
-    (Y, Z0, Z1, X),
-)
-UP_SUM_PARTS = (
-    (X, Z0, Y, Z1),
     (X, Y, Z0, Z1),
-    (Y, X, Z0, Z1),
     (X, Y, Z0, Z1),
     (Z0, Y, X, Z1),
 )
 OUT_SHARES = (80, 64)
 OUT_SUM_PARTS = (
+    (Y, X, Z0, Z1),
     (X, Y, Z0, Z1),
-    (Z0, Y, X, Z1),
 )
 PAIR_SUM_PARTS = (
     (Z0, Y, X, Z1),
     (X, Y, Z0, Z1),
     (X, Y, Z0, Z1),
-    (X, Y, Z0, Z1),
+    (Y, X, Z0, Z1),
     (X, Y, Z0, Z1),
 )
 SUM_STEPS = (
-    (-3, 0), (-3, 1), (-3, 2), (-3, 3), (0, -1), (1, -1), (2, -1), (-5, 0), (3, -1), (4, -1),
-    (5, -1), (6, -1), (7, -1), (-5, 1), (8, -1), (0, 0), (9, -1), (10, -1), (11, -1), (2, 0),
-    (-5, 2), (0, 1), (3, 0), (9, 0), (-5, 3), (-2, 0), (-2, 1), (5, 0), (11, 0), (1, 0),
-    (0, 2), (4, 0), (6, 0), (3, 1), (-6, 0), (-2, 2), (5, 1), (-2, 3), (4, 1), (7, 0),
-    (8, 0), (12, -1), (13, -1), (14, -1), (15, -1), (16, -1), (3, 2), (2, 1), (-4, 0), (4, 2),
-    (9, 1), (10, 0), (11, 1), (0, 3), (12, 0), (1, 1), (6, 1), (2, 2), (7, 1), (5, 2),
-    (1, 2), (6, 2), (8, 1), (3, 3), (7, 2), (13, 0), (5, 3), (10, 1), (1, 3), (12, 1),
-    (6, 3), (14, 0), (8, 2), (13, 1), (7, 3), (10, 2), (14, 1), (15, 0), (8, 3), (13, 2),
-    (16, 0), (4, 3), (10, 3), (9, 2), (15, 1), (14, 2), (11, 2), (16, 1), (2, 3), (13, 3),
-    (9, 3), (12, 2), (15, 2), (14, 3), (11, 3), (16, 2), (12, 3), (15, 3), (16, 3),
+    (-3, 0), (-3, 1), (-3, 2), (-3, 3), (0, -1), (1, -1), (-5, 0), (2, -1), (3, -1), (4, -1),
+    (5, -1), (-5, 1), (6, -1), (0, 0), (7, -1), (1, 0), (8, -1), (9, -1), (-5, 2), (4, 0),
+    (10, -1), (11, -1), (-5, 3), (2, 0), (-2, 0), (5, 0), (0, 1), (-2, 1), (3, 0), (9, 0),
+    (4, 1), (7, 0), (5, 1), (1, 1), (6, 0), (-6, 0), (-2, 2), (3, 1), (-2, 3), (4, 2),
+    (8, 0), (10, 0), (12, -1), (13, -1), (14, -1), (15, -1), (16, -1), (5, 2), (0, 2), (9, 1),
+    (-4, 0), (11, 0), (3, 2), (7, 1), (2, 1), (1, 2), (4, 3), (12, 0), (6, 1), (0, 3),
+    (8, 1), (7, 2), (10, 1), (1, 3), (6, 2), (15, 0), (5, 3), (8, 2), (13, 0), (7, 3),
+    (11, 1), (10, 2), (2, 2), (6, 3), (14, 0), (8, 3), (12, 1), (11, 2), (16, 0), (10, 3),
+    (13, 1), (9, 2), (3, 3), (2, 3), (14, 1), (11, 3), (15, 1), (16, 1), (13, 2), (9, 3),
+    (12, 2), (14, 2), (15, 2), (16, 2), (13, 3), (12, 3), (14, 3), (15, 3), (16, 3),
 )
 NOTE_STEP = 5
 KV_PIECES = 4
@@ -1202,7 +1202,7 @@
         answer(distance).wait_send()
 
 
-ANSWER_AFTER = 12
+ANSWER_AFTER = 26
 
 
 def scatter(

time: 503 us -> 484 us (0.962)
  Pallas kernels: 462 us -> 444 us
    pallas_call x1, Pallas kernels: 204 us -> 186 us  [scatter(): pl.pallas_call(scatter_kernel, out_shape=(jax.ShapeDtypeStruct((rows, wid...]
where the time goes in v5:
time: 484 us; the launch traced here: 476 us
  Pallas kernels  444 us (92%)
  other arithmetic  14.6 us (3%)
  local copies, waits for them, and re-layouts  12.5 us (3%)
    pallas_call x1, Pallas kernels, scatter(): pl.pallas_call(scatter_kernel, out_shape=(jax.ShapeDtypeStruct((rows, wid...  186 us
    pallas_call x1, Pallas kernels, gather(): pl.pallas_call(gather_kernel, out_shape=(blocks, blocks, blocks, jax.Shap...  158 us
    pallas_call x1, Pallas kernels, middle(): pl.pallas_call(functools.partial(middle_kernel, heads), out_shape=(jax.Sh...  66.6 us
    pallas_call x1, Pallas kernels, attend_back(): pl.pallas_call(functools.partial(attend_back_kernel, heads), out_shape=(j...  23.5 us
    add x5, other arithmetic, adam_update(): average_new = average_decay * average + (1.0 - average_decay) * master_new  10.2 us
    pallas_call x1, Pallas kernels, attend(): pl.pallas_call(functools.partial(attend_kernel, heads), out_shape=(jax.Sh...  9.79 us

profile of v5, /device:TPU:0, one launch (start us, length us, event | category | flops | bytes accessed | tf_op | source)
XLA Modules:
  0.0 476.1 jit_solution(13977654472180215412)
XLA Ops:
  1.3 0.7 convert_element_type.20
  2.0 0.8 reshape.99
  2.8 0.7 copy.64
  3.5 0.9 copy.67.keep_ref
  4.3 1.2 convert_element_type.19
  5.5 1.0 copy.65
  6.5 157.7 %gather.1 = (bf16[2,2,2,2,2,144,1152]{6,5,4,3,2,1,0:T(8,128)(2,1)}, bf16[2,2,2,2,2,144,1152]{6,5,4,3,2,1,0:T(8,128)(2,1)}, bf16[2,2,2,2,2,144,1152]{6,5,4,3,2,1,...) custom-call(f32[1,1152]{1,0:T(1,128)} %cond_ref.1, ...), custom_call_target="tpu_custom_call" | custom-call | flops 4076863488 | bytes 33177600 | tf_op jit(solution)/shard_map/gather/pallas_call | solution.py:619
  164.2 1.4 fusion.22
  165.6 0.8 slice_bitcast_fusion
  166.6 1.0 reshape_reshape.4.up_bias
  167.6 9.8 %attend.1 = (bf16[512,1152]{1,0:T(8,128)(2,1)}, f32[16,512]{1,0:T(8,128)}) custom-call(s32[1,8]{1,0:T(1,128)} %len_ref.3, s32[10,16]{1,0:T(8,128)} %table_ref.3, s32[1]{0:T(128)S(6)} %copy.75.bucket_ref, bf16[512,1152]{1,0:T(8,128)(2,1)} %get-tuple-element.61.q_ref, bf16[2048,2304]{1,0:T(8,128)(2,1)} %bitcast.38), custom_call_target="tpu_custom_call" | custom-call | flops 9663676416 | bytes 23592960 | tf_op jit(solution)/shard_map/attend/pallas_call | solution.py:1438
  177.4 66.6 %middle.1 = (bf16[512,1152]{1,0:T(8,128)(2,1)}, f32[512,1152]{1,0:T(8,128)}, bf16[16,144,1152]{2,1,0:T(8,128)(2,1)}, bf16[16,144,1152]{2,1,0:T(8,128)(2,1)}, bf1...) custom-call(s32[1]{0:T(128)S(6)} %copy.75.bucket_ref, ...), custom_call_target="tpu_custom_call" | custom-call | flops 32614907904 | bytes 42467328 | tf_op jit(solution)/shard_map/middle/pallas_call | solution.py:1709
  244.1 23.5 %attend_back.1 = (bf16[512,1152]{1,0:T(8,128)(2,1)}, bf16[2,512,2304]{2,1,0:T(8,128)(2,1)}, bf16[2,512,2304]{2,1,0:T(8,128)(2,1)}) custom-call(s32[1,8]{1,0:T(1,128)} %len_ref.3, bf16[512,1152]{1,0:T(8,128)(2,1)} %get-tuple-element.61.q_ref, bf16[512,1152]{1,0:T(8,128)(2,1)} %get-tuple-element.70.do_ref, f32[16,512]{1,0:T(8,128)} %get-tuple-element.71.log_ref, ...), custom_call_target="tpu_custom_call" | custom-call | flops 24159191040 | bytes 47185920 | tf_op jit(solution)/shard_map/attend_back/pallas_call | solution.py:1820
  269.2 185.9 %scatter.1 = (f32[144,1152]{1,0:T(8,128)}, f32[144,384]{1,0:T(8,128)}, f32[144,896]{1,0:T(8,128)}, f32[512,1152]{1,0:T(8,128)}, f32[8,1728]{1,0:T(8,128)}, /*ind...) custom-call(bf16[2,512,2304]{2,1,0:T(8,128)(2,1)} %get-tuple-element, ...), custom_call_target="tpu_custom_call" | custom-call | flops 8153726976 | bytes 49766400 | tf_op jit(solution)/shard_map/scatter/pallas_call | solution.py:1235
  455.1 0.8 slice_reduce_fusion
  456.6 0.7 slice_bitcast_fusion.1
  458.2 1.2 bitcast_convert_fusion
  459.7 2.4 multiply_add_fusion.9
  462.2 3.0 multiply_add_fusion.7
  465.2 2.2 multiply_add_fusion.5
  467.8 2.0 multiply_add_fusion.6
  469.8 0.8 copy-done.4
  470.9 3.4 multiply_add_fusion.2
  474.3 1.4 copy.76
  (65 shorter events, 4.4 us)
Async XLA Ops:
  244.1 23.5 %copy-start.19 = (f32[8,1152]{1,0:T(8,128)S(1)}, f32[8,1152]{1,0:T(8,128)}, u32[]{:S(2)}) copy-start(f32[8,1152]{1,0:T(8,128)} %get-tuple-element.84) | copy-start | bytes 110596
  244.1 23.5 %copy-start.20 = (f32[4,1,1152]{2,1,0:T(1,128)S(1)}, f32[4,1,1152]{2,1,0:T(1,128)}, u32[]{:S(2)}) copy-start(f32[4,1,1152]{2,1,0:T(1,128)} %get-tuple-element.85) | copy-start | bytes 55300
  269.2 186.8 %copy-start.22 = (f32[1,1152]{1,0:T(1,128)S(1)}, f32[1,1152]{1,0:T(1,128)}, u32[]{:S(2)}) copy-start(f32[1,1152]{1,0:T(1,128)} %cond_ref.1) | copy-start | bytes 13828
  269.2 188.3 %copy-start.21 = (f32[504]{0:T(512)S(1)}, f32[504]{0:T(512)}, u32[]{:S(2)}) copy-start(f32[504]{0:T(512)} %param.60) | copy-start | bytes 6052
  269.2 188.4 %copy-start.24 = (f32[504]{0:T(512)S(1)}, f32[504]{0:T(512)}, u32[]{:S(2)}) copy-start(f32[504]{0:T(512)} %param.63) | copy-start | bytes 6052
  269.2 188.4 %copy-start.25 = (f32[504]{0:T(512)S(1)}, f32[504]{0:T(512)}, u32[]{:S(2)}) copy-start(f32[504]{0:T(512)} %param.61) | copy-start | bytes 6052
  269.2 188.4 %copy-start.26 = (f32[504]{0:T(512)S(1)}, f32[504]{0:T(512)}, u32[]{:S(2)}) copy-start(f32[504]{0:T(512)} %param.62) | copy-start | bytes 6052
  455.1 4.6 copy-start.17
  458.2 4.0 copy-start.14
  458.2 4.0 copy-start.15
  458.2 4.0 copy-start.16
  462.1 3.0 copy-start.1
  462.1 3.0 copy-start.6
  462.1 3.0 copy-start.7
  462.1 3.0 copy-start.8
  465.2 2.3 copy-start.9
  465.2 2.3 copy-start.10
  465.2 2.3 copy-start.11
  465.2 2.6 copy-start.13
  467.8 2.8 copy-start.4
  467.8 3.1 copy-start.5
  467.8 3.1 copy-start.18
  467.8 3.1 copy-start.23
  470.9 3.4 copy-start.2
  (3 other events, 6.3 us)

commit v6 on v5

--- a/solution.py
+++ b/solution.py
@@ -557,6 +557,10 @@
             kv[:, :width] = acc[:, width : 2 * width].astype(bfloat)
             kv[:, width:] = (acc[:, 2 * width :] + bias_ref[7:8, :]).astype(bfloat)
 
+    def relay(piece):
+        kv_step(piece, "over").wait_recv()
+        kv_step(piece, "far").start()
+
     for step, (part, phase) in enumerate(GATHER_STEPS):
         if step == NOTE_STEP:
             modulations()
@@ -577,12 +581,10 @@
                 kv_step(phase, kind).start()
         else:
             moving[part].advance(phase)
-    def relay(piece):
-        kv_step(piece, "over").wait_recv()
-        kv_step(piece, "far").start()
-
-    for piece in range(KV_PIECES):
-        kv_expected(piece, functools.partial(relay, piece))
+        behind = len(GATHER_STEPS) - 1 - step
+        if behind < 2 * KV_PIECES and behind % 2 == 0:
+            piece = KV_PIECES - 1 - behind // 2
+            kv_expected(piece, functools.partial(relay, piece))
     for part in rest:
         part.collect()
     for part in moving:

time: 484 us -> 482 us (level)
  the two profiles are of different devices: /device:TPU:0 before, /device:TPU:1 now
where the time goes in v6:
time: 482 us; the launch traced here: 474 us
  Pallas kernels  442 us (92%)
  other arithmetic  14.6 us (3%)
  local copies, waits for them, and re-layouts  12.5 us (3%)
    pallas_call x1, Pallas kernels, scatter(): pl.pallas_call(scatter_kernel, out_shape=(jax.ShapeDtypeStruct((rows, wid...  168 us
    pallas_call x1, Pallas kernels, gather(): pl.pallas_call(gather_kernel, out_shape=(blocks, blocks, blocks, jax.Shap...  155 us
    pallas_call x1, Pallas kernels, middle(): pl.pallas_call(functools.partial(middle_kernel, heads), out_shape=(jax.Sh...  66.7 us
    pallas_call x1, Pallas kernels, attend_back(): pl.pallas_call(functools.partial(attend_back_kernel, heads), out_shape=(j...  33.1 us
    pallas_call x1, Pallas kernels, attend(): pl.pallas_call(functools.partial(attend_kernel, heads), out_shape=(jax.Sh...  19.1 us
    add x5, other arithmetic, adam_update(): average_new = average_decay * average + (1.0 - average_decay) * master_new  10.2 us

profile of v6, /device:TPU:1, one launch (start us, length us, event | category | flops | bytes accessed | tf_op | source)
XLA Modules:
  0.0 474.1 jit_solution(8624753481225496125)
XLA Ops:
  1.3 0.7 convert_element_type.20
  2.0 0.8 reshape.99
  2.8 0.7 copy.64
  3.5 0.9 copy.67.keep_ref
  4.3 1.2 convert_element_type.19
  5.5 1.0 copy.65
  6.5 155.1 %gather.1 = (bf16[2,2,2,2,2,144,1152]{6,5,4,3,2,1,0:T(8,128)(2,1)}, bf16[2,2,2,2,2,144,1152]{6,5,4,3,2,1,0:T(8,128)(2,1)}, bf16[2,2,2,2,2,144,1152]{6,5,4,3,2,1,...) custom-call(f32[1,1152]{1,0:T(1,128)} %cond_ref.1, ...), custom_call_target="tpu_custom_call" | custom-call | flops 4076863488 | bytes 33177600 | tf_op jit(solution)/shard_map/gather/pallas_call | solution.py:621
  161.6 1.4 fusion.22
  163.0 0.8 slice_bitcast_fusion
  164.0 1.0 reshape_reshape.4.up_bias
  165.0 19.1 %attend.1 = (bf16[512,1152]{1,0:T(8,128)(2,1)}, f32[16,512]{1,0:T(8,128)}) custom-call(s32[1,8]{1,0:T(1,128)} %len_ref.3, s32[10,16]{1,0:T(8,128)} %table_ref.3, s32[1]{0:T(128)S(6)} %copy.75.bucket_ref, bf16[512,1152]{1,0:T(8,128)(2,1)} %get-tuple-element.61.q_ref, bf16[2048,2304]{1,0:T(8,128)(2,1)} %bitcast.38), custom_call_target="tpu_custom_call" | custom-call | flops 9663676416 | bytes 23592960 | tf_op jit(solution)/shard_map/attend/pallas_call | solution.py:1440
  184.2 66.7 %middle.1 = (bf16[512,1152]{1,0:T(8,128)(2,1)}, f32[512,1152]{1,0:T(8,128)}, bf16[16,144,1152]{2,1,0:T(8,128)(2,1)}, bf16[16,144,1152]{2,1,0:T(8,128)(2,1)}, bf1...) custom-call(s32[1]{0:T(128)S(6)} %copy.75.bucket_ref, ...), custom_call_target="tpu_custom_call" | custom-call | flops 32614907904 | bytes 42467328 | tf_op jit(solution)/shard_map/middle/pallas_call | solution.py:1711
  250.9 33.1 %attend_back.1 = (bf16[512,1152]{1,0:T(8,128)(2,1)}, bf16[2,512,2304]{2,1,0:T(8,128)(2,1)}, bf16[2,512,2304]{2,1,0:T(8,128)(2,1)}) custom-call(s32[1,8]{1,0:T(1,128)} %len_ref.3, bf16[512,1152]{1,0:T(8,128)(2,1)} %get-tuple-element.61.q_ref, bf16[512,1152]{1,0:T(8,128)(2,1)} %get-tuple-element.70.do_ref, f32[16,512]{1,0:T(8,128)} %get-tuple-element.71.log_ref, ...), custom_call_target="tpu_custom_call" | custom-call | flops 24159191040 | bytes 47185920 | tf_op jit(solution)/shard_map/attend_back/pallas_call | solution.py:1822
  285.6 167.6 %scatter.1 = (f32[144,1152]{1,0:T(8,128)}, f32[144,384]{1,0:T(8,128)}, f32[144,896]{1,0:T(8,128)}, f32[512,1152]{1,0:T(8,128)}, f32[8,1728]{1,0:T(8,128)}, /*ind...) custom-call(bf16[2,512,2304]{2,1,0:T(8,128)(2,1)} %get-tuple-element, ...), custom_call_target="tpu_custom_call" | custom-call | flops 8153726976 | bytes 49766400 | tf_op jit(solution)/shard_map/scatter/pallas_call | solution.py:1237
  453.2 0.8 slice_reduce_fusion
  454.7 0.7 slice_bitcast_fusion.1
  456.3 1.2 bitcast_convert_fusion
  457.8 2.4 multiply_add_fusion.9
  460.2 3.0 multiply_add_fusion.7
  463.3 2.2 multiply_add_fusion.5
  465.9 2.0 multiply_add_fusion.6
  467.9 0.8 copy-done.4
  469.0 3.4 multiply_add_fusion.2
  472.3 1.4 copy.76
  (65 shorter events, 4.4 us)
Async XLA Ops:
  250.9 33.1 %copy-start.19 = (f32[8,1152]{1,0:T(8,128)S(1)}, f32[8,1152]{1,0:T(8,128)}, u32[]{:S(2)}) copy-start(f32[8,1152]{1,0:T(8,128)} %get-tuple-element.84) | copy-start | bytes 110596
  250.9 33.1 %copy-start.20 = (f32[4,1,1152]{2,1,0:T(1,128)S(1)}, f32[4,1,1152]{2,1,0:T(1,128)}, u32[]{:S(2)}) copy-start(f32[4,1,1152]{2,1,0:T(1,128)} %get-tuple-element.85) | copy-start | bytes 55300
  285.6 168.5 %copy-start.22 = (f32[1,1152]{1,0:T(1,128)S(1)}, f32[1,1152]{1,0:T(1,128)}, u32[]{:S(2)}) copy-start(f32[1,1152]{1,0:T(1,128)} %cond_ref.1) | copy-start | bytes 13828
  285.6 170.0 %copy-start.21 = (f32[504]{0:T(512)S(1)}, f32[504]{0:T(512)}, u32[]{:S(2)}) copy-start(f32[504]{0:T(512)} %param.60) | copy-start | bytes 6052
  285.6 170.1 %copy-start.24 = (f32[504]{0:T(512)S(1)}, f32[504]{0:T(512)}, u32[]{:S(2)}) copy-start(f32[504]{0:T(512)} %param.63) | copy-start | bytes 6052
  285.6 170.1 %copy-start.25 = (f32[504]{0:T(512)S(1)}, f32[504]{0:T(512)}, u32[]{:S(2)}) copy-start(f32[504]{0:T(512)} %param.61) | copy-start | bytes 6052
  285.6 170.1 %copy-start.26 = (f32[504]{0:T(512)S(1)}, f32[504]{0:T(512)}, u32[]{:S(2)}) copy-start(f32[504]{0:T(512)} %param.62) | copy-start | bytes 6052
  453.2 4.6 copy-start.17
  456.3 4.0 copy-start.14
  456.3 4.0 copy-start.15
  456.3 4.0 copy-start.16
  460.2 3.0 copy-start.1
  460.2 3.0 copy-start.6
  460.2 3.0 copy-start.7
  460.2 3.0 copy-start.8
  463.2 2.3 copy-start.9
  463.2 2.3 copy-start.10
  463.3 2.3 copy-start.11
  463.3 2.6 copy-start.13
  465.9 2.8 copy-start.4
  465.9 3.1 copy-start.5
  465.9 3.1 copy-start.18
  465.9 3.1 copy-start.23
  469.0 3.4 copy-start.2
  (3 other events, 6.3 us)
